TPU v7x, 32 devices: a whole 2x2x4 slice. The times are simulated.
32 devices in a mesh: section: 2 (over x), expert: 16 (over z, y, core).
Axes of the slice: x: 2, y: 2, z: 4, core: 2. Of those that a mesh axis runs over, the one named last changes fastest.
Arguments:
- emitted: bfloat16 [2, 2, 1024, 2048], P('section', None, 'expert'), may hold values from -6 to 6
- levels: int32 [2, 2, 1024], P('section', None, 'expert'), may hold values from 0 to 999
- expert_ids: int32 [2, 2, 1024, 6], P('section', None, 'expert'), may hold values from 0 to 15, all different within a row; in each aligned block of 64 rows (0 to 63, 64 to 127, ..., all dimensions but the last counted through in order) at most 32 rows name the same one
- gate_values: float32 [2, 2, 1024, 6], P('section', None, 'expert'), may hold values from 0.05 to 0.5
- w_gate: bfloat16 [2, 16, 2048, 768], P('section', 'expert'), may hold values from -0.125 to 0.125
- w_up: bfloat16 [2, 16, 2048, 768], P('section', 'expert'), may hold values from -0.125 to 0.125
- w_down: bfloat16 [2, 16, 768, 2048], P('section', 'expert'), may hold values from -0.21875 to 0.21875
- w_mod: bfloat16 [2, 256, 4096], P('section'), may hold values from -0.375 to 0.375
Outputs:
- layer_out: bfloat16 [2, 2, 1024, 2048], P('section', None, 'expert')
Inputs may be any that keep to these rules, and one draw needn't show every extreme that they name: `expert_ids`: each token names 6 different experts. Among the 64 tokens of one device of expert in one microbatch at one section, no expert is named by more than 32 tokens, and in every draw some expert is named by exactly 32 of them.
All inputs are finite; a program needn't handle non-finite values.
Results may differ from a plain program's by a relative error of at most 0.006.
Values may be sent and summed in bfloat16 or wider, within the bound.
No kernel may reach another device: no remote copies, remote signals or barrier semaphores. Data moves between devices by JAX's collectives and lax.ppermute only.
A program may use at most 64 MiB of HBM per device.

v0:
```python
import math

import jax
import jax.numpy as jnp
from jax import lax
from jax.sharding import PartitionSpec as P

epsilon = 1e-06
CORES = 2
LANES = 128


def level_embedding(levels, entries):
    half_width = entries // 2
    frequency = jnp.exp(-math.log(10000.0) * jnp.arange(half_width, dtype=jnp.float32) / half_width)
    angles = levels.astype(jnp.float32)[:, None] * frequency[None, :]
    return jnp.concatenate([jnp.cos(angles), jnp.sin(angles)], axis=1).astype(jnp.bfloat16)


def chip_cycle(mesh):
    line = list(mesh.devices.reshape(mesh.devices.shape[0], -1)[0])
    chips = len(line) // CORES
    places = [tuple(getattr(line[CORES * c], "coords", (0, 0, c))) for c in range(chips)]
    spans = [sorted({p[d] for p in places}) for d in range(3)]
    wide = [d for d in range(3) if len(spans[d]) > 1]
    if len(set(places)) != chips or len(wide) != 2 or math.prod(len(spans[d]) for d in wide) != chips:
        return list(range(chips))
    rows, cols = wide if len(spans[wide[0]]) % 2 == 0 else wide[::-1]
    if len(spans[rows]) % 2:
        return list(range(chips))
    if len(spans[rows]) > len(spans[cols]) and len(spans[cols]) % 2 == 0:
        rows, cols = cols, rows
    at = {(p[rows], p[cols]): c for c, p in enumerate(places)}
    order = []
    for i, r in enumerate(spans[rows]):
        along = spans[cols][1:]
        order += [(r, c) for c in (along if i % 2 == 0 else along[::-1])]
    order += [(r, spans[cols][0]) for r in reversed(spans[rows])]
    return [at[place] for place in order]


def build(cycle):
    chips = len(cycle)
    experts = chips * CORES
    far = chips // 2
    halved = chips % 2 == 0

    def hop(value, step):
        pairs = [
            (cycle[i] * CORES + c, cycle[(i + step) % chips] * CORES + c)
            for i in range(chips)
            for c in range(CORES)
        ]
        return lax.ppermute(value, "expert", pairs)

    def swap(value):
        return lax.ppermute(value, "expert", [(i, i ^ 1) for i in range(experts)])

    def shards(emitted, levels, expert_ids, gate_values, w_gate, w_up, w_down, w_mod):
        sections = lax.axis_size("section")
        batches, tok_rows, features = emitted.shape[1:]
        around = [(s, (s + 1) % sections) for s in range(sections)]
        arrived = [lax.ppermute(emitted[0, b], "section", around) for b in range(batches)]
        mine = (w_gate[0, 0], w_up[0, 0], w_down[0, 0])
        other = tuple(swap(w) for w in mine)
        me = lax.axis_index("expert")
        mod_weight = w_mod[0]

        def payload(b):
            embed = level_embedding(levels[0, b], mod_weight.shape[0])
            modulation = jnp.dot(embed, mod_weight, preferred_element_type=jnp.float32)
            values = arrived[b].astype(jnp.float32)
            mean_square = jnp.mean(values * values, axis=1, keepdims=True)
            normed = (
                values * lax.rsqrt(mean_square + epsilon) * (1.0 + modulation[:, :features])
                + modulation[:, features:]
            ).astype(jnp.bfloat16)
            gates = gate_values[0, b]
            high = lax.reduce_precision(gates, 8, 7)
            extra = jnp.concatenate(
                [
                    expert_ids[0, b].astype(jnp.bfloat16),
                    high.astype(jnp.bfloat16),
                    (gates - high).astype(jnp.bfloat16),
                ],
                axis=1,
            )
            lanes = -(-extra.shape[1] // LANES) * LANES
            extra = jnp.pad(extra, ((0, 0), (0, lanes - extra.shape[1])))
            return jnp.concatenate([normed, extra], axis=1)

        top = expert_ids.shape[3]

        def partial(block):
            normed = block[:, :features]
            extra = block[:, features : features + 3 * top].astype(jnp.float32)
            ids, gates = extra[:, :top], extra[:, top : 2 * top] + extra[:, 2 * top :]
            total = 0.0
            for (gate_weight, up_weight, down_weight), expert in ((mine, me), (other, me ^ 1)):
                weight = jnp.sum(
                    jnp.where(ids == expert.astype(jnp.float32), gates, 0.0), axis=1, keepdims=True
                )
                gate_part = jnp.dot(normed, gate_weight, preferred_element_type=jnp.float32)
                up_part = jnp.dot(normed, up_weight, preferred_element_type=jnp.float32)
                hidden = (jax.nn.silu(gate_part) * up_part * weight).astype(jnp.bfloat16)
                total += jnp.dot(hidden, down_weight, preferred_element_type=jnp.float32)
            return total.astype(jnp.bfloat16)

        def added(a, b):
            return (a.astype(jnp.float32) + b.astype(jnp.float32)).astype(jnp.bfloat16)

        results = []
        for b in range(batches):
            own = payload(b)
            forth, back = [own], [own]
            for k in range(1, far + 1):
                last = halved and k == far
                half = tok_rows // 2
                forth.append(hop(forth[-1][:half] if last else forth[-1], 1))
                back.append(hop(back[-1][half:] if last else back[-1], -1))
            near = jnp.concatenate(forth[:far] + back[1:far])
            away = jnp.concatenate([forth[far], back[far]])
            near_sum, away_sum = partial(near), partial(away)
            pieces = [near_sum[i * tok_rows : (i + 1) * tok_rows] for i in range(2 * far - 1)]
            forth_sum, back_sum = pieces[:far], [pieces[0]] + pieces[far:]
            fs, bs = away_sum[: away_sum.shape[0] // 2], away_sum[away_sum.shape[0] // 2 :]
            for k in range(far - 1, -1, -1):
                fs, bs = hop(fs, -1), hop(bs, 1)
                if k:
                    if halved and k == far - 1:
                        half = tok_rows // 2
                        fs = jnp.concatenate([added(fs, forth_sum[k][:half]), forth_sum[k][half:]])
                        bs = jnp.concatenate([back_sum[k][:half], added(bs, back_sum[k][half:])])
                    else:
                        fs, bs = added(fs, forth_sum[k]), added(bs, back_sum[k])
            total = (
                arrived[b].astype(jnp.float32)
                + pieces[0].astype(jnp.float32)
                + fs.astype(jnp.float32)
                + bs.astype(jnp.float32)
            )
            results.append(total.astype(jnp.bfloat16))
        return jnp.stack(results)[None]

    return shards


def solution(mesh):
    placed = (
        P("section", None, "expert", None),
        P("section", None, "expert"),
        P("section", None, "expert", None),
        P("section", None, "expert", None),
        P("section", "expert", None, None),
        P("section", "expert", None, None),
        P("section", "expert", None, None),
        P("section", None, None),
    )
    return jax.shard_map(
        build(chip_cycle(mesh)),
        mesh=mesh,
        in_specs=placed,
        out_specs=P("section", None, "expert", None),
        check_vma=False,
    )
```

profile of v0, /device:TPU:0, one launch (start us, length us, event | category | flops | bytes accessed | tf_op | source)
XLA Modules:
  0.0 201.4 jit_solution(7211838897839394699)
XLA Ops:
  1.2 3.0 %collective-permute-start = (bf16[64,2048]{1,0:T(8,128)(2,1)S(1)}, bf16[64,2048]{1,0:T(8,128)(2,1)S(1)}, u32[]{:S(2)}, u32[]{:S(2)}) collective-permute-start(bf16[64,2048]{1,0:T(8,128)(2,1)S(1)} %get-tuple-element.29), channel_id=1, source_target_pairs={{0,16},{16,0},{1,17},{17,1},{2,18},{18,2},{3,19},{19,3},{4,20},{20... | collective-permute-start | bytes 786440 | tf_op jit(solution)/shard_map/ppermute | solution.py:63
  8.6 2.7 %collective-permute-done = bf16[64,2048]{1,0:T(8,128)(2,1)S(1)} collective-permute-done((bf16[64,2048]{1,0:T(8,128)(2,1)S(1)}, bf16[64,2048]{1,0:T(8,128)(2,1)S(1)}, u32[]{:S(2)}, u32[]{:S(2)}) %collective-permute-start) | collective-permute-done | bytes 262176 | tf_op jit(solution)/shard_map/ppermute | solution.py:63
  11.7 2.2 %collective-permute-start.1 = (bf16[64,2176]{1,0:T(8,128)(2,1)S(1)}, bf16[64,2176]{1,0:T(8,128)(2,1)S(1)}, u32[]{:S(2)}, u32[]{:S(2)}) collective-permute-start(bf16[64,2176]{1,0:T(8,128)(2,1)S(1)} %get-tuple-element.32), channel_id=1, source_target_pairs={{4,8},{5,9},{8,12},{9,13},{12,14},{13,15},{14,10},{15,11},{10,6},{... | collective-permute-start | bytes 835592 | tf_op jit(solution)/shard_map/ppermute | solution.py:54
  13.9 2.2 %collective-permute-done.20 = bf16[64,2048]{1,0:T(8,128)(2,1)S(1)} collective-permute-done((bf16[64,2048]{1,0:T(8,128)(2,1)S(1)}, bf16[64,2048]{1,0:T(8,128)(2,1)S(1)}, u32[]{:S(2)}, u32[]{:S(2)}) %collective-permute-start.20) | collective-permute-done | bytes 262176 | tf_op jit(solution)/shard_map/ppermute | solution.py:63
  16.5 1.9 collective-permute-start.21
  20.9 3.9 %collective-permute-done.21 = bf16[64,2176]{1,0:T(8,128)(2,1)S(1)} collective-permute-done((bf16[64,2176]{1,0:T(8,128)(2,1)S(1)}, bf16[64,2176]{1,0:T(8,128)(2,1)S(1)}, u32[]{:S(2)}, u32[]{:S(2)}) %collective-permute-start.21) | collective-permute-done | bytes 278560 | tf_op jit(solution)/shard_map/ppermute | solution.py:54
  28.1 6.2 %collective-permute-done.2 = bf16[64,2176]{1,0:T(8,128)(2,1)S(1)} collective-permute-done((bf16[64,2176]{1,0:T(8,128)(2,1)S(1)}, bf16[64,2176]{1,0:T(8,128)(2,1)S(1)}, u32[]{:S(2)}, u32[]{:S(2)}) %collective-permute-start.2) | collective-permute-done | bytes 278560 | tf_op jit(solution)/shard_map/ppermute | solution.py:54
  36.0 2.0 collective-permute-done.22
  42.5 2.0 %collective-permute-done.3 = bf16[64,2176]{1,0:T(8,128)(2,1)S(1)} collective-permute-done((bf16[64,2176]{1,0:T(8,128)(2,1)S(1)}, bf16[64,2176]{1,0:T(8,128)(2,1)S(1)}, u32[]{:S(2)}, u32[]{:S(2)}) %collective-permute-start.3) | collective-permute-done | bytes 278560 | tf_op jit(solution)/shard_map/ppermute | solution.py:54
  46.1 4.4 %collective-permute-done.25 = bf16[64,2176]{1,0:T(8,128)(2,1)S(1)} collective-permute-done((bf16[64,2176]{1,0:T(8,128)(2,1)S(1)}, bf16[64,2176]{1,0:T(8,128)(2,1)S(1)}, u32[]{:S(2)}, u32[]{:S(2)}) %collective-permute-start.25) | collective-permute-done | bytes 278560 | tf_op jit(solution)/shard_map/ppermute | solution.py:54
  52.2 2.5 %collective-permute-done.6 = bf16[64,2176]{1,0:T(8,128)(2,1)S(1)} collective-permute-done((bf16[64,2176]{1,0:T(8,128)(2,1)S(1)}, bf16[64,2176]{1,0:T(8,128)(2,1)S(1)}, u32[]{:S(2)}, u32[]{:S(2)}) %collective-permute-start.6) | collective-permute-done | bytes 278560 | tf_op jit(solution)/shard_map/ppermute | solution.py:54
  55.2 2.7 %fusion.20 = f32[448,768]{1,0:T(8,128)} fusion(bf16[448,2176]{1,0:T(8,128)(2,1)S(1)} %constant_dynamic-update-slice_fusion, bf16[1,1,2048,768]{3,2,1,0:T(8,128)(2,1)S(1)} %copy-done.1), kind=kOutput, calls=%fused_computation.28 | convolution fusion | flops 1409286144 | bytes 6356992 | tf_op jit(solution)/shard_map/dot_general | solution.py:103
  58.1 3.5 %collective-permute-done.26 = bf16[64,2176]{1,0:T(8,128)(2,1)S(1)} collective-permute-done((bf16[64,2176]{1,0:T(8,128)(2,1)S(1)}, bf16[64,2176]{1,0:T(8,128)(2,1)S(1)}, u32[]{:S(2)}, u32[]{:S(2)}) %collective-permute-start.26) | collective-permute-done | bytes 278560 | tf_op jit(solution)/shard_map/ppermute | solution.py:54
  61.6 2.7 %fusion.12 = f32[448,768]{1,0:T(8,128)} fusion(bf16[448,2176]{1,0:T(8,128)(2,1)S(1)} %constant_dynamic-update-slice_fusion.9, bf16[1,1,2048,768]{3,2,1,0:T(8,128)(2,1)S(1)} %copy-done.1), kind=kOutput, calls=%fused_computation.20 | convolution fusion | flops 1409286144 | bytes 6356992 | tf_op jit(solution)/shard_map/dot_general | solution.py:103
  68.5 9.1 %fusion.31 = f32[448,2048]{1,0:T(8,128)} fusion(f32[448,768]{1,0:T(8,128)} %fusion.20, bf16[448,2176]{1,0:T(8,128)(2,1)} %copy-done.7, f32[448]{0:T(512)S(1)} %get-tuple-element.6, bf16[1,1,768,2048]{3,2,1,0:T(8,128)(2,1)} %param.14, bf16[1,1,2048,768]{3,2,1,0:T(8,128)(2,1)} %param.13), kind=kOutput, calls=%fused_computation.30 | convolution fusion | flops 2820980736 | bytes 13174528 | tf_op jit(solution)/shard_map/dot_general | solution.py:106
  77.6 9.1 %fusion.36 = f32[448,2048]{1,0:T(8,128)} fusion(f32[448,768]{1,0:T(8,128)} %fusion.12, bf16[448,2176]{1,0:T(8,128)(2,1)} %copy-done.8, f32[448]{0:T(512)S(1)} %get-tuple-element.8, bf16[1,1,768,2048]{3,2,1,0:T(8,128)(2,1)} %param.14, bf16[1,1,2048,768]{3,2,1,0:T(8,128)(2,1)} %param.13), kind=kOutput, calls=%fused_computation.31 | convolution fusion | flops 2820980736 | bytes 13174528 | tf_op jit(solution)/shard_map/dot_general | solution.py:106
  89.2 2.7 %collective-permute-done.27 = bf16[32,2176]{1,0:T(8,128)(2,1)S(1)} collective-permute-done((bf16[32,2176]{1,0:T(8,128)(2,1)S(1)}, bf16[32,2176]{1,0:T(8,128)(2,1)S(1)}, u32[]{:S(2)}, u32[]{:S(2)}) %collective-permute-start.27) | collective-permute-done | bytes 139296 | tf_op jit(solution)/shard_map/ppermute | solution.py:54
  92.4 4.5 %collective-permute-done.28 = bf16[32,2176]{1,0:T(8,128)(2,1)S(1)} collective-permute-done((bf16[32,2176]{1,0:T(8,128)(2,1)S(1)}, bf16[32,2176]{1,0:T(8,128)(2,1)S(1)}, u32[]{:S(2)}, u32[]{:S(2)}) %collective-permute-start.28) | collective-permute-done | bytes 139296 | tf_op jit(solution)/shard_map/ppermute | solution.py:54
  97.6 3.2 %fusion.91 = f32[64,768]{1,0:T(8,128)} fusion(bf16[64,2176]{1,0:T(8,128)(2,1)S(1)} %constant_dynamic-update-slice_fusion.7, bf16[1,1,2048,768]{3,2,1,0:T(8,128)(2,1)} %param.12), kind=kOutput, calls=%fused_computation.113 | convolution fusion | flops 201326592 | bytes 3604480 | tf_op jit(solution)/shard_map/dot_general | solution.py:103
  101.5 5.1 %fusion.98 = f32[64,2048]{1,0:T(8,128)} fusion(f32[64,768]{1,0:T(8,128)} %fusion.91, bf16[64,2176]{1,0:T(8,128)(2,1)S(1)} %constant_dynamic-update-slice_fusion.7, f32[64]{0:T(128)S(1)} %get-tuple-element.10, bf16[1,1,768,2048]{3,2,1,0:T(8,128)(2,1)} %param.14, bf16[1,1,2048,768]{3,2,1,0:T(8,128)(2,1)} %param.13), kind=kOutput, calls=%fused_computation.115 | convolution fusion | flops 402997248 | bytes 7275008 | tf_op jit(solution)/shard_map/dot_general | solution.py:106
  106.7 5.0 %fusion.81 = f32[64,2048]{1,0:T(8,128)} fusion(f32[64,768]{1,0:T(8,128)S(1)} %fusion.74, bf16[64,2176]{1,0:T(8,128)(2,1)S(1)} %constant_dynamic-update-slice_fusion.16, f32[64]{0:T(128)S(1)} %get-tuple-element.12, bf16[1,1,768,2048]{3,2,1,0:T(8,128)(2,1)} %param.14, bf16[1,1,2048,768]{3,2,1,0:T(8,128)(2,1)} %param.13), kind=kOutput, calls=%fused_computation.106 | convolution fusion | flops 402997248 | bytes 7275008 | tf_op jit(solution)/shard_map/dot_general | solution.py:106
  111.7 3.2 %fusion.87 = f32[64,768]{1,0:T(8,128)} fusion(bf16[2048,768]{1,0:T(8,128)(2,1)} %collective-permute-done.7, bf16[64,2176]{1,0:T(8,128)(2,1)S(1)} %constant_dynamic-update-slice_fusion.7), kind=kOutput, calls=%fused_computation.109 | convolution fusion | flops 201326592 | bytes 3604480 | tf_op jit(solution)/shard_map/dot_general | solution.py:103
  114.9 4.4 %fusion = bf16[64,2048]{1,0:T(8,128)(2,1)S(1)} fusion(f32[64,2048]{1,0:T(8,128)} %fusion.98, bf16[768,2048]{1,0:T(8,128)(2,1)} %collective-permute-done.9, f32[64,768]{1,0:T(8,128)} %fusion.87, bf16[2048,768]{1,0:T(8,128)(2,1)} %collective-permute-done.8, bf16[64,2176]{1,0:T(8,128)(2,1)S(1)} %constant_dynamic-update-slice_fusion.7, f32[64]{0:T(128)S(1)} %get-tuple-element.9), kind=kOutput, calls=%fused_computation.4 | convolution fusion | flops 403259392 | bytes 7537152 | tf_op jit(solution)/shard_map/dot_general | solution.py:106
  122.1 5.1 %fusion.16 = f32[448,768]{1,0:T(8,128)} fusion(bf16[2048,768]{1,0:T(8,128)(2,1)} %collective-permute-done.7, bf16[448,2176]{1,0:T(8,128)(2,1)} %copy-done.7), kind=kOutput, calls=%fused_computation.24 | convolution fusion | flops 1409286144 | bytes 6356992 | tf_op jit(solution)/shard_map/dot_general | solution.py:103
  127.2 9.6 %add_convert_fusion.1 = bf16[448,2048]{1,0:T(8,128)(2,1)} fusion(f32[448,2048]{1,0:T(8,128)} %fusion.31, bf16[768,2048]{1,0:T(8,128)(2,1)} %collective-permute-done.9, f32[448,768]{1,0:T(8,128)} %fusion.16, bf16[2048,768]{1,0:T(8,128)(2,1)} %collective-permute-done.8, bf16[448,2176]{1,0:T(8,128)(2,1)} %copy-done.7, f32[448]{0:T(512)S(1)} %get-tuple-element.5), kind=kOutput, calls=%fused_computation.1 | convolution fusion | flops 2822815744 | bytes 15009536 | tf_op jit(solution)/shard_map/dot_general | solution.py:106
  138.4 3.2 %fusion.70 = f32[64,768]{1,0:T(8,128)} fusion(bf16[2048,768]{1,0:T(8,128)(2,1)} %collective-permute-done.7, bf16[64,2176]{1,0:T(8,128)(2,1)S(1)} %constant_dynamic-update-slice_fusion.16), kind=kOutput, calls=%fused_computation.100 | convolution fusion | flops 201326592 | bytes 3604480 | tf_op jit(solution)/shard_map/dot_general | solution.py:103
  141.6 5.1 %fusion.1 = bf16[64,2048]{1,0:T(8,128)(2,1)} fusion(f32[64,2048]{1,0:T(8,128)S(1)} %copy-done.3, bf16[768,2048]{1,0:T(8,128)(2,1)} %collective-permute-done.9, f32[64,768]{1,0:T(8,128)} %fusion.70, bf16[2048,768]{1,0:T(8,128)(2,1)} %collective-permute-done.8, bf16[64,2176]{1,0:T(8,128)(2,1)S(1)} %constant_dynamic-update-slice_fusion.16, f32[64]{0:T(128)} %get-tuple-element.11), kind=kOutput, calls=%fused_computation.5 | convolution fusion | flops 403259392 | bytes 7536896 | tf_op jit(solution)/shard_map/dot_general | solution.py:106
  150.4 5.1 %fusion.8 = f32[448,768]{1,0:T(8,128)} fusion(bf16[2048,768]{1,0:T(8,128)(2,1)} %collective-permute-done.7, bf16[448,2176]{1,0:T(8,128)(2,1)} %copy-done.8), kind=kOutput, calls=%fused_computation.16 | convolution fusion | flops 1409286144 | bytes 6356992 | tf_op jit(solution)/shard_map/dot_general | solution.py:103
  155.5 9.6 %add_convert_fusion = bf16[448,2048]{1,0:T(8,128)(2,1)} fusion(f32[448,2048]{1,0:T(8,128)} %fusion.36, bf16[768,2048]{1,0:T(8,128)(2,1)} %collective-permute-done.9, f32[448,768]{1,0:T(8,128)} %fusion.8, bf16[2048,768]{1,0:T(8,128)(2,1)} %collective-permute-done.8, bf16[448,2176]{1,0:T(8,128)(2,1)} %copy-done.8, f32[448]{0:T(512)S(1)} %copy-done.9), kind=kOutput, calls=%fused_computation | convolution fusion | flops 2822815744 | bytes 15009536 | tf_op jit(solution)/shard_map/dot_general | solution.py:106
  173.0 3.9 %collective-permute-done.17 = bf16[64,2048]{1,0:T(8,128)(2,1)S(1)} collective-permute-done((bf16[64,2048]{1,0:T(8,128)(2,1)S(1)}, bf16[64,2048]{1,0:T(8,128)(2,1)S(1)}, u32[]{:S(2)}, u32[]{:S(2)}) %collective-permute-start.17) | collective-permute-done | bytes 262176 | tf_op jit(solution)/shard_map/ppermute | solution.py:54
  186.3 3.4 %collective-permute-done.14 = bf16[64,2048]{1,0:T(8,128)(2,1)S(1)} collective-permute-done((bf16[64,2048]{1,0:T(8,128)(2,1)S(1)}, bf16[64,2048]{1,0:T(8,128)(2,1)S(1)}, u32[]{:S(2)}, u32[]{:S(2)}) %collective-permute-start.14) | collective-permute-done | bytes 262176 | tf_op jit(solution)/shard_map/ppermute | solution.py:54
  196.9 3.0 %collective-permute-done.32 = bf16[64,2048]{1,0:T(8,128)(2,1)S(1)} collective-permute-done((bf16[64,2048]{1,0:T(8,128)(2,1)S(1)}, bf16[64,2048]{1,0:T(8,128)(2,1)S(1)}, u32[]{:S(2)}, u32[]{:S(2)}) %collective-permute-start.32) | collective-permute-done | bytes 262176 | tf_op jit(solution)/shard_map/ppermute | solution.py:54
  (145 shorter events, 64.8 us)
Async XLA Ops:
  1.2 10.1 %collective-permute-start = (bf16[64,2048]{1,0:T(8,128)(2,1)S(1)}, bf16[64,2048]{1,0:T(8,128)(2,1)S(1)}, u32[]{:S(2)}, u32[]{:S(2)}) collective-permute-start(bf16[64,2048]{1,0:T(8,128)(2,1)S(1)} %get-tuple-element.29), channel_id=1, source_target_pairs={{0,16},{16,0},{1,17},{17,1},{2,18},{18,2},{3,19},{19,3},{4,20},{20... | collective-permute-start | bytes 786440 | tf_op jit(solution)/shard_map/ppermute | solution.py:63
  4.2 107.5 %collective-permute-start.7 = (bf16[2048,768]{1,0:T(8,128)(2,1)}, bf16[2048,768]{1,0:T(8,128)(2,1)}, u32[]{:S(2)}, u32[]{:S(2)}) collective-permute-start(bf16[2048,768]{1,0:T(8,128)(2,1)} %bitcast.79), channel_id=1, source_target_pairs={{0,1},{1,0},{2,3},{3,2},{4,5},{5,4},{6,7},{7,6},{8,9},{9,8},{10,11... | collective-permute-start | bytes 9437192 | tf_op jit(solution)/shard_map/ppermute | solution.py:57
  4.2 110.7 %collective-permute-start.8 = (bf16[2048,768]{1,0:T(8,128)(2,1)}, bf16[2048,768]{1,0:T(8,128)(2,1)}, u32[]{:S(2)}, u32[]{:S(2)}) collective-permute-start(bf16[2048,768]{1,0:T(8,128)(2,1)} %bitcast.78), channel_id=1, source_target_pairs={{0,1},{1,0},{2,3},{3,2},{4,5},{5,4},{6,7},{7,6},{8,9},{9,8},{10,11... | collective-permute-start | bytes 9437192 | tf_op jit(solution)/shard_map/ppermute | solution.py:57
  4.7 11.4 %collective-permute-start.20 = (bf16[64,2048]{1,0:T(8,128)(2,1)S(1)}, bf16[64,2048]{1,0:T(8,128)(2,1)S(1)}, u32[]{:S(2)}, u32[]{:S(2)}) collective-permute-start(bf16[64,2048]{1,0:T(8,128)(2,1)S(1)} %get-tuple-element.30), channel_id=1, source_target_pairs={{0,16},{16,0},{1,17},{17,1},{2,18},{18,2},{3,19},{19,3},{4,20},{20... | collective-permute-start | bytes 786440 | tf_op jit(solution)/shard_map/ppermute | solution.py:63
  11.7 7.4 %collective-permute-start.1 = (bf16[64,2176]{1,0:T(8,128)(2,1)S(1)}, bf16[64,2176]{1,0:T(8,128)(2,1)S(1)}, u32[]{:S(2)}, u32[]{:S(2)}) collective-permute-start(bf16[64,2176]{1,0:T(8,128)(2,1)S(1)} %get-tuple-element.32), channel_id=1, source_target_pairs={{4,8},{5,9},{8,12},{9,13},{12,14},{13,15},{14,10},{15,11},{10,6},{... | collective-permute-start | bytes 835592 | tf_op jit(solution)/shard_map/ppermute | solution.py:54
  13.9 12.5 %collective-permute-start.4 = (bf16[64,2176]{1,0:T(8,128)(2,1)S(1)}, bf16[64,2176]{1,0:T(8,128)(2,1)S(1)}, u32[]{:S(2)}, u32[]{:S(2)}) collective-permute-start(bf16[64,2176]{1,0:T(8,128)(2,1)S(1)} %get-tuple-element.32), channel_id=1, source_target_pairs={{4,0},{5,1},{8,4},{9,5},{12,8},{13,9},{14,12},{15,13},{10,14},{11,... | collective-permute-start | bytes 835592 | tf_op jit(solution)/shard_map/ppermute | solution.py:54
  16.5 8.2 %collective-permute-start.21 = (bf16[64,2176]{1,0:T(8,128)(2,1)S(1)}, bf16[64,2176]{1,0:T(8,128)(2,1)S(1)}, u32[]{:S(2)}, u32[]{:S(2)}) collective-permute-start(bf16[64,2176]{1,0:T(8,128)(2,1)S(1)} %get-tuple-element.34), channel_id=1, source_target_pairs={{4,8},{5,9},{8,12},{9,13},{12,14},{13,15},{14,10},{15,11},{10,6},{... | collective-permute-start | bytes 835592 | tf_op jit(solution)/shard_map/ppermute | solution.py:54
  19.1 20.5 %collective-permute-start.24 = (bf16[64,2176]{1,0:T(8,128)(2,1)S(1)}, bf16[64,2176]{1,0:T(8,128)(2,1)S(1)}, u32[]{:S(2)}, u32[]{:S(2)}) collective-permute-start(bf16[64,2176]{1,0:T(8,128)(2,1)S(1)} %get-tuple-element.34), channel_id=1, source_target_pairs={{4,0},{5,1},{8,4},{9,5},{12,8},{13,9},{14,12},{15,13},{10,14},{11,... | collective-permute-start | bytes 835592 | tf_op jit(solution)/shard_map/ppermute | solution.py:54
  24.8 9.6 %collective-permute-start.2 = (bf16[64,2176]{1,0:T(8,128)(2,1)S(1)}, bf16[64,2176]{1,0:T(8,128)(2,1)S(1)}, u32[]{:S(2)}, u32[]{:S(2)}) collective-permute-start(bf16[64,2176]{1,0:T(8,128)(2,1)S(1)} %collective-permute-done.1), channel_id=1, source_target_pairs={{4,8},{5,9},{8,12},{9,13},{12,14},{13,15},{14,10},{15,11},{10,6},{... | collective-permute-start | bytes 835592 | tf_op jit(solution)/shard_map/ppermute | solution.py:54
  26.5 11.5 %collective-permute-start.22 = (bf16[64,2176]{1,0:T(8,128)(2,1)S(1)}, bf16[64,2176]{1,0:T(8,128)(2,1)S(1)}, u32[]{:S(2)}, u32[]{:S(2)}) collective-permute-start(bf16[64,2176]{1,0:T(8,128)(2,1)S(1)} %collective-permute-done.21), channel_id=1, source_target_pairs={{4,8},{5,9},{8,12},{9,13},{12,14},{13,15},{14,10},{15,11},{10,6},{... | collective-permute-start | bytes 835592 | tf_op jit(solution)/shard_map/ppermute | solution.py:54
  34.4 6.5 %collective-permute-start.5 = (bf16[64,2176]{1,0:T(8,128)(2,1)S(1)}, bf16[64,2176]{1,0:T(8,128)(2,1)S(1)}, u32[]{:S(2)}, u32[]{:S(2)}) collective-permute-start(bf16[64,2176]{1,0:T(8,128)(2,1)S(1)} %collective-permute-done.4), channel_id=1, source_target_pairs={{4,0},{5,1},{8,4},{9,5},{12,8},{13,9},{14,12},{15,13},{10,14},{11,... | collective-permute-start | bytes 835592 | tf_op jit(solution)/shard_map/ppermute | solution.py:54
  38.0 6.5 %collective-permute-start.3 = (bf16[64,2176]{1,0:T(8,128)(2,1)S(1)}, bf16[64,2176]{1,0:T(8,128)(2,1)S(1)}, u32[]{:S(2)}, u32[]{:S(2)}) collective-permute-start(bf16[64,2176]{1,0:T(8,128)(2,1)S(1)} %collective-permute-done.2), channel_id=1, source_target_pairs={{4,8},{5,9},{8,12},{9,13},{12,14},{13,15},{14,10},{15,11},{10,6},{... | collective-permute-start | bytes 835592 | tf_op jit(solution)/shard_map/ppermute | solution.py:54
  39.6 75.3 %collective-permute-start.9 = (bf16[768,2048]{1,0:T(8,128)(2,1)}, bf16[768,2048]{1,0:T(8,128)(2,1)}, u32[]{:S(2)}, u32[]{:S(2)}) collective-permute-start(bf16[768,2048]{1,0:T(8,128)(2,1)} %bitcast.7), channel_id=1, source_target_pairs={{0,1},{1,0},{2,3},{3,2},{4,5},{5,4},{6,7},{7,6},{8,9},{9,8},{10,11... | collective-permute-start | bytes 9437192 | tf_op jit(solution)/shard_map/ppermute | solution.py:57
  40.9 9.6 %collective-permute-start.25 = (bf16[64,2176]{1,0:T(8,128)(2,1)S(1)}, bf16[64,2176]{1,0:T(8,128)(2,1)S(1)}, u32[]{:S(2)}, u32[]{:S(2)}) collective-permute-start(bf16[64,2176]{1,0:T(8,128)(2,1)S(1)} %collective-permute-done.24), channel_id=1, source_target_pairs={{4,0},{5,1},{8,4},{9,5},{12,8},{13,9},{14,12},{15,13},{10,14},{11,... | collective-permute-start | bytes 835592 | tf_op jit(solution)/shard_map/ppermute | solution.py:54
  44.6 10.1 %collective-permute-start.6 = (bf16[64,2176]{1,0:T(8,128)(2,1)S(1)}, bf16[64,2176]{1,0:T(8,128)(2,1)S(1)}, u32[]{:S(2)}, u32[]{:S(2)}) collective-permute-start(bf16[64,2176]{1,0:T(8,128)(2,1)S(1)} %collective-permute-done.5), channel_id=1, source_target_pairs={{4,0},{5,1},{8,4},{9,5},{12,8},{13,9},{14,12},{15,13},{10,14},{11,... | collective-permute-start | bytes 835592 | tf_op jit(solution)/shard_map/ppermute | solution.py:54
  50.5 7.4 %collective-permute-start.23 = (bf16[64,2176]{1,0:T(8,128)(2,1)S(1)}, bf16[64,2176]{1,0:T(8,128)(2,1)S(1)}, u32[]{:S(2)}, u32[]{:S(2)}) collective-permute-start(bf16[64,2176]{1,0:T(8,128)(2,1)S(1)} %collective-permute-done.22), channel_id=1, source_target_pairs={{4,8},{5,9},{8,12},{9,13},{12,14},{13,15},{14,10},{15,11},{10,6},{... | collective-permute-start | bytes 835592 | tf_op jit(solution)/shard_map/ppermute | solution.py:54
  54.7 6.9 %collective-permute-start.26 = (bf16[64,2176]{1,0:T(8,128)(2,1)S(1)}, bf16[64,2176]{1,0:T(8,128)(2,1)S(1)}, u32[]{:S(2)}, u32[]{:S(2)}) collective-permute-start(bf16[64,2176]{1,0:T(8,128)(2,1)S(1)} %collective-permute-done.25), channel_id=1, source_target_pairs={{4,0},{5,1},{8,4},{9,5},{12,8},{13,9},{14,12},{15,13},{10,14},{11,... | collective-permute-start | bytes 835592 | tf_op jit(solution)/shard_map/ppermute | solution.py:54
  65.0 21.7 %collective-permute-start.10 = (bf16[32,2176]{1,0:T(8,128)(2,1)}, bf16[32,2176]{1,0:T(8,128)(2,1)}, u32[]{:S(2)}, u32[]{:S(2)}) collective-permute-start(bf16[32,2176]{1,0:T(8,128)(2,1)} %slice.255), channel_id=1, source_target_pairs={{4,8},{5,9},{8,12},{9,13},{12,14},{13,15},{14,10},{15,11},{10,6},{... | collective-permute-start | bytes 417800 | tf_op jit(solution)/shard_map/ppermute | solution.py:54
  66.5 25.6 %collective-permute-start.11 = (bf16[32,2176]{1,0:T(8,128)(2,1)S(1)}, bf16[32,2176]{1,0:T(8,128)(2,1)S(1)}, u32[]{:S(2)}, u32[]{:S(2)}) collective-permute-start(bf16[32,2176]{1,0:T(8,128)(2,1)S(1)} %slice.256), channel_id=1, source_target_pairs={{4,0},{5,1},{8,4},{9,5},{12,8},{13,9},{14,12},{15,13},{10,14},{11,... | collective-permute-start | bytes 417800 | tf_op jit(solution)/shard_map/ppermute | solution.py:54
  120.0 46.2 %collective-permute-start.12 = (bf16[32,2048]{1,0:T(8,128)(2,1)}, bf16[32,2048]{1,0:T(8,128)(2,1)}, u32[]{:S(2)}, u32[]{:S(2)}) collective-permute-start(bf16[32,2048]{1,0:T(8,128)(2,1)} %get-tuple-element.35), channel_id=1, source_target_pairs={{4,0},{5,1},{8,4},{9,5},{12,8},{13,9},{14,12},{15,13},{10,14},{11,... | collective-permute-start | bytes 393224 | tf_op jit(solution)/shard_map/ppermute | solution.py:54
  120.3 46.0 %collective-permute-start.16 = (bf16[32,2048]{1,0:T(8,128)(2,1)}, bf16[32,2048]{1,0:T(8,128)(2,1)}, u32[]{:S(2)}, u32[]{:S(2)}) collective-permute-start(bf16[32,2048]{1,0:T(8,128)(2,1)} %get-tuple-element.36), channel_id=1, source_target_pairs={{4,8},{5,9},{8,12},{9,13},{12,14},{13,15},{14,10},{15,11},{10,6},{... | collective-permute-start | bytes 393224 | tf_op jit(solution)/shard_map/ppermute | solution.py:54
  148.4 21.4 %collective-permute-start.29 = (bf16[32,2048]{1,0:T(8,128)(2,1)}, bf16[32,2048]{1,0:T(8,128)(2,1)}, u32[]{:S(2)}, u32[]{:S(2)}) collective-permute-start(bf16[32,2048]{1,0:T(8,128)(2,1)} %get-tuple-element.37), channel_id=1, source_target_pairs={{4,0},{5,1},{8,4},{9,5},{12,8},{13,9},{14,12},{15,13},{10,14},{11,... | collective-permute-start | bytes 393224 | tf_op jit(solution)/shard_map/ppermute | solution.py:54
  148.7 21.1 %collective-permute-start.33 = (bf16[32,2048]{1,0:T(8,128)(2,1)}, bf16[32,2048]{1,0:T(8,128)(2,1)}, u32[]{:S(2)}, u32[]{:S(2)}) collective-permute-start(bf16[32,2048]{1,0:T(8,128)(2,1)} %get-tuple-element.38), channel_id=1, source_target_pairs={{4,8},{5,9},{8,12},{9,13},{12,14},{13,15},{14,10},{15,11},{10,6},{... | collective-permute-start | bytes 393224 | tf_op jit(solution)/shard_map/ppermute | solution.py:54
  167.6 9.2 %collective-permute-start.17 = (bf16[64,2048]{1,0:T(8,128)(2,1)S(1)}, bf16[64,2048]{1,0:T(8,128)(2,1)S(1)}, u32[]{:S(2)}, u32[]{:S(2)}) collective-permute-start(bf16[64,2048]{1,0:T(8,128)(2,1)S(1)} %pad_maximum_fusion.1), channel_id=1, source_target_pairs={{4,8},{5,9},{8,12},{9,13},{12,14},{13,15},{14,10},{15,11},{10,6},{... | collective-permute-start | bytes 786440 | tf_op jit(solution)/shard_map/ppermute | solution.py:54
  169.2 9.3 %collective-permute-start.13 = (bf16[64,2048]{1,0:T(8,128)(2,1)S(1)}, bf16[64,2048]{1,0:T(8,128)(2,1)S(1)}, u32[]{:S(2)}, u32[]{:S(2)}) collective-permute-start(bf16[64,2048]{1,0:T(8,128)(2,1)S(1)} %pad_maximum_fusion), channel_id=1, source_target_pairs={{4,0},{5,1},{8,4},{9,5},{12,8},{13,9},{14,12},{15,13},{10,14},{11,... | collective-permute-start | bytes 786440 | tf_op jit(solution)/shard_map/ppermute | solution.py:54
  170.8 11.6 %collective-permute-start.34 = (bf16[64,2048]{1,0:T(8,128)(2,1)S(1)}, bf16[64,2048]{1,0:T(8,128)(2,1)S(1)}, u32[]{:S(2)}, u32[]{:S(2)}) collective-permute-start(bf16[64,2048]{1,0:T(8,128)(2,1)S(1)} %pad_maximum_fusion.3), channel_id=1, source_target_pairs={{4,8},{5,9},{8,12},{9,13},{12,14},{13,15},{14,10},{15,11},{10,6},{... | collective-permute-start | bytes 786440 | tf_op jit(solution)/shard_map/ppermute | solution.py:54
  172.4 11.7 %collective-permute-start.30 = (bf16[64,2048]{1,0:T(8,128)(2,1)S(1)}, bf16[64,2048]{1,0:T(8,128)(2,1)S(1)}, u32[]{:S(2)}, u32[]{:S(2)}) collective-permute-start(bf16[64,2048]{1,0:T(8,128)(2,1)S(1)} %pad_maximum_fusion.2), channel_id=1, source_target_pairs={{4,0},{5,1},{8,4},{9,5},{12,8},{13,9},{14,12},{15,13},{10,14},{11,... | collective-permute-start | bytes 786440 | tf_op jit(solution)/shard_map/ppermute | solution.py:54
  178.6 11.1 %collective-permute-start.14 = (bf16[64,2048]{1,0:T(8,128)(2,1)S(1)}, bf16[64,2048]{1,0:T(8,128)(2,1)S(1)}, u32[]{:S(2)}, u32[]{:S(2)}) collective-permute-start(bf16[64,2048]{1,0:T(8,128)(2,1)S(1)} %get-tuple-element.15), channel_id=1, source_target_pairs={{4,0},{5,1},{8,4},{9,5},{12,8},{13,9},{14,12},{15,13},{10,14},{11,... | collective-permute-start | bytes 786440 | tf_op jit(solution)/shard_map/ppermute | solution.py:54
  179.2 10.5 %collective-permute-start.18 = (bf16[64,2048]{1,0:T(8,128)(2,1)S(1)}, bf16[64,2048]{1,0:T(8,128)(2,1)S(1)}, u32[]{:S(2)}, u32[]{:S(2)}) collective-permute-start(bf16[64,2048]{1,0:T(8,128)(2,1)S(1)} %get-tuple-element.16), channel_id=1, source_target_pairs={{4,8},{5,9},{8,12},{9,13},{12,14},{13,15},{14,10},{15,11},{10,6},{... | collective-permute-start | bytes 786440 | tf_op jit(solution)/shard_map/ppermute | solution.py:54
  184.2 9.0 %collective-permute-start.31 = (bf16[64,2048]{1,0:T(8,128)(2,1)S(1)}, bf16[64,2048]{1,0:T(8,128)(2,1)S(1)}, u32[]{:S(2)}, u32[]{:S(2)}) collective-permute-start(bf16[64,2048]{1,0:T(8,128)(2,1)S(1)} %get-tuple-element.23), channel_id=1, source_target_pairs={{4,0},{5,1},{8,4},{9,5},{12,8},{13,9},{14,12},{15,13},{10,14},{11,... | collective-permute-start | bytes 786440 | tf_op jit(solution)/shard_map/ppermute | solution.py:54
  184.8 8.6 %collective-permute-start.35 = (bf16[64,2048]{1,0:T(8,128)(2,1)S(1)}, bf16[64,2048]{1,0:T(8,128)(2,1)S(1)}, u32[]{:S(2)}, u32[]{:S(2)}) collective-permute-start(bf16[64,2048]{1,0:T(8,128)(2,1)S(1)} %get-tuple-element.24), channel_id=1, source_target_pairs={{4,8},{5,9},{8,12},{9,13},{12,14},{13,15},{14,10},{15,11},{10,6},{... | collective-permute-start | bytes 786440 | tf_op jit(solution)/shard_map/ppermute | solution.py:54
  189.8 6.4 %collective-permute-start.15 = (bf16[64,2048]{1,0:T(8,128)(2,1)S(1)}, bf16[64,2048]{1,0:T(8,128)(2,1)S(1)}, u32[]{:S(2)}, u32[]{:S(2)}) collective-permute-start(bf16[64,2048]{1,0:T(8,128)(2,1)S(1)} %get-tuple-element.13), channel_id=1, source_target_pairs={{4,0},{5,1},{8,4},{9,5},{12,8},{13,9},{14,12},{15,13},{10,14},{11,... | collective-permute-start | bytes 786440 | tf_op jit(solution)/shard_map/ppermute | solution.py:54
  (15 other events, 120.5 us)
where the time goes:
time: 202 us; the launch traced here: 201 us
  matrix products  83.8 us (41%)
  waiting for transfers between devices  57.1 us (28%)
  starting transfers between devices  41.9 us (21%)
  local copies, waits for them, and re-layouts  9.45 us (5%)
  other arithmetic  8.7 us (4%)
    dot_general x8, matrix products, partial(): total += jnp.dot(hidden, down_weight, preferred_element_type=jnp.float32)  56.9 us
    ppermute x32, waiting for transfers between devices, hop(): return lax.ppermute(value, 'expert', pairs)  52.1 us
    ppermute x32, starting transfers between devices, hop(): return lax.ppermute(value, 'expert', pairs)  38.3 us
    dot_general x8, matrix products, partial(): gate_part = jnp.dot(normed, gate_weight, preferred_element_type=jnp.float32)  26 us
    ppermute x2, waiting for transfers between devices, shards(): lax.ppermute(emitted[0, b], 'section', around)  4.95 us
  transfers between devices with their start and end apart: 37, of which 24 were waited for; matrix products, arithmetic and copies ran while one was open for 47% of the time, Pallas kernels for 0%

commit v1 on v0

v1 whole, which is shorter than its diff:
```python
import functools
import math

import jax
import jax.numpy as jnp
from jax import lax
from jax.experimental import pallas as pl
from jax.experimental.pallas import tpu as pltpu
from jax.sharding import PartitionSpec as P

epsilon = 1e-06
CORES = 2
LANES = 128
FF_CHUNK = 256
OUT_CHUNK = 512
VMEM_GRANT = 16 << 20


def level_embedding(levels, entries):
    half_width = entries // 2
    frequency = jnp.exp(-math.log(10000.0) * jnp.arange(half_width, dtype=jnp.float32) / half_width)
    angles = levels.astype(jnp.float32)[:, None] * frequency[None, :]
    return jnp.concatenate([jnp.cos(angles), jnp.sin(angles)], axis=1).astype(jnp.bfloat16)


def chip_cycle(mesh):
    line = list(mesh.devices.reshape(mesh.devices.shape[0], -1)[0])
    chips = len(line) // CORES
    places = [tuple(getattr(line[CORES * c], "coords", (0, 0, c))) for c in range(chips)]
    spans = [sorted({p[d] for p in places}) for d in range(3)]
    wide = [d for d in range(3) if len(spans[d]) > 1]
    if len(set(places)) != chips or len(wide) != 2 or math.prod(len(spans[d]) for d in wide) != chips:
        return list(range(chips))
    rows, cols = wide if len(spans[wide[0]]) % 2 == 0 else wide[::-1]
    if len(spans[rows]) % 2:
        return list(range(chips))
    if len(spans[rows]) > len(spans[cols]) and len(spans[cols]) % 2 == 0:
        rows, cols = cols, rows
    at = {(p[rows], p[cols]): c for c, p in enumerate(places)}
    order = []
    for i, r in enumerate(spans[rows]):
        along = spans[cols][1:]
        order += [(r, c) for c in (along if i % 2 == 0 else along[::-1])]
    order += [(r, spans[cols][0]) for r in reversed(spans[rows])]
    return [at[place] for place in order]


def chunk_of(extent, most):
    return next(c for c in range(min(extent, most), 0, -1) if extent % c == 0)


def group_kernel(sizes, features, experts, ff, me_ref, *refs):
    count = len(sizes)
    blocks, weights = refs[:count], refs[count : count + 6]
    outs = refs[count + 6 : 2 * count + 6]
    rows, hidden = refs[2 * count + 6 :]
    ff_chunk, out_chunk = chunk_of(ff, FF_CHUNK), chunk_of(features, OUT_CHUNK)
    shares = [[], []]
    start = 0
    for block, size in zip(blocks, sizes):
        rows[start : start + size, :] = block[:, :features]
        extra = block[:, features:].astype(jnp.float32)
        lane = lax.broadcasted_iota(jnp.int32, extra.shape, 1)
        for i in range(CORES):
            expert = me_ref[0] ^ i
            named = (lane == expert) | (lane == expert + experts)
            shares[i].append(jnp.sum(jnp.where(named, extra, 0.0), axis=1, keepdims=True))
        start += size
    for i in range(CORES):
        share = jnp.concatenate(shares[i], axis=0)
        gate_weight, up_weight = weights[3 * i], weights[3 * i + 1]
        for c in range(0, ff, ff_chunk):
            part = slice(c, c + ff_chunk)
            gate = jnp.dot(rows[...], gate_weight[:, part], preferred_element_type=jnp.float32)
            up = jnp.dot(rows[...], up_weight[:, part], preferred_element_type=jnp.float32)
            value = gate / (1.0 + jnp.exp(-gate)) * up * share
            hidden[:, i * ff + c : i * ff + c + ff_chunk] = value.astype(jnp.bfloat16)
    for n in range(0, features, out_chunk):
        part = slice(n, n + out_chunk)
        total = jnp.dot(hidden[:, :ff], weights[2][:, part], preferred_element_type=jnp.float32)
        total += jnp.dot(hidden[:, ff:], weights[5][:, part], preferred_element_type=jnp.float32)
        total = total.astype(jnp.bfloat16)
        start = 0
        for out, size in zip(outs, sizes):
            out[:, part] = total[start : start + size]
            start += size


def load_kernel(*refs):
    count = len(refs) // 2
    sems = refs[2 * count]
    copies = [pltpu.make_async_copy(refs[i], refs[count + i], sems.at[i]) for i in range(count)]
    for copy in copies:
        copy.start()
    for copy in copies:
        copy.wait()


def in_vmem(values):
    return pl.pallas_call(
        load_kernel,
        out_shape=[pltpu.VMEM(value.shape, value.dtype) for value in values],
        in_specs=[pl.BlockSpec(memory_space=pltpu.HBM)] * len(values),
        out_specs=[pl.BlockSpec(memory_space=pltpu.VMEM)] * len(values),
        scratch_shapes=[pltpu.SemaphoreType.DMA((len(values),))],
        compiler_params=pltpu.CompilerParams(vmem_limit_bytes=1 << 20),
        cost_estimate=pl.CostEstimate(
            flops=0, bytes_accessed=2 * sum(v.size * v.dtype.itemsize for v in values), transcendentals=0
        ),
    )(*[pltpu.with_memory_space_constraint(value, pltpu.HBM) for value in values])


def group_sums(me, blocks, weights, experts):
    sizes = [block.shape[0] for block in blocks]
    total = sum(sizes)
    features, ff = weights[0].shape
    near = pl.BlockSpec(memory_space=pltpu.VMEM)
    operands = [pltpu.with_memory_space_constraint(a, pltpu.VMEM) for a in (*blocks, *weights)]
    return pl.pallas_call(
        functools.partial(group_kernel, sizes, features, experts, ff),
        out_shape=[pltpu.VMEM((size, features), jnp.bfloat16) for size in sizes],
        in_specs=[pl.BlockSpec(memory_space=pltpu.SMEM)] + [near] * len(operands),
        out_specs=[near] * len(sizes),
        scratch_shapes=[
            pltpu.VMEM((total, features), jnp.bfloat16),
            pltpu.VMEM((total, CORES * ff), jnp.bfloat16),
        ],
        compiler_params=pltpu.CompilerParams(vmem_limit_bytes=VMEM_GRANT),
        cost_estimate=pl.CostEstimate(
            flops=6 * CORES * total * features * ff,
            bytes_accessed=4 * total * features,
            transcendentals=CORES * total * ff,
        ),
    )(me, *operands)


def build(cycle):
    chips = len(cycle)
    experts = chips * CORES
    far = chips // 2
    halved = chips % 2 == 0

    def hop(value, step):
        pairs = [
            (cycle[i] * CORES + c, cycle[(i + step) % chips] * CORES + c)
            for i in range(chips)
            for c in range(CORES)
        ]
        return lax.ppermute(value, "expert", pairs)

    def swap(value):
        return lax.ppermute(value, "expert", [(i, i ^ 1) for i in range(experts)])

    def shards(emitted, levels, expert_ids, gate_values, w_gate, w_up, w_down, w_mod):
        sections = lax.axis_size("section")
        batches, tok_rows, features = emitted.shape[1:]
        half = tok_rows // 2
        around = [(s, (s + 1) % sections) for s in range(sections)]
        arrived = [lax.ppermute(emitted[0, b], "section", around) for b in range(batches)]
        mine = (w_gate[0, 0], w_up[0, 0], w_down[0, 0])
        weights = mine + tuple(swap(w) for w in mine)
        me = lax.axis_index("expert").astype(jnp.int32).reshape(1)
        mod_weight = w_mod[0]
        lanes = -(-2 * experts // LANES) * LANES

        def payload(b):
            embed = level_embedding(levels[0, b], mod_weight.shape[0])
            modulation = jnp.dot(embed, mod_weight, preferred_element_type=jnp.float32)
            values = arrived[b].astype(jnp.float32)
            mean_square = jnp.mean(values * values, axis=1, keepdims=True)
            normed = (
                values * lax.rsqrt(mean_square + epsilon) * (1.0 + modulation[:, :features])
                + modulation[:, features:]
            ).astype(jnp.bfloat16)
            named = expert_ids[0, b][:, :, None] == jnp.arange(experts, dtype=jnp.int32)
            shares = jnp.sum(jnp.where(named, gate_values[0, b][:, :, None], 0.0), axis=1)
            high = lax.reduce_precision(shares, 8, 7)
            extra = jnp.concatenate([high, shares - high], axis=1).astype(jnp.bfloat16)
            extra = jnp.pad(extra, ((0, 0), (0, lanes - extra.shape[1])))
            return jnp.concatenate([normed, extra], axis=1)

        def added(a, b):
            return (a.astype(jnp.float32) + b.astype(jnp.float32)).astype(jnp.bfloat16)

        def tied(values):
            return lax.optimization_barrier(values)

        chains = [(b, step) for b in range(batches) for step in (1, -1)]
        first_half = (batches + 1) // 2
        top = {
            (b, step): far if not halved or (step == 1) == (b < first_half) else far - 1 for b, step in chains
        }
        own = [payload(b) for b in range(batches)]
        blocks = {(*chain, 0): own[chain[0]] for chain in chains}
        sums = {}

        def add_sums(keys):
            for key, value in zip(keys, group_sums(me, [blocks[key] for key in keys], weights, experts)):
                sums[key] = value

        for k in range(1, far + 1):
            moving = [chain for chain in chains if top[chain] >= k]
            sent = [blocks[(*chain, k - 1)] for chain in moving]
            if k > 1:
                sent = tied(sent)
            got = [hop(value, chain[1]) for value, chain in zip(sent, moving)]
            keys = [(*chain, k - 1) for chain in chains]
            if k == 1:
                weights = in_vmem(weights)
                got, weights = tied((got, weights))
            elif k == 2:
                keys = [(b, 1, 0) for b in range(batches)] + [(*chain, 1) for chain in chains]
                add_sums(keys)
                got, done = tied((got, [sums[key] for key in keys]))
                sums.update(zip(keys, done))
            else:
                add_sums(keys)
                got, done = tied((got, [sums[key] for key in keys]))
                sums.update(zip(keys, done))
            blocks.update({(*chain, k): value for chain, value in zip(moving, got)})

        last_keys = [(*chain, far) for chain in chains if top[chain] == far]
        add_sums(last_keys)
        total = {}
        for chain in chains:
            value = sums[(*chain, top[chain])]
            for place in range(top[chain] - 1, -1, -1):
                value = hop(value, -chain[1])
                if place:
                    value = added(value, sums[(*chain, place)])
            total[chain] = value
        results = []
        for b in range(batches):
            value = arrived[b].astype(jnp.float32) + sums[(b, 1, 0)].astype(jnp.float32)
            for step in (1, -1):
                value += total[b, step].astype(jnp.float32)
            results.append(value.astype(jnp.bfloat16))
        return jnp.stack(results)[None]

    return shards


def solution(mesh):
    placed = (
        P("section", None, "expert", None),
        P("section", None, "expert"),
        P("section", None, "expert", None),
        P("section", None, "expert", None),
        P("section", "expert", None, None),
        P("section", "expert", None, None),
        P("section", "expert", None, None),
        P("section", None, None),
    )
    return jax.shard_map(
        build(chip_cycle(mesh)),
        mesh=mesh,
        in_specs=placed,
        out_specs=P("section", None, "expert", None),
        check_vma=False,
    )
```

time: 202 us -> 110 us (0.54)
  matrix products: 83.8 us -> 0.96 us
  Pallas kernels: 0 us -> 28.1 us
  waiting for transfers between devices: 57.1 us -> 37.2 us
  starting transfers between devices: 41.9 us -> 35.3 us
  local copies, waits for them, and re-layouts: 9.45 us -> 3.66 us
  other arithmetic: 8.7 us -> 3.74 us
    dot_general x16 -> x0, matrix products: 82.9 us -> none  [the longest x8 56.9 us: partial(): total += jnp.dot(hidden, down_weight, preferred_element_type=jnp.float32)]
    pallas_call x0 -> x5, Pallas kernels: none -> 28.1 us  [the longest x4 21.6 us: group_sums(): pl.pallas_call(functools.partial(group_kernel, sizes, features, experts,...]
    ppermute x32 -> x28, waiting for transfers between devices: 52.1 us -> 33.2 us  [hop(): return lax.ppermute(value, 'expert', pairs)]
    ppermute x32 -> x28, starting transfers between devices: 38.3 us -> 31.7 us  [hop(): return lax.ppermute(value, 'expert', pairs)]
    slice x9 -> x2, local copies, waits for them, and re-layouts: 6.69 us -> 1.55 us  [the longest x1 0.77 us: payload(): named = expert_ids[0, b][:, :, None] == jnp.arange(experts, dtype=jnp.int32)]
    convert_element_type x6 -> x10, other arithmetic: 2.82 us -> 0.65 us  [added(): return (a.astype(jnp.float32) + b.astype(jnp.float32)).astype(jnp.bfloat16)]
    reduce_sum x4 -> x2, other arithmetic: 2.1 us -> 0.03 us  [payload(): jnp.sum(jnp.where(named, gate_values[0, b][:, :, None], 0.0), axis=1)]
  transfers between devices with their start and end apart: 37 -> 33, of which waited for: 24 -> 14; matrix products, arithmetic and copies ran while one was open for 47% -> 5% of each run, Pallas kernels for 0% -> 23%
where the time goes in v1:
time: 110 us; the launch traced here: 109 us
  waiting for transfers between devices  37.2 us (34%)
  starting transfers between devices  35.3 us (32%)
  Pallas kernels  28.1 us (26%)
  other arithmetic  3.74 us (3%)
  local copies, waits for them, and re-layouts  3.66 us (3%)
    ppermute x28, waiting for transfers between devices, hop(): return lax.ppermute(value, 'expert', pairs)  33.2 us
    ppermute x28, starting transfers between devices, hop(): return lax.ppermute(value, 'expert', pairs)  31.7 us
    pallas_call x4, Pallas kernels, group_sums(): pl.pallas_call(functools.partial(group_kernel, sizes, features, experts,...  21.6 us
    pallas_call x1, Pallas kernels, in_vmem(): pl.pallas_call(load_kernel, out_shape=[pltpu.VMEM(value.shape, value.dtyp...  6.49 us
    ppermute x2, waiting for transfers between devices, shards(): lax.ppermute(emitted[0, b], 'section', around)  4.03 us
    ppermute x2, starting transfers between devices, shards(): lax.ppermute(emitted[0, b], 'section', around)  3.08 us
  transfers between devices with their start and end apart: 33, of which 14 were waited for; matrix products, arithmetic and copies ran while one was open for 5% of the time, Pallas kernels for 23%

profile of v1, /device:TPU:0, one launch (start us, length us, event | category | flops | bytes accessed | tf_op | source)
XLA Modules:
  0.0 109.3 jit_solution(3170237144360704636)
XLA Ops:
  1.2 3.0 %collective-permute-start.3 = (bf16[64,2048]{1,0:T(8,128)(2,1)S(1)}, bf16[64,2048]{1,0:T(8,128)(2,1)S(1)}, u32[]{:S(2)}, u32[]{:S(2)}) collective-permute-start(bf16[64,2048]{1,0:T(8,128)(2,1)S(1)} %get-tuple-element.137), channel_id=1, source_target_pairs={{0,16},{16,0},{1,17},{17,1},{2,18},{18,2},{3,19},{19,3},{4,20},{20... | collective-permute-start | bytes 786440 | tf_op jit(solution)/shard_map/ppermute | solution.py:159
  9.0 2.3 %collective-permute-done.3 = bf16[64,2048]{1,0:T(8,128)(2,1)S(1)} collective-permute-done((bf16[64,2048]{1,0:T(8,128)(2,1)S(1)}, bf16[64,2048]{1,0:T(8,128)(2,1)S(1)}, u32[]{:S(2)}, u32[]{:S(2)}) %collective-permute-start.3) | collective-permute-done | bytes 262176 | tf_op jit(solution)/shard_map/ppermute | solution.py:159
  12.3 2.2 %collective-permute-start.4 = (bf16[64,2176]{1,0:T(8,128)(2,1)S(1)}, bf16[64,2176]{1,0:T(8,128)(2,1)S(1)}, u32[]{:S(2)}, u32[]{:S(2)}) collective-permute-start(bf16[64,2176]{1,0:T(8,128)(2,1)S(1)} %pad_maximum_fusion.1.refs_1_), channel_id=1, source_target_pairs={{4,8},{5,9},{8,12},{9,13},{12,14},{13,15},{14,10},{15,11},{10,6},{... | collective-permute-start | bytes 835592 | tf_op jit(solution)/shard_map/ppermute | solution.py:149
  14.5 1.7 %collective-permute-done = bf16[64,2048]{1,0:T(8,128)(2,1)S(1)} collective-permute-done((bf16[64,2048]{1,0:T(8,128)(2,1)S(1)}, bf16[64,2048]{1,0:T(8,128)(2,1)S(1)}, u32[]{:S(2)}, u32[]{:S(2)}) %collective-permute-start) | collective-permute-done | bytes 262176 | tf_op jit(solution)/shard_map/ppermute | solution.py:159
  16.2 1.8 %collective-permute-start.5 = (bf16[64,2176]{1,0:T(8,128)(2,1)S(1)}, bf16[64,2176]{1,0:T(8,128)(2,1)S(1)}, u32[]{:S(2)}, u32[]{:S(2)}) collective-permute-start(bf16[64,2176]{1,0:T(8,128)(2,1)S(1)} %pad_maximum_fusion.1.refs_1_), channel_id=1, source_target_pairs={{4,0},{5,1},{8,4},{9,5},{12,8},{13,9},{14,12},{15,13},{10,14},{11,... | collective-permute-start | bytes 835592 | tf_op jit(solution)/shard_map/ppermute | solution.py:149
  18.9 1.4 %collective-permute-start.2 = (bf16[64,2176]{1,0:T(8,128)(2,1)S(1)}, bf16[64,2176]{1,0:T(8,128)(2,1)}, u32[]{:S(2)}, u32[]{:S(2)}) collective-permute-start(bf16[64,2176]{1,0:T(8,128)(2,1)S(1)} %pad_maximum_fusion.refs_0_), channel_id=1, source_target_pairs={{4,0},{5,1},{8,4},{9,5},{12,8},{13,9},{14,12},{15,13},{10,14},{11,... | collective-permute-start | bytes 835592 | tf_op jit(solution)/shard_map/ppermute | solution.py:149
  20.4 6.5 %shard_map.82 = (bf16[2048,768]{1,0:T(8,128)(2,1)S(1)}, bf16[2048,768]{1,0:T(8,128)(2,1)S(1)}, bf16[768,2048]{1,0:T(8,128)(2,1)S(1)}, bf16[2048,768]{1,0:T(8,128...) custom-call(bf16[2048,768]{1,0:T(8,128)(2,1)} %bitcast.32, bf16[2048,768]{1,0:T(8,128)(2,1)} %bitcast.34, ...), custom_call_target="tpu_custom_call" | custom-call | bytes 37748736 | tf_op jit(solution)/shard_map/pallas_call | solution.py:100
  26.9 3.2 %collective-permute-done.2.refs_3_ = bf16[64,2176]{1,0:T(8,128)(2,1)} collective-permute-done((bf16[64,2176]{1,0:T(8,128)(2,1)S(1)}, bf16[64,2176]{1,0:T(8,128)(2,1)}, u32[]{:S(2)}, u32[]{:S(2)}) %collective-permute-start.2) | collective-permute-done | bytes 278560 | tf_op jit(solution)/shard_map/ppermute | solution.py:149
  30.1 1.5 %collective-permute-start.10 = (bf16[64,2176]{1,0:T(8,128)(2,1)}, bf16[64,2176]{1,0:T(8,128)(2,1)S(1)}, u32[]{:S(2)}, u32[]{:S(2)}) collective-permute-start(bf16[64,2176]{1,0:T(8,128)(2,1)} %collective-permute-done.2.refs_3_), channel_id=1, source_target_pairs={{4,0},{5,1},{8,4},{9,5},{12,8},{13,9},{14,12},{15,13},{10,14},{11,... | collective-permute-start | bytes 835592 | tf_op jit(solution)/shard_map/ppermute | solution.py:149
  32.1 1.5 %collective-permute-start.12 = (bf16[64,2176]{1,0:T(8,128)(2,1)S(1)}, bf16[64,2176]{1,0:T(8,128)(2,1)S(1)}, u32[]{:S(2)}, u32[]{:S(2)}) collective-permute-start(bf16[64,2176]{1,0:T(8,128)(2,1)S(1)} %collective-permute-done.5.refs_5_), channel_id=1, source_target_pairs={{4,0},{5,1},{8,4},{9,5},{12,8},{13,9},{14,12},{15,13},{10,14},{11,... | collective-permute-start | bytes 835592 | tf_op jit(solution)/shard_map/ppermute | solution.py:149
  34.1 8.5 %shard_map.83 = (bf16[64,2048]{1,0:T(8,128)(2,1)S(1)}, bf16[64,2048]{1,0:T(8,128)(2,1)S(1)}, bf16[64,2048]{1,0:T(8,128)(2,1)S(1)}, bf16[64,2048]{1,0:T(8,128)(2,...) custom-call(s32[1]{0:T(128)} %bitcast.12.me_ref, bf16[64,2176]{1,0:T(8,128)(2,1)S(1)} %pad_maximum_fusion.refs_0_, ...), custom_call_target="tpu_custom_call" | custom-call | flops 7247757312 | bytes 3145728 | tf_op jit(solution)/shard_map/pallas_call | solution.py:119
  44.9 1.5 %collective-permute-start.14 = (bf16[64,2176]{1,0:T(8,128)(2,1)S(1)}, bf16[64,2176]{1,0:T(8,128)(2,1)S(1)}, u32[]{:S(2)}, u32[]{:S(2)}) collective-permute-start(bf16[64,2176]{1,0:T(8,128)(2,1)S(1)} %collective-permute-done.10.refs_1_), channel_id=1, source_target_pairs={{4,0},{5,1},{8,4},{9,5},{12,8},{13,9},{14,12},{15,13},{10,14},{11,... | collective-permute-start | bytes 835592 | tf_op jit(solution)/shard_map/ppermute | solution.py:149
  46.9 1.5 %collective-permute-start.16 = (bf16[64,2176]{1,0:T(8,128)(2,1)S(1)}, bf16[64,2176]{1,0:T(8,128)(2,1)S(1)}, u32[]{:S(2)}, u32[]{:S(2)}) collective-permute-start(bf16[64,2176]{1,0:T(8,128)(2,1)S(1)} %collective-permute-done.12.refs_3_), channel_id=1, source_target_pairs={{4,0},{5,1},{8,4},{9,5},{12,8},{13,9},{14,12},{15,13},{10,14},{11,... | collective-permute-start | bytes 835592 | tf_op jit(solution)/shard_map/ppermute | solution.py:149
  48.4 5.2 %shard_map.84 = (bf16[64,2048]{1,0:T(8,128)(2,1)S(1)}, bf16[64,2048]{1,0:T(8,128)(2,1)S(1)}, bf16[64,2048]{1,0:T(8,128)(2,1)S(1)}, bf16[64,2048]{1,0:T(8,128)(2,1)S(1)}) custom-call(s32[1]{0:T(128)} %bitcast.12.me_ref, bf16[64,2176]{1,0:T(8,128)(2,1)S(1)} %collective-permute-done.9.refs_0_, bf16[64,2176]{1,0:T(8,128)(2,1)S(1)} %collective-permute-done.10.refs_1_, ...), custom_call_target="tpu_custom_call" | custom-call | flops 4831838208 | bytes 2097152 | tf_op jit(solution)/shard_map/pallas_call | solution.py:119
  53.6 3.4 %collective-permute-done.15.refs_2_ = bf16[64,2176]{1,0:T(8,128)(2,1)S(1)} collective-permute-done((bf16[64,2176]{1,0:T(8,128)(2,1)S(1)}, bf16[64,2176]{1,0:T(8,128)(2,1)S(1)}, u32[]{:S(2)}, u32[]{:S(2)}) %collective-permute-start.15) | collective-permute-done | bytes 278560 | tf_op jit(solution)/shard_map/ppermute | solution.py:149
  57.6 1.4 %collective-permute-start.18 = (bf16[64,2176]{1,0:T(8,128)(2,1)S(1)}, bf16[64,2176]{1,0:T(8,128)(2,1)S(1)}, u32[]{:S(2)}, u32[]{:S(2)}) collective-permute-start(bf16[64,2176]{1,0:T(8,128)(2,1)S(1)} %collective-permute-done.16.refs_3_), channel_id=1, source_target_pairs={{4,0},{5,1},{8,4},{9,5},{12,8},{13,9},{14,12},{15,13},{10,14},{11,... | collective-permute-start | bytes 835592 | tf_op jit(solution)/shard_map/ppermute | solution.py:149
  59.0 5.1 %shard_map.85 = (bf16[64,2048]{1,0:T(8,128)(2,1)S(1)}, bf16[64,2048]{1,0:T(8,128)(2,1)S(1)}, bf16[64,2048]{1,0:T(8,128)(2,1)S(1)}, bf16[64,2048]{1,0:T(8,128)(2,1)S(1)}) custom-call(s32[1]{0:T(128)} %bitcast.12.me_ref, bf16[64,2176]{1,0:T(8,128)(2,1)S(1)} %collective-permute-done.13.refs_0_, bf16[64,2176]{1,0:T(8,128)(2,1)S(1)} %collective-permute-done.14.refs_1_, ...), custom_call_target="tpu_custom_call" | custom-call | flops 4831838208 | bytes 2097152 | tf_op jit(solution)/shard_map/pallas_call | solution.py:119
  64.2 2.8 %shard_map.86 = (bf16[64,2048]{1,0:T(8,128)(2,1)S(1)}, bf16[64,2048]{1,0:T(8,128)(2,1)S(1)}) custom-call(s32[1]{0:T(128)} %bitcast.12.me_ref, bf16[64,2176]{1,0:T(8,128)(2,1)S(1)} %collective-permute-done.17.refs_0_, bf16[64,2176]{1,0:T(8,128)(2,1)S(1)} %collective-permute-done.18.refs_1_, bf16[2048,768]{1,0:T(8,128)(2,1)S(1)} %get-tuple-element.85.refs_6_.refs_4_.refs_2_, ...), custom_call_target="tpu_custom_call" | custom-call | flops 2415919104 | bytes 1048576 | tf_op jit(solution)/shard_map/pallas_call | solution.py:119
  66.9 1.8 %collective-permute-start.19 = (bf16[64,2048]{1,0:T(8,128)(2,1)S(1)}, bf16[64,2048]{1,0:T(8,128)(2,1)S(1)}, u32[]{:S(2)}, u32[]{:S(2)}) collective-permute-start(bf16[64,2048]{1,0:T(8,128)(2,1)S(1)} %get-tuple-element.122), channel_id=1, source_target_pairs={{4,0},{5,1},{8,4},{9,5},{12,8},{13,9},{14,12},{15,13},{10,14},{11,... | collective-permute-start | bytes 786440 | tf_op jit(solution)/shard_map/ppermute | solution.py:149
  69.0 1.7 %collective-permute-start.26 = (bf16[64,2048]{1,0:T(8,128)(2,1)S(1)}, bf16[64,2048]{1,0:T(8,128)(2,1)S(1)}, u32[]{:S(2)}, u32[]{:S(2)}) collective-permute-start(bf16[64,2048]{1,0:T(8,128)(2,1)S(1)} %get-tuple-element.130), channel_id=1, source_target_pairs={{4,0},{5,1},{8,4},{9,5},{12,8},{13,9},{14,12},{15,13},{10,14},{11,... | collective-permute-start | bytes 786440 | tf_op jit(solution)/shard_map/ppermute | solution.py:149
  71.2 5.0 %collective-permute-done.19 = bf16[64,2048]{1,0:T(8,128)(2,1)S(1)} collective-permute-done((bf16[64,2048]{1,0:T(8,128)(2,1)S(1)}, bf16[64,2048]{1,0:T(8,128)(2,1)S(1)}, u32[]{:S(2)}, u32[]{:S(2)}) %collective-permute-start.19) | collective-permute-done | bytes 262176 | tf_op jit(solution)/shard_map/ppermute | solution.py:149
  76.3 1.8 %collective-permute-start.20 = (bf16[64,2048]{1,0:T(8,128)(2,1)S(1)}, bf16[64,2048]{1,0:T(8,128)(2,1)S(1)}, u32[]{:S(2)}, u32[]{:S(2)}) collective-permute-start(bf16[64,2048]{1,0:T(8,128)(2,1)S(1)} %add_convert_fusion.9), channel_id=1, source_target_pairs={{4,0},{5,1},{8,4},{9,5},{12,8},{13,9},{14,12},{15,13},{10,14},{11,... | collective-permute-start | bytes 786440 | tf_op jit(solution)/shard_map/ppermute | solution.py:149
  78.7 3.2 %collective-permute-done.26 = bf16[64,2048]{1,0:T(8,128)(2,1)S(1)} collective-permute-done((bf16[64,2048]{1,0:T(8,128)(2,1)S(1)}, bf16[64,2048]{1,0:T(8,128)(2,1)S(1)}, u32[]{:S(2)}, u32[]{:S(2)}) %collective-permute-start.26) | collective-permute-done | bytes 262176 | tf_op jit(solution)/shard_map/ppermute | solution.py:149
  81.9 1.8 %collective-permute-start.27 = (bf16[64,2048]{1,0:T(8,128)(2,1)S(1)}, bf16[64,2048]{1,0:T(8,128)(2,1)S(1)}, u32[]{:S(2)}, u32[]{:S(2)}) collective-permute-start(bf16[64,2048]{1,0:T(8,128)(2,1)S(1)} %add_convert_fusion.4), channel_id=1, source_target_pairs={{4,0},{5,1},{8,4},{9,5},{12,8},{13,9},{14,12},{15,13},{10,14},{11,... | collective-permute-start | bytes 786440 | tf_op jit(solution)/shard_map/ppermute | solution.py:149
  84.3 3.2 %collective-permute-done.20 = bf16[64,2048]{1,0:T(8,128)(2,1)S(1)} collective-permute-done((bf16[64,2048]{1,0:T(8,128)(2,1)S(1)}, bf16[64,2048]{1,0:T(8,128)(2,1)S(1)}, u32[]{:S(2)}, u32[]{:S(2)}) %collective-permute-start.20) | collective-permute-done | bytes 262176 | tf_op jit(solution)/shard_map/ppermute | solution.py:149
  87.5 1.8 %collective-permute-start.21 = (bf16[64,2048]{1,0:T(8,128)(2,1)S(1)}, bf16[64,2048]{1,0:T(8,128)(2,1)S(1)}, u32[]{:S(2)}, u32[]{:S(2)}) collective-permute-start(bf16[64,2048]{1,0:T(8,128)(2,1)S(1)} %add_convert_fusion.8), channel_id=1, source_target_pairs={{4,0},{5,1},{8,4},{9,5},{12,8},{13,9},{14,12},{15,13},{10,14},{11,... | collective-permute-start | bytes 786440 | tf_op jit(solution)/shard_map/ppermute | solution.py:149
  89.9 3.2 %collective-permute-done.27 = bf16[64,2048]{1,0:T(8,128)(2,1)S(1)} collective-permute-done((bf16[64,2048]{1,0:T(8,128)(2,1)S(1)}, bf16[64,2048]{1,0:T(8,128)(2,1)S(1)}, u32[]{:S(2)}, u32[]{:S(2)}) %collective-permute-start.27) | collective-permute-done | bytes 262176 | tf_op jit(solution)/shard_map/ppermute | solution.py:149
  93.1 1.8 %collective-permute-start.28 = (bf16[64,2048]{1,0:T(8,128)(2,1)S(1)}, bf16[64,2048]{1,0:T(8,128)(2,1)S(1)}, u32[]{:S(2)}, u32[]{:S(2)}) collective-permute-start(bf16[64,2048]{1,0:T(8,128)(2,1)S(1)} %add_convert_fusion.3), channel_id=1, source_target_pairs={{4,0},{5,1},{8,4},{9,5},{12,8},{13,9},{14,12},{15,13},{10,14},{11,... | collective-permute-start | bytes 786440 | tf_op jit(solution)/shard_map/ppermute | solution.py:149
  95.5 2.6 %collective-permute-done.21 = bf16[64,2048]{1,0:T(8,128)(2,1)S(1)} collective-permute-done((bf16[64,2048]{1,0:T(8,128)(2,1)S(1)}, bf16[64,2048]{1,0:T(8,128)(2,1)S(1)}, u32[]{:S(2)}, u32[]{:S(2)}) %collective-permute-start.21) | collective-permute-done | bytes 262176 | tf_op jit(solution)/shard_map/ppermute | solution.py:149
  99.4 2.4 %collective-permute-done.31 = bf16[64,2048]{1,0:T(8,128)(2,1)S(1)} collective-permute-done((bf16[64,2048]{1,0:T(8,128)(2,1)S(1)}, bf16[64,2048]{1,0:T(8,128)(2,1)S(1)}, u32[]{:S(2)}, u32[]{:S(2)}) %collective-permute-start.31) | collective-permute-done | bytes 262176 | tf_op jit(solution)/shard_map/ppermute | solution.py:149
  102.7 1.8 %collective-permute-done.22 = bf16[64,2048]{1,0:T(8,128)(2,1)S(1)} collective-permute-done((bf16[64,2048]{1,0:T(8,128)(2,1)S(1)}, bf16[64,2048]{1,0:T(8,128)(2,1)S(1)}, u32[]{:S(2)}, u32[]{:S(2)}) %collective-permute-start.22) | collective-permute-done | bytes 262176 | tf_op jit(solution)/shard_map/ppermute | solution.py:149
  104.7 3.6 %collective-permute-done.32 = bf16[64,2048]{1,0:T(8,128)(2,1)S(1)} collective-permute-done((bf16[64,2048]{1,0:T(8,128)(2,1)S(1)}, bf16[64,2048]{1,0:T(8,128)(2,1)S(1)}, u32[]{:S(2)}, u32[]{:S(2)}) %collective-permute-start.32) | collective-permute-done | bytes 262176 | tf_op jit(solution)/shard_map/ppermute | solution.py:149
  (92 shorter events, 19.0 us)
Async XLA Ops:
  1.2 10.1 %collective-permute-start.3 = (bf16[64,2048]{1,0:T(8,128)(2,1)S(1)}, bf16[64,2048]{1,0:T(8,128)(2,1)S(1)}, u32[]{:S(2)}, u32[]{:S(2)}) collective-permute-start(bf16[64,2048]{1,0:T(8,128)(2,1)S(1)} %get-tuple-element.137), channel_id=1, source_target_pairs={{0,16},{16,0},{1,17},{17,1},{2,18},{18,2},{3,19},{19,3},{4,20},{20... | collective-permute-start | bytes 786440 | tf_op jit(solution)/shard_map/ppermute | solution.py:159
  4.2 11.9 %collective-permute-start = (bf16[64,2048]{1,0:T(8,128)(2,1)S(1)}, bf16[64,2048]{1,0:T(8,128)(2,1)S(1)}, u32[]{:S(2)}, u32[]{:S(2)}) collective-permute-start(bf16[64,2048]{1,0:T(8,128)(2,1)S(1)} %get-tuple-element.138), channel_id=1, source_target_pairs={{0,16},{16,0},{1,17},{17,1},{2,18},{18,2},{3,19},{19,3},{4,20},{20... | collective-permute-start | bytes 786440 | tf_op jit(solution)/shard_map/ppermute | solution.py:159
  4.3 14.0 %collective-permute-start.6 = (bf16[2048,768]{1,0:T(8,128)(2,1)}, bf16[2048,768]{1,0:T(8,128)(2,1)}, u32[]{:S(2)}, u32[]{:S(2)}) collective-permute-start(bf16[2048,768]{1,0:T(8,128)(2,1)} %bitcast.31), channel_id=1, source_target_pairs={{0,1},{1,0},{2,3},{3,2},{4,5},{5,4},{6,7},{7,6},{8,9},{9,8},{10,11... | collective-permute-start | bytes 9437192 | tf_op jit(solution)/shard_map/ppermute | solution.py:152
  4.3 14.6 %collective-permute-start.7 = (bf16[2048,768]{1,0:T(8,128)(2,1)}, bf16[2048,768]{1,0:T(8,128)(2,1)}, u32[]{:S(2)}, u32[]{:S(2)}) collective-permute-start(bf16[2048,768]{1,0:T(8,128)(2,1)} %bitcast.33), channel_id=1, source_target_pairs={{0,1},{1,0},{2,3},{3,2},{4,5},{5,4},{6,7},{7,6},{8,9},{9,8},{10,11... | collective-permute-start | bytes 9437192 | tf_op jit(solution)/shard_map/ppermute | solution.py:152
  4.8 15.6 %collective-permute-start.8 = (bf16[768,2048]{1,0:T(8,128)(2,1)}, bf16[768,2048]{1,0:T(8,128)(2,1)}, u32[]{:S(2)}, u32[]{:S(2)}) collective-permute-start(bf16[768,2048]{1,0:T(8,128)(2,1)} %bitcast.35), channel_id=1, source_target_pairs={{0,1},{1,0},{2,3},{3,2},{4,5},{5,4},{6,7},{7,6},{8,9},{9,8},{10,11... | collective-permute-start | bytes 9437192 | tf_op jit(solution)/shard_map/ppermute | solution.py:152
  12.3 14.6 %collective-permute-start.4 = (bf16[64,2176]{1,0:T(8,128)(2,1)S(1)}, bf16[64,2176]{1,0:T(8,128)(2,1)S(1)}, u32[]{:S(2)}, u32[]{:S(2)}) collective-permute-start(bf16[64,2176]{1,0:T(8,128)(2,1)S(1)} %pad_maximum_fusion.1.refs_1_), channel_id=1, source_target_pairs={{4,8},{5,9},{8,12},{9,13},{12,14},{13,15},{14,10},{15,11},{10,6},{... | collective-permute-start | bytes 835592 | tf_op jit(solution)/shard_map/ppermute | solution.py:149
  16.2 10.7 %collective-permute-start.5 = (bf16[64,2176]{1,0:T(8,128)(2,1)S(1)}, bf16[64,2176]{1,0:T(8,128)(2,1)S(1)}, u32[]{:S(2)}, u32[]{:S(2)}) collective-permute-start(bf16[64,2176]{1,0:T(8,128)(2,1)S(1)} %pad_maximum_fusion.1.refs_1_), channel_id=1, source_target_pairs={{4,0},{5,1},{8,4},{9,5},{12,8},{13,9},{14,12},{15,13},{10,14},{11,... | collective-permute-start | bytes 835592 | tf_op jit(solution)/shard_map/ppermute | solution.py:149
  18.3 8.6 %collective-permute-start.1 = (bf16[64,2176]{1,0:T(8,128)(2,1)S(1)}, bf16[64,2176]{1,0:T(8,128)(2,1)S(1)}, u32[]{:S(2)}, u32[]{:S(2)}) collective-permute-start(bf16[64,2176]{1,0:T(8,128)(2,1)S(1)} %pad_maximum_fusion.refs_0_), channel_id=1, source_target_pairs={{4,8},{5,9},{8,12},{9,13},{12,14},{13,15},{14,10},{15,11},{10,6},{... | collective-permute-start | bytes 835592 | tf_op jit(solution)/shard_map/ppermute | solution.py:149
  18.9 11.1 %collective-permute-start.2 = (bf16[64,2176]{1,0:T(8,128)(2,1)S(1)}, bf16[64,2176]{1,0:T(8,128)(2,1)}, u32[]{:S(2)}, u32[]{:S(2)}) collective-permute-start(bf16[64,2176]{1,0:T(8,128)(2,1)S(1)} %pad_maximum_fusion.refs_0_), channel_id=1, source_target_pairs={{4,0},{5,1},{8,4},{9,5},{12,8},{13,9},{14,12},{15,13},{10,14},{11,... | collective-permute-start | bytes 835592 | tf_op jit(solution)/shard_map/ppermute | solution.py:149
  30.1 12.6 %collective-permute-start.10 = (bf16[64,2176]{1,0:T(8,128)(2,1)}, bf16[64,2176]{1,0:T(8,128)(2,1)S(1)}, u32[]{:S(2)}, u32[]{:S(2)}) collective-permute-start(bf16[64,2176]{1,0:T(8,128)(2,1)} %collective-permute-done.2.refs_3_), channel_id=1, source_target_pairs={{4,0},{5,1},{8,4},{9,5},{12,8},{13,9},{14,12},{15,13},{10,14},{11,... | collective-permute-start | bytes 835592 | tf_op jit(solution)/shard_map/ppermute | solution.py:149
  31.5 11.2 %collective-permute-start.11 = (bf16[64,2176]{1,0:T(8,128)(2,1)S(1)}, bf16[64,2176]{1,0:T(8,128)(2,1)S(1)}, u32[]{:S(2)}, u32[]{:S(2)}) collective-permute-start(bf16[64,2176]{1,0:T(8,128)(2,1)S(1)} %collective-permute-done.4.refs_4_), channel_id=1, source_target_pairs={{4,8},{5,9},{8,12},{9,13},{12,14},{13,15},{14,10},{15,11},{10,6},{... | collective-permute-start | bytes 835592 | tf_op jit(solution)/shard_map/ppermute | solution.py:149
  32.1 11.1 %collective-permute-start.12 = (bf16[64,2176]{1,0:T(8,128)(2,1)S(1)}, bf16[64,2176]{1,0:T(8,128)(2,1)S(1)}, u32[]{:S(2)}, u32[]{:S(2)}) collective-permute-start(bf16[64,2176]{1,0:T(8,128)(2,1)S(1)} %collective-permute-done.5.refs_5_), channel_id=1, source_target_pairs={{4,0},{5,1},{8,4},{9,5},{12,8},{13,9},{14,12},{15,13},{10,14},{11,... | collective-permute-start | bytes 835592 | tf_op jit(solution)/shard_map/ppermute | solution.py:149
  33.6 10.8 %collective-permute-start.9 = (bf16[64,2176]{1,0:T(8,128)(2,1)S(1)}, bf16[64,2176]{1,0:T(8,128)(2,1)S(1)}, u32[]{:S(2)}, u32[]{:S(2)}) collective-permute-start(bf16[64,2176]{1,0:T(8,128)(2,1)S(1)} %collective-permute-done.1.refs_2_), channel_id=1, source_target_pairs={{4,8},{5,9},{8,12},{9,13},{12,14},{13,15},{14,10},{15,11},{10,6},{... | collective-permute-start | bytes 835592 | tf_op jit(solution)/shard_map/ppermute | solution.py:149
  44.3 9.2 %collective-permute-start.13 = (bf16[64,2176]{1,0:T(8,128)(2,1)S(1)}, bf16[64,2176]{1,0:T(8,128)(2,1)S(1)}, u32[]{:S(2)}, u32[]{:S(2)}) collective-permute-start(bf16[64,2176]{1,0:T(8,128)(2,1)S(1)} %collective-permute-done.9.refs_0_), channel_id=1, source_target_pairs={{4,8},{5,9},{8,12},{9,13},{12,14},{13,15},{14,10},{15,11},{10,6},{... | collective-permute-start | bytes 835592 | tf_op jit(solution)/shard_map/ppermute | solution.py:149
  44.9 8.7 %collective-permute-start.14 = (bf16[64,2176]{1,0:T(8,128)(2,1)S(1)}, bf16[64,2176]{1,0:T(8,128)(2,1)S(1)}, u32[]{:S(2)}, u32[]{:S(2)}) collective-permute-start(bf16[64,2176]{1,0:T(8,128)(2,1)S(1)} %collective-permute-done.10.refs_1_), channel_id=1, source_target_pairs={{4,0},{5,1},{8,4},{9,5},{12,8},{13,9},{14,12},{15,13},{10,14},{11,... | collective-permute-start | bytes 835592 | tf_op jit(solution)/shard_map/ppermute | solution.py:149
  46.3 10.6 %collective-permute-start.15 = (bf16[64,2176]{1,0:T(8,128)(2,1)S(1)}, bf16[64,2176]{1,0:T(8,128)(2,1)S(1)}, u32[]{:S(2)}, u32[]{:S(2)}) collective-permute-start(bf16[64,2176]{1,0:T(8,128)(2,1)S(1)} %collective-permute-done.11.refs_2_), channel_id=1, source_target_pairs={{4,8},{5,9},{8,12},{9,13},{12,14},{13,15},{14,10},{15,11},{10,6},{... | collective-permute-start | bytes 835592 | tf_op jit(solution)/shard_map/ppermute | solution.py:149
  46.9 10.0 %collective-permute-start.16 = (bf16[64,2176]{1,0:T(8,128)(2,1)S(1)}, bf16[64,2176]{1,0:T(8,128)(2,1)S(1)}, u32[]{:S(2)}, u32[]{:S(2)}) collective-permute-start(bf16[64,2176]{1,0:T(8,128)(2,1)S(1)} %collective-permute-done.12.refs_3_), channel_id=1, source_target_pairs={{4,0},{5,1},{8,4},{9,5},{12,8},{13,9},{14,12},{15,13},{10,14},{11,... | collective-permute-start | bytes 835592 | tf_op jit(solution)/shard_map/ppermute | solution.py:149
  57.0 7.2 %collective-permute-start.17 = (bf16[64,2176]{1,0:T(8,128)(2,1)S(1)}, bf16[64,2176]{1,0:T(8,128)(2,1)S(1)}, u32[]{:S(2)}, u32[]{:S(2)}) collective-permute-start(bf16[64,2176]{1,0:T(8,128)(2,1)S(1)} %collective-permute-done.13.refs_0_), channel_id=1, source_target_pairs={{4,8},{5,9},{8,12},{9,13},{12,14},{13,15},{14,10},{15,11},{10,6},{... | collective-permute-start | bytes 835592 | tf_op jit(solution)/shard_map/ppermute | solution.py:149
  57.6 6.6 %collective-permute-start.18 = (bf16[64,2176]{1,0:T(8,128)(2,1)S(1)}, bf16[64,2176]{1,0:T(8,128)(2,1)S(1)}, u32[]{:S(2)}, u32[]{:S(2)}) collective-permute-start(bf16[64,2176]{1,0:T(8,128)(2,1)S(1)} %collective-permute-done.16.refs_3_), channel_id=1, source_target_pairs={{4,0},{5,1},{8,4},{9,5},{12,8},{13,9},{14,12},{15,13},{10,14},{11,... | collective-permute-start | bytes 835592 | tf_op jit(solution)/shard_map/ppermute | solution.py:149
  66.9 9.3 %collective-permute-start.19 = (bf16[64,2048]{1,0:T(8,128)(2,1)S(1)}, bf16[64,2048]{1,0:T(8,128)(2,1)S(1)}, u32[]{:S(2)}, u32[]{:S(2)}) collective-permute-start(bf16[64,2048]{1,0:T(8,128)(2,1)S(1)} %get-tuple-element.122), channel_id=1, source_target_pairs={{4,0},{5,1},{8,4},{9,5},{12,8},{13,9},{14,12},{15,13},{10,14},{11,... | collective-permute-start | bytes 786440 | tf_op jit(solution)/shard_map/ppermute | solution.py:149
  68.7 9.4 %collective-permute-start.23 = (bf16[64,2048]{1,0:T(8,128)(2,1)S(1)}, bf16[64,2048]{1,0:T(8,128)(2,1)S(1)}, u32[]{:S(2)}, u32[]{:S(2)}) collective-permute-start(bf16[64,2048]{1,0:T(8,128)(2,1)S(1)} %get-tuple-element.126), channel_id=1, source_target_pairs={{4,8},{5,9},{8,12},{9,13},{12,14},{13,15},{14,10},{15,11},{10,6},{... | collective-permute-start | bytes 786440 | tf_op jit(solution)/shard_map/ppermute | solution.py:149
  69.0 12.8 %collective-permute-start.26 = (bf16[64,2048]{1,0:T(8,128)(2,1)S(1)}, bf16[64,2048]{1,0:T(8,128)(2,1)S(1)}, u32[]{:S(2)}, u32[]{:S(2)}) collective-permute-start(bf16[64,2048]{1,0:T(8,128)(2,1)S(1)} %get-tuple-element.130), channel_id=1, source_target_pairs={{4,0},{5,1},{8,4},{9,5},{12,8},{13,9},{14,12},{15,13},{10,14},{11,... | collective-permute-start | bytes 786440 | tf_op jit(solution)/shard_map/ppermute | solution.py:149
  70.8 12.9 %collective-permute-start.29 = (bf16[64,2048]{1,0:T(8,128)(2,1)S(1)}, bf16[64,2048]{1,0:T(8,128)(2,1)S(1)}, u32[]{:S(2)}, u32[]{:S(2)}) collective-permute-start(bf16[64,2048]{1,0:T(8,128)(2,1)S(1)} %get-tuple-element.133), channel_id=1, source_target_pairs={{4,8},{5,9},{8,12},{9,13},{12,14},{13,15},{14,10},{15,11},{10,6},{... | collective-permute-start | bytes 786440 | tf_op jit(solution)/shard_map/ppermute | solution.py:149
  76.3 11.2 %collective-permute-start.20 = (bf16[64,2048]{1,0:T(8,128)(2,1)S(1)}, bf16[64,2048]{1,0:T(8,128)(2,1)S(1)}, u32[]{:S(2)}, u32[]{:S(2)}) collective-permute-start(bf16[64,2048]{1,0:T(8,128)(2,1)S(1)} %add_convert_fusion.9), channel_id=1, source_target_pairs={{4,0},{5,1},{8,4},{9,5},{12,8},{13,9},{14,12},{15,13},{10,14},{11,... | collective-permute-start | bytes 786440 | tf_op jit(solution)/shard_map/ppermute | solution.py:149
  78.2 11.2 %collective-permute-start.24 = (bf16[64,2048]{1,0:T(8,128)(2,1)S(1)}, bf16[64,2048]{1,0:T(8,128)(2,1)S(1)}, u32[]{:S(2)}, u32[]{:S(2)}) collective-permute-start(bf16[64,2048]{1,0:T(8,128)(2,1)S(1)} %add_convert_fusion.6), channel_id=1, source_target_pairs={{4,8},{5,9},{8,12},{9,13},{12,14},{13,15},{14,10},{15,11},{10,6},{... | collective-permute-start | bytes 786440 | tf_op jit(solution)/shard_map/ppermute | solution.py:149
  81.9 11.2 %collective-permute-start.27 = (bf16[64,2048]{1,0:T(8,128)(2,1)S(1)}, bf16[64,2048]{1,0:T(8,128)(2,1)S(1)}, u32[]{:S(2)}, u32[]{:S(2)}) collective-permute-start(bf16[64,2048]{1,0:T(8,128)(2,1)S(1)} %add_convert_fusion.4), channel_id=1, source_target_pairs={{4,0},{5,1},{8,4},{9,5},{12,8},{13,9},{14,12},{15,13},{10,14},{11,... | collective-permute-start | bytes 786440 | tf_op jit(solution)/shard_map/ppermute | solution.py:149
  83.8 11.2 %collective-permute-start.30 = (bf16[64,2048]{1,0:T(8,128)(2,1)S(1)}, bf16[64,2048]{1,0:T(8,128)(2,1)S(1)}, u32[]{:S(2)}, u32[]{:S(2)}) collective-permute-start(bf16[64,2048]{1,0:T(8,128)(2,1)S(1)} %add_convert_fusion.2), channel_id=1, source_target_pairs={{4,8},{5,9},{8,12},{9,13},{12,14},{13,15},{14,10},{15,11},{10,6},{... | collective-permute-start | bytes 786440 | tf_op jit(solution)/shard_map/ppermute | solution.py:149
  87.5 10.5 %collective-permute-start.21 = (bf16[64,2048]{1,0:T(8,128)(2,1)S(1)}, bf16[64,2048]{1,0:T(8,128)(2,1)S(1)}, u32[]{:S(2)}, u32[]{:S(2)}) collective-permute-start(bf16[64,2048]{1,0:T(8,128)(2,1)S(1)} %add_convert_fusion.8), channel_id=1, source_target_pairs={{4,0},{5,1},{8,4},{9,5},{12,8},{13,9},{14,12},{15,13},{10,14},{11,... | collective-permute-start | bytes 786440 | tf_op jit(solution)/shard_map/ppermute | solution.py:149
  89.4 13.3 %collective-permute-start.25 = (bf16[64,2048]{1,0:T(8,128)(2,1)S(1)}, bf16[64,2048]{1,0:T(8,128)(2,1)S(1)}, u32[]{:S(2)}, u32[]{:S(2)}) collective-permute-start(bf16[64,2048]{1,0:T(8,128)(2,1)S(1)} %add_convert_fusion.5), channel_id=1, source_target_pairs={{4,8},{5,9},{8,12},{9,13},{12,14},{13,15},{14,10},{15,11},{10,6},{... | collective-permute-start | bytes 786440 | tf_op jit(solution)/shard_map/ppermute | solution.py:149
  93.1 11.5 %collective-permute-start.28 = (bf16[64,2048]{1,0:T(8,128)(2,1)S(1)}, bf16[64,2048]{1,0:T(8,128)(2,1)S(1)}, u32[]{:S(2)}, u32[]{:S(2)}) collective-permute-start(bf16[64,2048]{1,0:T(8,128)(2,1)S(1)} %add_convert_fusion.3), channel_id=1, source_target_pairs={{4,0},{5,1},{8,4},{9,5},{12,8},{13,9},{14,12},{15,13},{10,14},{11,... | collective-permute-start | bytes 786440 | tf_op jit(solution)/shard_map/ppermute | solution.py:149
  95.0 6.8 %collective-permute-start.31 = (bf16[64,2048]{1,0:T(8,128)(2,1)S(1)}, bf16[64,2048]{1,0:T(8,128)(2,1)S(1)}, u32[]{:S(2)}, u32[]{:S(2)}) collective-permute-start(bf16[64,2048]{1,0:T(8,128)(2,1)S(1)} %add_convert_fusion.1), channel_id=1, source_target_pairs={{4,8},{5,9},{8,12},{9,13},{12,14},{13,15},{14,10},{15,11},{10,6},{... | collective-permute-start | bytes 786440 | tf_op jit(solution)/shard_map/ppermute | solution.py:149
  98.1 6.4 %collective-permute-start.22 = (bf16[64,2048]{1,0:T(8,128)(2,1)S(1)}, bf16[64,2048]{1,0:T(8,128)(2,1)S(1)}, u32[]{:S(2)}, u32[]{:S(2)}) collective-permute-start(bf16[64,2048]{1,0:T(8,128)(2,1)S(1)} %add_convert_fusion.7), channel_id=1, source_target_pairs={{4,0},{5,1},{8,4},{9,5},{12,8},{13,9},{14,12},{15,13},{10,14},{11,... | collective-permute-start | bytes 786440 | tf_op jit(solution)/shard_map/ppermute | solution.py:149
  (6 other events, 68.0 us)

commit v2 on v1

--- a/solution.py
+++ b/solution.py
@@ -13,6 +13,7 @@
 LANES = 128
 FF_CHUNK = 256
 OUT_CHUNK = 512
+CHUNK_BLOCKS = 4
 VMEM_GRANT = 16 << 20
 
 
@@ -49,7 +50,7 @@
     return next(c for c in range(min(extent, most), 0, -1) if extent % c == 0)
 
 
-def group_kernel(sizes, features, experts, ff, me_ref, *refs):
+def dense_kernel(sizes, features, experts, ff, me_ref, *refs):
     count = len(sizes)
     blocks, weights = refs[:count], refs[count : count + 6]
     outs = refs[count + 6 : 2 * count + 6]
@@ -86,6 +87,80 @@
             start += size
 
 
+def picked_kernel(chunks, size, room, experts, me_ref, *refs):
+    count = sum(chunks)
+    blocks, weights = refs[:count], refs[count : count + 6]
+    outs = refs[count + 6 : 2 * count + 6]
+    picked, hidden, place = refs[2 * count + 6 :]
+    features, ff = weights[0].shape
+    ff_chunk, out_chunk = chunk_of(ff, FF_CHUNK), chunk_of(features, OUT_CHUNK)
+    total = count * room
+    shares = [[] for _ in range(CORES)]
+    first = 0
+    for chunk in chunks:
+        tokens, slots = chunk * size, chunk * room
+        values = jnp.concatenate([block[...] for block in blocks[first : first + chunk]], axis=0)
+        extra = values[:, features:].astype(jnp.float32)
+        lane = lax.broadcasted_iota(jnp.int32, extra.shape, 1)
+        named = jnp.where(extra > 0.0, 1.0, 0.0)
+        row = lax.broadcasted_iota(jnp.int32, (tokens, tokens), 0)
+        column = lax.broadcasted_iota(jnp.int32, (tokens, tokens), 1)
+        earlier = jnp.where((column < row) & (column // size == row // size), 1.0, 0.0)
+        before = jnp.dot(
+            earlier.astype(jnp.bfloat16), named.astype(jnp.bfloat16), preferred_element_type=jnp.float32
+        )
+        slot = lax.broadcasted_iota(jnp.int32, (tokens, slots), 1)
+        start = lax.broadcasted_iota(jnp.int32, (tokens, slots), 0) // size * room
+        for i in range(CORES):
+            expert = me_ref[0] ^ i
+            here = jnp.sum(jnp.where(lane == expert, before, 0.0), axis=1, keepdims=True)
+            takes = jnp.sum(jnp.where(lane == expert, named, 0.0), axis=1, keepdims=True)
+            match = (slot - start).astype(jnp.float32) == jnp.where(takes > 0.0, here, -1.0 * size * count)
+            match = jnp.where(match, 1.0, 0.0).astype(jnp.bfloat16)
+            place[first * size : first * size + tokens, i * slots : (i + 1) * slots] = match
+            found = lax.dot_general(
+                match, values, (((0,), (0,)), ((), ())), preferred_element_type=jnp.float32
+            )
+            at = i * total + first * room
+            picked[at : at + slots, :] = found[:, :features].astype(jnp.bfloat16)
+            both = lax.broadcasted_iota(jnp.int32, (slots, extra.shape[1]), 1)
+            both = (both == expert) | (both == expert + experts)
+            shares[i].append(jnp.sum(jnp.where(both, found[:, features:], 0.0), axis=1, keepdims=True))
+        first += chunk
+    for i in range(CORES):
+        share = jnp.concatenate(shares[i], axis=0)
+        gate_weight, up_weight = weights[3 * i], weights[3 * i + 1]
+        rows = slice(i * total, (i + 1) * total)
+        for c in range(0, ff, ff_chunk):
+            part = slice(c, c + ff_chunk)
+            gate = jnp.dot(picked[rows, :], gate_weight[:, part], preferred_element_type=jnp.float32)
+            up = jnp.dot(picked[rows, :], up_weight[:, part], preferred_element_type=jnp.float32)
+            value = gate / (1.0 + jnp.exp(-gate)) * up * share
+            hidden[rows, part] = value.astype(jnp.bfloat16)
+    for n in range(0, features, out_chunk):
+        part = slice(n, n + out_chunk)
+        made = [
+            jnp.dot(
+                hidden[i * total : (i + 1) * total, :],
+                weights[3 * i + 2][:, part],
+                preferred_element_type=jnp.float32,
+            ).astype(jnp.bfloat16)
+            for i in range(CORES)
+        ]
+        first = 0
+        for chunk in chunks:
+            tokens, slots = chunk * size, chunk * room
+            mixed = jnp.concatenate([m[first * room : first * room + slots] for m in made], axis=0)
+            spread = jnp.dot(
+                place[first * size : first * size + tokens, : CORES * slots],
+                mixed,
+                preferred_element_type=jnp.float32,
+            ).astype(jnp.bfloat16)
+            for j in range(chunk):
+                outs[first + j][:, part] = spread[j * size : (j + 1) * size]
+            first += chunk
+
+
 def load_kernel(*refs):
     count = len(refs) // 2
     sems = refs[2 * count]
@@ -105,31 +180,44 @@
         scratch_shapes=[pltpu.SemaphoreType.DMA((len(values),))],
         compiler_params=pltpu.CompilerParams(vmem_limit_bytes=1 << 20),
         cost_estimate=pl.CostEstimate(
-            flops=0, bytes_accessed=2 * sum(v.size * v.dtype.itemsize for v in values), transcendentals=0
+            flops=0, bytes_accessed=0, transcendentals=0
         ),
     )(*[pltpu.with_memory_space_constraint(value, pltpu.HBM) for value in values])
 
 
-def group_sums(me, blocks, weights, experts):
-    sizes = [block.shape[0] for block in blocks]
-    total = sum(sizes)
+def group_sums(me, blocks, weights, experts, room):
+    count, size = len(blocks), blocks[0].shape[0]
     features, ff = weights[0].shape
+    total = count * size
+    if count >= CHUNK_BLOCKS:
+        rows = count * room
+        chunks = [min(CHUNK_BLOCKS, count - first) for first in range(0, count, CHUNK_BLOCKS)]
+        kernel = functools.partial(picked_kernel, chunks, size, room, experts)
+        scratch_shapes = [
+            pltpu.VMEM((CORES * rows, features), jnp.bfloat16),
+            pltpu.VMEM((CORES * rows, ff), jnp.bfloat16),
+            pltpu.VMEM((total, CORES * CHUNK_BLOCKS * room), jnp.bfloat16),
+        ]
+    else:
+        rows = total
+        kernel = functools.partial(dense_kernel, [size] * count, features, experts, ff)
+        scratch_shapes = [
+            pltpu.VMEM((total, features), jnp.bfloat16),
+            pltpu.VMEM((total, CORES * ff), jnp.bfloat16),
+        ]
     near = pl.BlockSpec(memory_space=pltpu.VMEM)
     operands = [pltpu.with_memory_space_constraint(a, pltpu.VMEM) for a in (*blocks, *weights)]
     return pl.pallas_call(
-        functools.partial(group_kernel, sizes, features, experts, ff),
-        out_shape=[pltpu.VMEM((size, features), jnp.bfloat16) for size in sizes],
+        kernel,
+        out_shape=[pltpu.VMEM((size, features), jnp.bfloat16)] * count,
         in_specs=[pl.BlockSpec(memory_space=pltpu.SMEM)] + [near] * len(operands),
-        out_specs=[near] * len(sizes),
-        scratch_shapes=[
-            pltpu.VMEM((total, features), jnp.bfloat16),
-            pltpu.VMEM((total, CORES * ff), jnp.bfloat16),
-        ],
+        out_specs=[near] * count,
+        scratch_shapes=scratch_shapes,
         compiler_params=pltpu.CompilerParams(vmem_limit_bytes=VMEM_GRANT),
         cost_estimate=pl.CostEstimate(
-            flops=6 * CORES * total * features * ff,
+            flops=6 * CORES * rows * features * ff,
             bytes_accessed=4 * total * features,
-            transcendentals=CORES * total * ff,
+            transcendentals=CORES * rows * ff,
         ),
     )(me, *operands)
 
@@ -158,7 +246,9 @@
         around = [(s, (s + 1) % sections) for s in range(sections)]
         arrived = [lax.ppermute(emitted[0, b], "section", around) for b in range(batches)]
         mine = (w_gate[0, 0], w_up[0, 0], w_down[0, 0])
-        weights = mine + tuple(swap(w) for w in mine)
+        down, arrived[0] = lax.optimization_barrier((mine[2], arrived[0]))
+        weights = mine + (swap(mine[0]), swap(mine[1]), swap(down))
+        room = min(tok_rows, 4 * tok_rows * expert_ids.shape[3] // (3 * experts))
         me = lax.axis_index("expert").astype(jnp.int32).reshape(1)
         mod_weight = w_mod[0]
         lanes = -(-2 * experts // LANES) * LANES
@@ -190,44 +280,53 @@
         top = {
             (b, step): far if not halved or (step == 1) == (b < first_half) else far - 1 for b, step in chains
         }
+        part = tok_rows // 2 if halved else tok_rows
+        kept = {1: slice(0, part), -1: slice(tok_rows - part, tok_rows)}
         own = [payload(b) for b in range(batches)]
         blocks = {(*chain, 0): own[chain[0]] for chain in chains}
         sums = {}
 
         def add_sums(keys):
-            for key, value in zip(keys, group_sums(me, [blocks[key] for key in keys], weights, experts)):
+            for key, value in zip(keys, group_sums(me, [blocks[key] for key in keys], weights, experts, room)):
                 sums[key] = value
 
+        waiting = []
         for k in range(1, far + 1):
-            moving = [chain for chain in chains if top[chain] >= k]
-            sent = [blocks[(*chain, k - 1)] for chain in moving]
-            if k > 1:
-                sent = tied(sent)
-            got = [hop(value, chain[1]) for value, chain in zip(sent, moving)]
-            keys = [(*chain, k - 1) for chain in chains]
+            for b in range(batches):
+                moving = [(b, step) for step in (1, -1) if top[b, step] >= k]
+                sent = [blocks[(*chain, k - 1)] for chain in moving]
+                if waiting and b == batches - 1:
+                    sent, done = tied((sent, [sums[key] for key in waiting]))
+                    sums.update(zip(waiting, done))
+                    waiting = []
+                blocks.update({(*chain, k): hop(value, chain[1]) for value, chain in zip(sent, moving)})
             if k == 1:
-                weights = in_vmem(weights)
-                got, weights = tied((got, weights))
-            elif k == 2:
-                keys = [(b, 1, 0) for b in range(batches)] + [(*chain, 1) for chain in chains]
-                add_sums(keys)
-                got, done = tied((got, [sums[key] for key in keys]))
-                sums.update(zip(keys, done))
+                first = [(*chain, 1) for chain in chains]
+                got, weights = tied(([blocks[key] for key in first], in_vmem(weights)))
+                blocks.update(zip(first, got))
             else:
-                add_sums(keys)
-                got, done = tied((got, [sums[key] for key in keys]))
-                sums.update(zip(keys, done))
-            blocks.update({(*chain, k): value for chain, value in zip(moving, got)})
-
-        last_keys = [(*chain, far) for chain in chains if top[chain] == far]
-        add_sums(last_keys)
+                waiting = [(*c, k - 1) for c in chains if k < far or top[c] == far]
+                waiting += [(b, 1, 0) for b in range(batches)] if k == 2 else []
+                add_sums(waiting)
+
+        add_sums([(*chain, top[chain]) for chain in chains])
         total = {}
         for chain in chains:
-            value = sums[(*chain, top[chain])]
-            for place in range(top[chain] - 1, -1, -1):
-                value = hop(value, -chain[1])
-                if place:
-                    value = added(value, sums[(*chain, place)])
+            step = chain[1]
+            if not halved:
+                value = sums[(*chain, far)]
+            else:
+                value = next(sums[chain[0], way, far] for way in (1, -1) if top[chain[0], way] == far)[kept[step]]
+            for place in range(far - 1, -1, -1):
+                value = hop(value, -step)
+                near = sums[(*chain, place)] if place else None
+                if place and halved and place == far - 1:
+                    fresh = added(value, near[kept[step]])
+                    value = jnp.concatenate(
+                        [fresh, near[part:]] if step == 1 else [near[: tok_rows - part], fresh]
+                    )
+                elif place:
+                    value = added(value, near)
             total[chain] = value
         results = []
         for b in range(batches):

time: 110 us -> 108 us (0.982)
  Pallas kernels: 28.1 us -> 24 us
  waiting for transfers between devices: 37.2 us -> 39.1 us
  starting transfers between devices: 35.3 us -> 36.7 us
    pallas_call x4, Pallas kernels: 21.6 us -> 17.5 us  [group_sums(): pl.pallas_call(kernel, out_shape=[pltpu.VMEM((size, features), jnp.bfloat...]
    ppermute x28 -> x30, starting transfers between devices: 31.7 us -> 33.1 us  [hop(): return lax.ppermute(value, 'expert', pairs)]
    ppermute x28 -> x30, waiting for transfers between devices: 33.2 us -> 34.5 us  [hop(): return lax.ppermute(value, 'expert', pairs)]
  transfers between devices with their start and end apart: 33 -> 35, of which waited for: 14 -> 21; matrix products, arithmetic and copies ran while one was open for 5% -> 5% of each run, Pallas kernels for 23% -> 18%
where the time goes in v2:
time: 108 us
  waiting for transfers between devices  39.1 us (36%)
  starting transfers between devices  36.7 us (34%)
  Pallas kernels  24 us (22%)
  other arithmetic  3.85 us (4%)
  local copies, waits for them, and re-layouts  3.2 us (3%)
    ppermute x30, waiting for transfers between devices, hop(): return lax.ppermute(value, 'expert', pairs)  34.5 us
    ppermute x30, starting transfers between devices, hop(): return lax.ppermute(value, 'expert', pairs)  33.1 us
    pallas_call x4, Pallas kernels, group_sums(): pl.pallas_call(kernel, out_shape=[pltpu.VMEM((size, features), jnp.bfloat...  17.5 us
    pallas_call x1, Pallas kernels, in_vmem(): pl.pallas_call(load_kernel, out_shape=[pltpu.VMEM(value.shape, value.dtyp...  6.49 us
    ppermute x2, waiting for transfers between devices, shards(): lax.ppermute(emitted[0, b], 'section', around)  4.56 us
    ppermute x2, starting transfers between devices, shards(): lax.ppermute(emitted[0, b], 'section', around)  3.08 us
  transfers between devices with their start and end apart: 35, of which 21 were waited for; matrix products, arithmetic and copies ran while one was open for 5% of the time, Pallas kernels for 18%

profile of v2, /device:TPU:0, one launch (start us, length us, event | category | flops | bytes accessed | tf_op | source)
XLA Modules:
  0.0 108.1 jit_solution(14381261966361455193)
XLA Ops:
  1.2 3.0 %collective-permute-start = (bf16[64,2048]{1,0:T(8,128)(2,1)S(1)}, bf16[64,2048]{1,0:T(8,128)(2,1)S(1)}, u32[]{:S(2)}, u32[]{:S(2)}) collective-permute-start(bf16[64,2048]{1,0:T(8,128)(2,1)S(1)} %get-tuple-element.100), channel_id=1, source_target_pairs={{0,16},{16,0},{1,17},{17,1},{2,18},{18,2},{3,19},{19,3},{4,20},{20... | collective-permute-start | bytes 786440 | tf_op jit(solution)/shard_map/ppermute | solution.py:247
  8.1 3.3 %collective-permute-done = bf16[64,2048]{1,0:T(8,128)(2,1)S(1)} collective-permute-done((bf16[64,2048]{1,0:T(8,128)(2,1)S(1)}, bf16[64,2048]{1,0:T(8,128)(2,1)S(1)}, u32[]{:S(2)}, u32[]{:S(2)}) %collective-permute-start) | collective-permute-done | bytes 262176 | tf_op jit(solution)/shard_map/ppermute | solution.py:247
  12.7 2.2 %collective-permute-start.1 = (bf16[64,2176]{1,0:T(8,128)(2,1)S(1)}, bf16[64,2176]{1,0:T(8,128)(2,1)S(1)}, u32[]{:S(2)}, u32[]{:S(2)}) collective-permute-start(bf16[64,2176]{1,0:T(8,128)(2,1)S(1)} %pad_maximum_fusion.refs_4_), channel_id=1, source_target_pairs={{4,8},{5,9},{8,12},{9,13},{12,14},{13,15},{14,10},{15,11},{10,6},{... | collective-permute-start | bytes 835592 | tf_op jit(solution)/shard_map/ppermute | solution.py:237
  16.2 1.8 %collective-permute-start.2 = (bf16[64,2176]{1,0:T(8,128)(2,1)S(1)}, bf16[64,2176]{1,0:T(8,128)(2,1)S(1)}, u32[]{:S(2)}, u32[]{:S(2)}) collective-permute-start(bf16[64,2176]{1,0:T(8,128)(2,1)S(1)} %pad_maximum_fusion.refs_4_), channel_id=1, source_target_pairs={{4,0},{5,1},{8,4},{9,5},{12,8},{13,9},{14,12},{15,13},{10,14},{11,... | collective-permute-start | bytes 835592 | tf_op jit(solution)/shard_map/ppermute | solution.py:237
  20.4 6.5 %shard_map.82 = (bf16[2048,768]{1,0:T(8,128)(2,1)S(1)}, bf16[2048,768]{1,0:T(8,128)(2,1)S(1)}, bf16[768,2048]{1,0:T(8,128)(2,1)S(1)}, bf16[2048,768]{1,0:T(8,128...) custom-call(bf16[2048,768]{1,0:T(8,128)(2,1)} %bitcast.32, bf16[2048,768]{1,0:T(8,128)(2,1)} %bitcast.34, ...), custom_call_target="tpu_custom_call" | custom-call | tf_op jit(solution)/shard_map/pallas_call | solution.py:175
  28.1 1.9 %collective-permute-done.5.refs_3_ = bf16[64,2176]{1,0:T(8,128)(2,1)} collective-permute-done((bf16[64,2176]{1,0:T(8,128)(2,1)S(1)}, bf16[64,2176]{1,0:T(8,128)(2,1)}, u32[]{:S(2)}, u32[]{:S(2)}) %collective-permute-start.5) | collective-permute-done | bytes 278560 | tf_op jit(solution)/shard_map/ppermute | solution.py:237
  30.1 1.5 %collective-permute-start.10 = (bf16[64,2176]{1,0:T(8,128)(2,1)}, bf16[64,2176]{1,0:T(8,128)(2,1)S(1)}, u32[]{:S(2)}, u32[]{:S(2)}) collective-permute-start(bf16[64,2176]{1,0:T(8,128)(2,1)} %collective-permute-done.5.refs_3_), channel_id=1, source_target_pairs={{4,0},{5,1},{8,4},{9,5},{12,8},{13,9},{14,12},{15,13},{10,14},{11,... | collective-permute-start | bytes 835592 | tf_op jit(solution)/shard_map/ppermute | solution.py:237
  32.1 1.5 %collective-permute-start.11 = (bf16[64,2176]{1,0:T(8,128)(2,1)S(1)}, bf16[64,2176]{1,0:T(8,128)(2,1)S(1)}, u32[]{:S(2)}, u32[]{:S(2)}) collective-permute-start(bf16[64,2176]{1,0:T(8,128)(2,1)S(1)} %collective-permute-done.1.refs_0_), channel_id=1, source_target_pairs={{4,8},{5,9},{8,12},{9,13},{12,14},{13,15},{14,10},{15,11},{10,6},{... | collective-permute-start | bytes 835592 | tf_op jit(solution)/shard_map/ppermute | solution.py:237
  34.1 6.7 %shard_map.83 = (bf16[64,2048]{1,0:T(8,128)(2,1)S(1)}, bf16[64,2048]{1,0:T(8,128)(2,1)S(1)}, bf16[64,2048]{1,0:T(8,128)(2,1)S(1)}, bf16[64,2048]{1,0:T(8,128)(2,...) custom-call(s32[1]{0:T(128)} %bitcast.12.me_ref, ...), custom_call_target="tpu_custom_call" | custom-call | flops 3623878656 | bytes 3145728 | tf_op jit(solution)/shard_map/pallas_call | solution.py:210
  41.0 1.6 %collective-permute-start.17 = (bf16[64,2176]{1,0:T(8,128)(2,1)S(1)}, bf16[64,2176]{1,0:T(8,128)(2,1)S(1)}, u32[]{:S(2)}, u32[]{:S(2)}) collective-permute-start(bf16[64,2176]{1,0:T(8,128)(2,1)S(1)} %collective-permute-done.10.refs_3_), channel_id=1, source_target_pairs={{4,0},{5,1},{8,4},{9,5},{12,8},{13,9},{14,12},{15,13},{10,14},{11,... | collective-permute-start | bytes 835592 | tf_op jit(solution)/shard_map/ppermute | solution.py:237
  42.6 1.8 %collective-permute-done.11.refs_0_ = bf16[64,2176]{1,0:T(8,128)(2,1)S(1)} collective-permute-done((bf16[64,2176]{1,0:T(8,128)(2,1)S(1)}, bf16[64,2176]{1,0:T(8,128)(2,1)S(1)}, u32[]{:S(2)}, u32[]{:S(2)}) %collective-permute-start.11) | collective-permute-done | bytes 278560 | tf_op jit(solution)/shard_map/ppermute | solution.py:237
  44.9 1.5 %collective-permute-start.16 = (bf16[64,2176]{1,0:T(8,128)(2,1)S(1)}, bf16[64,2176]{1,0:T(8,128)(2,1)S(1)}, u32[]{:S(2)}, u32[]{:S(2)}) collective-permute-start(bf16[64,2176]{1,0:T(8,128)(2,1)S(1)} %collective-permute-done.9.refs_2_), channel_id=1, source_target_pairs={{4,8},{5,9},{8,12},{9,13},{12,14},{13,15},{14,10},{15,11},{10,6},{... | collective-permute-start | bytes 835592 | tf_op jit(solution)/shard_map/ppermute | solution.py:237
  46.9 4.0 %shard_map.84 = (bf16[64,2048]{1,0:T(8,128)(2,1)S(1)}, bf16[64,2048]{1,0:T(8,128)(2,1)S(1)}, bf16[64,2048]{1,0:T(8,128)(2,1)S(1)}, bf16[64,2048]{1,0:T(8,128)(2,1)S(1)}) custom-call(s32[1]{0:T(128)} %bitcast.12.me_ref, bf16[64,2176]{1,0:T(8,128)(2,1)S(1)} %collective-permute-done.11.refs_0_, bf16[64,2176]{1,0:T(8,128)(2,1)S(1)} %collective-permute-done.14.refs_1_, ...), custom_call_target="tpu_custom_call" | custom-call | flops 2415919104 | bytes 2097152 | tf_op jit(solution)/shard_map/pallas_call | solution.py:210
  54.5 2.7 %shard_map.86 = (bf16[64,2048]{1,0:T(8,128)(2,1)S(1)}, bf16[64,2048]{1,0:T(8,128)(2,1)S(1)}) custom-call(s32[1]{0:T(128)} %bitcast.12.me_ref, bf16[64,2176]{1,0:T(8,128)(2,1)S(1)} %collective-permute-done.12.refs_0_, bf16[64,2176]{1,0:T(8,128)(2,1)S(1)} %collective-permute-done.17.refs_1_, bf16[2048,768]{1,0:T(8,128)(2,1)S(1)} %get-tuple-element.64.refs_6_.refs_4_.refs_2_, ...), custom_call_target="tpu_custom_call" | custom-call | flops 2415919104 | bytes 1048576 | tf_op jit(solution)/shard_map/pallas_call | solution.py:210
  57.3 1.6 %collective-permute-done.16.refs_2_ = bf16[64,2176]{1,0:T(8,128)(2,1)S(1)} collective-permute-done((bf16[64,2176]{1,0:T(8,128)(2,1)S(1)}, bf16[64,2176]{1,0:T(8,128)(2,1)S(1)}, u32[]{:S(2)}, u32[]{:S(2)}) %collective-permute-start.16) | collective-permute-done | bytes 278560 | tf_op jit(solution)/shard_map/ppermute | solution.py:237
  58.9 2.2 %collective-permute-done.18.refs_3_ = bf16[64,2176]{1,0:T(8,128)(2,1)S(1)} collective-permute-done((bf16[64,2176]{1,0:T(8,128)(2,1)S(1)}, bf16[64,2176]{1,0:T(8,128)(2,1)S(1)}, u32[]{:S(2)}, u32[]{:S(2)}) %collective-permute-start.18) | collective-permute-done | bytes 278560 | tf_op jit(solution)/shard_map/ppermute | solution.py:237
  61.9 4.0 %shard_map.85 = (bf16[64,2048]{1,0:T(8,128)(2,1)S(1)}, bf16[64,2048]{1,0:T(8,128)(2,1)S(1)}, bf16[64,2048]{1,0:T(8,128)(2,1)S(1)}, bf16[64,2048]{1,0:T(8,128)(2,1)S(1)}) custom-call(s32[1]{0:T(128)} %bitcast.12.me_ref, bf16[64,2176]{1,0:T(8,128)(2,1)S(1)} %collective-permute-done.13.refs_0_, bf16[64,2176]{1,0:T(8,128)(2,1)S(1)} %collective-permute-done.15.refs_1_, ...), custom_call_target="tpu_custom_call" | custom-call | flops 2415919104 | bytes 2097152 | tf_op jit(solution)/shard_map/pallas_call | solution.py:210
  65.9 1.6 %collective-permute-start.19 = (bf16[32,2048]{1,0:T(8,128)(2,1)S(1)}, bf16[32,2048]{1,0:T(8,128)(2,1)S(1)}, u32[]{:S(2)}, u32[]{:S(2)}) collective-permute-start(bf16[32,2048]{1,0:T(8,128)(2,1)S(1)} %get-tuple-element.101), channel_id=1, source_target_pairs={{4,0},{5,1},{8,4},{9,5},{12,8},{13,9},{14,12},{15,13},{10,14},{11,... | collective-permute-start | bytes 393224 | tf_op jit(solution)/shard_map/ppermute | solution.py:237
  68.0 1.6 %collective-permute-start.27 = (bf16[32,2048]{1,0:T(8,128)(2,1)S(1)}, bf16[32,2048]{1,0:T(8,128)(2,1)S(1)}, u32[]{:S(2)}, u32[]{:S(2)}) collective-permute-start(bf16[32,2048]{1,0:T(8,128)(2,1)S(1)} %get-tuple-element.103), channel_id=1, source_target_pairs={{4,0},{5,1},{8,4},{9,5},{12,8},{13,9},{14,12},{15,13},{10,14},{11,... | collective-permute-start | bytes 393224 | tf_op jit(solution)/shard_map/ppermute | solution.py:237
  70.2 2.2 %collective-permute-done.19 = bf16[32,2048]{1,0:T(8,128)(2,1)S(1)} collective-permute-done((bf16[32,2048]{1,0:T(8,128)(2,1)S(1)}, bf16[32,2048]{1,0:T(8,128)(2,1)S(1)}, u32[]{:S(2)}, u32[]{:S(2)}) %collective-permute-start.19) | collective-permute-done | bytes 131104 | tf_op jit(solution)/shard_map/ppermute | solution.py:237
  72.4 1.6 %collective-permute-start.20 = (bf16[64,2048]{1,0:T(8,128)(2,1)S(1)}, bf16[64,2048]{1,0:T(8,128)(2,1)S(1)}, u32[]{:S(2)}, u32[]{:S(2)}) collective-permute-start(bf16[64,2048]{1,0:T(8,128)(2,1)S(1)} %pad_maximum_fusion.2), channel_id=1, source_target_pairs={{4,0},{5,1},{8,4},{9,5},{12,8},{13,9},{14,12},{15,13},{10,14},{11,... | collective-permute-start | bytes 786440 | tf_op jit(solution)/shard_map/ppermute | solution.py:237
  75.2 1.6 %collective-permute-start.28 = (bf16[64,2048]{1,0:T(8,128)(2,1)S(1)}, bf16[64,2048]{1,0:T(8,128)(2,1)S(1)}, u32[]{:S(2)}, u32[]{:S(2)}) collective-permute-start(bf16[64,2048]{1,0:T(8,128)(2,1)S(1)} %pad_maximum_fusion.4), channel_id=1, source_target_pairs={{4,0},{5,1},{8,4},{9,5},{12,8},{13,9},{14,12},{15,13},{10,14},{11,... | collective-permute-start | bytes 786440 | tf_op jit(solution)/shard_map/ppermute | solution.py:237
  77.4 4.3 %collective-permute-done.20 = bf16[64,2048]{1,0:T(8,128)(2,1)S(1)} collective-permute-done((bf16[64,2048]{1,0:T(8,128)(2,1)S(1)}, bf16[64,2048]{1,0:T(8,128)(2,1)S(1)}, u32[]{:S(2)}, u32[]{:S(2)}) %collective-permute-start.20) | collective-permute-done | bytes 262176 | tf_op jit(solution)/shard_map/ppermute | solution.py:237
  81.8 1.6 %collective-permute-start.21 = (bf16[64,2048]{1,0:T(8,128)(2,1)S(1)}, bf16[64,2048]{1,0:T(8,128)(2,1)S(1)}, u32[]{:S(2)}, u32[]{:S(2)}) collective-permute-start(bf16[64,2048]{1,0:T(8,128)(2,1)S(1)} %add_convert_fusion.7), channel_id=1, source_target_pairs={{4,0},{5,1},{8,4},{9,5},{12,8},{13,9},{14,12},{15,13},{10,14},{11,... | collective-permute-start | bytes 786440 | tf_op jit(solution)/shard_map/ppermute | solution.py:237
  84.0 3.3 %collective-permute-done.28 = bf16[64,2048]{1,0:T(8,128)(2,1)S(1)} collective-permute-done((bf16[64,2048]{1,0:T(8,128)(2,1)S(1)}, bf16[64,2048]{1,0:T(8,128)(2,1)S(1)}, u32[]{:S(2)}, u32[]{:S(2)}) %collective-permute-start.28) | collective-permute-done | bytes 262176 | tf_op jit(solution)/shard_map/ppermute | solution.py:237
  87.4 1.6 %collective-permute-start.29 = (bf16[64,2048]{1,0:T(8,128)(2,1)S(1)}, bf16[64,2048]{1,0:T(8,128)(2,1)S(1)}, u32[]{:S(2)}, u32[]{:S(2)}) collective-permute-start(bf16[64,2048]{1,0:T(8,128)(2,1)S(1)} %add_convert_fusion.3), channel_id=1, source_target_pairs={{4,0},{5,1},{8,4},{9,5},{12,8},{13,9},{14,12},{15,13},{10,14},{11,... | collective-permute-start | bytes 786440 | tf_op jit(solution)/shard_map/ppermute | solution.py:237
  89.6 3.3 %collective-permute-done.21 = bf16[64,2048]{1,0:T(8,128)(2,1)S(1)} collective-permute-done((bf16[64,2048]{1,0:T(8,128)(2,1)S(1)}, bf16[64,2048]{1,0:T(8,128)(2,1)S(1)}, u32[]{:S(2)}, u32[]{:S(2)}) %collective-permute-start.21) | collective-permute-done | bytes 262176 | tf_op jit(solution)/shard_map/ppermute | solution.py:237
  93.0 1.6 %collective-permute-start.22 = (bf16[64,2048]{1,0:T(8,128)(2,1)S(1)}, bf16[64,2048]{1,0:T(8,128)(2,1)S(1)}, u32[]{:S(2)}, u32[]{:S(2)}) collective-permute-start(bf16[64,2048]{1,0:T(8,128)(2,1)S(1)} %add_convert_fusion.6), channel_id=1, source_target_pairs={{4,0},{5,1},{8,4},{9,5},{12,8},{13,9},{14,12},{15,13},{10,14},{11,... | collective-permute-start | bytes 786440 | tf_op jit(solution)/shard_map/ppermute | solution.py:237
  95.2 3.3 %collective-permute-done.29 = bf16[64,2048]{1,0:T(8,128)(2,1)S(1)} collective-permute-done((bf16[64,2048]{1,0:T(8,128)(2,1)S(1)}, bf16[64,2048]{1,0:T(8,128)(2,1)S(1)}, u32[]{:S(2)}, u32[]{:S(2)}) %collective-permute-start.29) | collective-permute-done | bytes 262176 | tf_op jit(solution)/shard_map/ppermute | solution.py:237
  98.6 1.6 %collective-permute-start.30 = (bf16[64,2048]{1,0:T(8,128)(2,1)S(1)}, bf16[64,2048]{1,0:T(8,128)(2,1)S(1)}, u32[]{:S(2)}, u32[]{:S(2)}) collective-permute-start(bf16[64,2048]{1,0:T(8,128)(2,1)S(1)} %add_convert_fusion.2), channel_id=1, source_target_pairs={{4,0},{5,1},{8,4},{9,5},{12,8},{13,9},{14,12},{15,13},{10,14},{11,... | collective-permute-start | bytes 786440 | tf_op jit(solution)/shard_map/ppermute | solution.py:237
  100.8 2.4 %collective-permute-done.22 = bf16[64,2048]{1,0:T(8,128)(2,1)S(1)} collective-permute-done((bf16[64,2048]{1,0:T(8,128)(2,1)S(1)}, bf16[64,2048]{1,0:T(8,128)(2,1)S(1)}, u32[]{:S(2)}, u32[]{:S(2)}) %collective-permute-start.22) | collective-permute-done | bytes 262176 | tf_op jit(solution)/shard_map/ppermute | solution.py:237
  104.5 1.5 %collective-permute-done.30 = bf16[64,2048]{1,0:T(8,128)(2,1)S(1)} collective-permute-done((bf16[64,2048]{1,0:T(8,128)(2,1)S(1)}, bf16[64,2048]{1,0:T(8,128)(2,1)S(1)}, u32[]{:S(2)}, u32[]{:S(2)}) %collective-permute-start.30) | collective-permute-done | bytes 262176 | tf_op jit(solution)/shard_map/ppermute | solution.py:237
  (108 shorter events, 26.6 us)
Async XLA Ops:
  1.2 10.1 %collective-permute-start = (bf16[64,2048]{1,0:T(8,128)(2,1)S(1)}, bf16[64,2048]{1,0:T(8,128)(2,1)S(1)}, u32[]{:S(2)}, u32[]{:S(2)}) collective-permute-start(bf16[64,2048]{1,0:T(8,128)(2,1)S(1)} %get-tuple-element.100), channel_id=1, source_target_pairs={{0,16},{16,0},{1,17},{17,1},{2,18},{18,2},{3,19},{19,3},{4,20},{20... | collective-permute-start | bytes 786440 | tf_op jit(solution)/shard_map/ppermute | solution.py:247
  4.2 11.9 %collective-permute-start.3 = (bf16[64,2048]{1,0:T(8,128)(2,1)S(1)}, bf16[64,2048]{1,0:T(8,128)(2,1)S(1)}, u32[]{:S(2)}, u32[]{:S(2)}) collective-permute-start(bf16[64,2048]{1,0:T(8,128)(2,1)S(1)} %get-tuple-element.99), channel_id=1, source_target_pairs={{0,16},{16,0},{1,17},{17,1},{2,18},{18,2},{3,19},{19,3},{4,20},{20... | collective-permute-start | bytes 786440 | tf_op jit(solution)/shard_map/ppermute | solution.py:247
  4.3 14.0 %collective-permute-start.6 = (bf16[2048,768]{1,0:T(8,128)(2,1)}, bf16[2048,768]{1,0:T(8,128)(2,1)}, u32[]{:S(2)}, u32[]{:S(2)}) collective-permute-start(bf16[2048,768]{1,0:T(8,128)(2,1)} %bitcast.31), channel_id=1, source_target_pairs={{0,1},{1,0},{2,3},{3,2},{4,5},{5,4},{6,7},{7,6},{8,9},{9,8},{10,11... | collective-permute-start | bytes 9437192 | tf_op jit(solution)/shard_map/ppermute | solution.py:240
  4.3 14.6 %collective-permute-start.7 = (bf16[2048,768]{1,0:T(8,128)(2,1)}, bf16[2048,768]{1,0:T(8,128)(2,1)}, u32[]{:S(2)}, u32[]{:S(2)}) collective-permute-start(bf16[2048,768]{1,0:T(8,128)(2,1)} %bitcast.33), channel_id=1, source_target_pairs={{0,1},{1,0},{2,3},{3,2},{4,5},{5,4},{6,7},{7,6},{8,9},{9,8},{10,11... | collective-permute-start | bytes 9437192 | tf_op jit(solution)/shard_map/ppermute | solution.py:240
  11.4 9.0 %collective-permute-start.8 = (bf16[768,2048]{1,0:T(8,128)(2,1)}, bf16[768,2048]{1,0:T(8,128)(2,1)}, u32[]{:S(2)}, u32[]{:S(2)}) collective-permute-start(bf16[768,2048]{1,0:T(8,128)(2,1)} %bitcast.35), channel_id=1, source_target_pairs={{0,1},{1,0},{2,3},{3,2},{4,5},{5,4},{6,7},{7,6},{8,9},{9,8},{10,11... | collective-permute-start | bytes 9437192 | tf_op jit(solution)/shard_map/ppermute | solution.py:240
  12.7 14.2 %collective-permute-start.1 = (bf16[64,2176]{1,0:T(8,128)(2,1)S(1)}, bf16[64,2176]{1,0:T(8,128)(2,1)S(1)}, u32[]{:S(2)}, u32[]{:S(2)}) collective-permute-start(bf16[64,2176]{1,0:T(8,128)(2,1)S(1)} %pad_maximum_fusion.refs_4_), channel_id=1, source_target_pairs={{4,8},{5,9},{8,12},{9,13},{12,14},{13,15},{14,10},{15,11},{10,6},{... | collective-permute-start | bytes 835592 | tf_op jit(solution)/shard_map/ppermute | solution.py:237
  16.2 10.7 %collective-permute-start.2 = (bf16[64,2176]{1,0:T(8,128)(2,1)S(1)}, bf16[64,2176]{1,0:T(8,128)(2,1)S(1)}, u32[]{:S(2)}, u32[]{:S(2)}) collective-permute-start(bf16[64,2176]{1,0:T(8,128)(2,1)S(1)} %pad_maximum_fusion.refs_4_), channel_id=1, source_target_pairs={{4,0},{5,1},{8,4},{9,5},{12,8},{13,9},{14,12},{15,13},{10,14},{11,... | collective-permute-start | bytes 835592 | tf_op jit(solution)/shard_map/ppermute | solution.py:237
  18.3 9.8 %collective-permute-start.4 = (bf16[64,2176]{1,0:T(8,128)(2,1)S(1)}, bf16[64,2176]{1,0:T(8,128)(2,1)S(1)}, u32[]{:S(2)}, u32[]{:S(2)}) collective-permute-start(bf16[64,2176]{1,0:T(8,128)(2,1)S(1)} %pad_maximum_fusion.1.refs_5_), channel_id=1, source_target_pairs={{4,8},{5,9},{8,12},{9,13},{12,14},{13,15},{14,10},{15,11},{10,6},{... | collective-permute-start | bytes 835592 | tf_op jit(solution)/shard_map/ppermute | solution.py:237
  18.9 11.1 %collective-permute-start.5 = (bf16[64,2176]{1,0:T(8,128)(2,1)S(1)}, bf16[64,2176]{1,0:T(8,128)(2,1)}, u32[]{:S(2)}, u32[]{:S(2)}) collective-permute-start(bf16[64,2176]{1,0:T(8,128)(2,1)S(1)} %pad_maximum_fusion.1.refs_5_), channel_id=1, source_target_pairs={{4,0},{5,1},{8,4},{9,5},{12,8},{13,9},{14,12},{15,13},{10,14},{11,... | collective-permute-start | bytes 835592 | tf_op jit(solution)/shard_map/ppermute | solution.py:237
  30.1 10.8 %collective-permute-start.10 = (bf16[64,2176]{1,0:T(8,128)(2,1)}, bf16[64,2176]{1,0:T(8,128)(2,1)S(1)}, u32[]{:S(2)}, u32[]{:S(2)}) collective-permute-start(bf16[64,2176]{1,0:T(8,128)(2,1)} %collective-permute-done.5.refs_3_), channel_id=1, source_target_pairs={{4,0},{5,1},{8,4},{9,5},{12,8},{13,9},{14,12},{15,13},{10,14},{11,... | collective-permute-start | bytes 835592 | tf_op jit(solution)/shard_map/ppermute | solution.py:237
  31.5 9.5 %collective-permute-start.9 = (bf16[64,2176]{1,0:T(8,128)(2,1)S(1)}, bf16[64,2176]{1,0:T(8,128)(2,1)S(1)}, u32[]{:S(2)}, u32[]{:S(2)}) collective-permute-start(bf16[64,2176]{1,0:T(8,128)(2,1)S(1)} %collective-permute-done.4.refs_2_), channel_id=1, source_target_pairs={{4,8},{5,9},{8,12},{9,13},{12,14},{13,15},{14,10},{15,11},{10,6},{... | collective-permute-start | bytes 835592 | tf_op jit(solution)/shard_map/ppermute | solution.py:237
  32.1 12.2 %collective-permute-start.11 = (bf16[64,2176]{1,0:T(8,128)(2,1)S(1)}, bf16[64,2176]{1,0:T(8,128)(2,1)S(1)}, u32[]{:S(2)}, u32[]{:S(2)}) collective-permute-start(bf16[64,2176]{1,0:T(8,128)(2,1)S(1)} %collective-permute-done.1.refs_0_), channel_id=1, source_target_pairs={{4,8},{5,9},{8,12},{9,13},{12,14},{13,15},{14,10},{15,11},{10,6},{... | collective-permute-start | bytes 835592 | tf_op jit(solution)/shard_map/ppermute | solution.py:237
  33.6 12.8 %collective-permute-start.14 = (bf16[64,2176]{1,0:T(8,128)(2,1)S(1)}, bf16[64,2176]{1,0:T(8,128)(2,1)S(1)}, u32[]{:S(2)}, u32[]{:S(2)}) collective-permute-start(bf16[64,2176]{1,0:T(8,128)(2,1)S(1)} %collective-permute-done.2.refs_1_), channel_id=1, source_target_pairs={{4,0},{5,1},{8,4},{9,5},{12,8},{13,9},{14,12},{15,13},{10,14},{11,... | collective-permute-start | bytes 835592 | tf_op jit(solution)/shard_map/ppermute | solution.py:237
  41.0 10.5 %collective-permute-start.17 = (bf16[64,2176]{1,0:T(8,128)(2,1)S(1)}, bf16[64,2176]{1,0:T(8,128)(2,1)S(1)}, u32[]{:S(2)}, u32[]{:S(2)}) collective-permute-start(bf16[64,2176]{1,0:T(8,128)(2,1)S(1)} %collective-permute-done.10.refs_3_), channel_id=1, source_target_pairs={{4,0},{5,1},{8,4},{9,5},{12,8},{13,9},{14,12},{15,13},{10,14},{11,... | collective-permute-start | bytes 835592 | tf_op jit(solution)/shard_map/ppermute | solution.py:237
  44.3 9.6 %collective-permute-start.12 = (bf16[64,2176]{1,0:T(8,128)(2,1)S(1)}, bf16[64,2176]{1,0:T(8,128)(2,1)S(1)}, u32[]{:S(2)}, u32[]{:S(2)}) collective-permute-start(bf16[64,2176]{1,0:T(8,128)(2,1)S(1)} %collective-permute-done.11.refs_0_), channel_id=1, source_target_pairs={{4,8},{5,9},{8,12},{9,13},{12,14},{13,15},{14,10},{15,11},{10,6},{... | collective-permute-start | bytes 835592 | tf_op jit(solution)/shard_map/ppermute | solution.py:237
  44.9 14.0 %collective-permute-start.16 = (bf16[64,2176]{1,0:T(8,128)(2,1)S(1)}, bf16[64,2176]{1,0:T(8,128)(2,1)S(1)}, u32[]{:S(2)}, u32[]{:S(2)}) collective-permute-start(bf16[64,2176]{1,0:T(8,128)(2,1)S(1)} %collective-permute-done.9.refs_2_), channel_id=1, source_target_pairs={{4,8},{5,9},{8,12},{9,13},{12,14},{13,15},{14,10},{15,11},{10,6},{... | collective-permute-start | bytes 835592 | tf_op jit(solution)/shard_map/ppermute | solution.py:237
  46.4 12.5 %collective-permute-start.15 = (bf16[64,2176]{1,0:T(8,128)(2,1)S(1)}, bf16[64,2176]{1,0:T(8,128)(2,1)S(1)}, u32[]{:S(2)}, u32[]{:S(2)}) collective-permute-start(bf16[64,2176]{1,0:T(8,128)(2,1)S(1)} %collective-permute-done.14.refs_1_), channel_id=1, source_target_pairs={{4,0},{5,1},{8,4},{9,5},{12,8},{13,9},{14,12},{15,13},{10,14},{11,... | collective-permute-start | bytes 835592 | tf_op jit(solution)/shard_map/ppermute | solution.py:237
  51.5 9.6 %collective-permute-start.18 = (bf16[64,2176]{1,0:T(8,128)(2,1)S(1)}, bf16[64,2176]{1,0:T(8,128)(2,1)S(1)}, u32[]{:S(2)}, u32[]{:S(2)}) collective-permute-start(bf16[64,2176]{1,0:T(8,128)(2,1)S(1)} %collective-permute-done.17.refs_1_), channel_id=1, source_target_pairs={{4,0},{5,1},{8,4},{9,5},{12,8},{13,9},{14,12},{15,13},{10,14},{11,... | collective-permute-start | bytes 835592 | tf_op jit(solution)/shard_map/ppermute | solution.py:237
  53.9 8.0 %collective-permute-start.13 = (bf16[64,2176]{1,0:T(8,128)(2,1)S(1)}, bf16[64,2176]{1,0:T(8,128)(2,1)S(1)}, u32[]{:S(2)}, u32[]{:S(2)}) collective-permute-start(bf16[64,2176]{1,0:T(8,128)(2,1)S(1)} %collective-permute-done.12.refs_0_), channel_id=1, source_target_pairs={{4,8},{5,9},{8,12},{9,13},{12,14},{13,15},{14,10},{15,11},{10,6},{... | collective-permute-start | bytes 835592 | tf_op jit(solution)/shard_map/ppermute | solution.py:237
  68.0 7.1 %collective-permute-start.27 = (bf16[32,2048]{1,0:T(8,128)(2,1)S(1)}, bf16[32,2048]{1,0:T(8,128)(2,1)S(1)}, u32[]{:S(2)}, u32[]{:S(2)}) collective-permute-start(bf16[32,2048]{1,0:T(8,128)(2,1)S(1)} %get-tuple-element.103), channel_id=1, source_target_pairs={{4,0},{5,1},{8,4},{9,5},{12,8},{13,9},{14,12},{15,13},{10,14},{11,... | collective-permute-start | bytes 393224 | tf_op jit(solution)/shard_map/ppermute | solution.py:237
  69.7 7.2 %collective-permute-start.31 = (bf16[32,2048]{1,0:T(8,128)(2,1)S(1)}, bf16[32,2048]{1,0:T(8,128)(2,1)S(1)}, u32[]{:S(2)}, u32[]{:S(2)}) collective-permute-start(bf16[32,2048]{1,0:T(8,128)(2,1)S(1)} %get-tuple-element.104), channel_id=1, source_target_pairs={{4,8},{5,9},{8,12},{9,13},{12,14},{13,15},{14,10},{15,11},{10,6},{... | collective-permute-start | bytes 393224 | tf_op jit(solution)/shard_map/ppermute | solution.py:237
  72.4 9.3 %collective-permute-start.20 = (bf16[64,2048]{1,0:T(8,128)(2,1)S(1)}, bf16[64,2048]{1,0:T(8,128)(2,1)S(1)}, u32[]{:S(2)}, u32[]{:S(2)}) collective-permute-start(bf16[64,2048]{1,0:T(8,128)(2,1)S(1)} %pad_maximum_fusion.2), channel_id=1, source_target_pairs={{4,0},{5,1},{8,4},{9,5},{12,8},{13,9},{14,12},{15,13},{10,14},{11,... | collective-permute-start | bytes 786440 | tf_op jit(solution)/shard_map/ppermute | solution.py:237
  74.1 9.3 %collective-permute-start.24 = (bf16[64,2048]{1,0:T(8,128)(2,1)S(1)}, bf16[64,2048]{1,0:T(8,128)(2,1)S(1)}, u32[]{:S(2)}, u32[]{:S(2)}) collective-permute-start(bf16[64,2048]{1,0:T(8,128)(2,1)S(1)} %pad_maximum_fusion.3), channel_id=1, source_target_pairs={{4,8},{5,9},{8,12},{9,13},{12,14},{13,15},{14,10},{15,11},{10,6},{... | collective-permute-start | bytes 786440 | tf_op jit(solution)/shard_map/ppermute | solution.py:237
  75.2 12.1 %collective-permute-start.28 = (bf16[64,2048]{1,0:T(8,128)(2,1)S(1)}, bf16[64,2048]{1,0:T(8,128)(2,1)S(1)}, u32[]{:S(2)}, u32[]{:S(2)}) collective-permute-start(bf16[64,2048]{1,0:T(8,128)(2,1)S(1)} %pad_maximum_fusion.4), channel_id=1, source_target_pairs={{4,0},{5,1},{8,4},{9,5},{12,8},{13,9},{14,12},{15,13},{10,14},{11,... | collective-permute-start | bytes 786440 | tf_op jit(solution)/shard_map/ppermute | solution.py:237
  76.9 12.1 %collective-permute-start.32 = (bf16[64,2048]{1,0:T(8,128)(2,1)S(1)}, bf16[64,2048]{1,0:T(8,128)(2,1)S(1)}, u32[]{:S(2)}, u32[]{:S(2)}) collective-permute-start(bf16[64,2048]{1,0:T(8,128)(2,1)S(1)} %pad_maximum_fusion.5), channel_id=1, source_target_pairs={{4,8},{5,9},{8,12},{9,13},{12,14},{13,15},{14,10},{15,11},{10,6},{... | collective-permute-start | bytes 786440 | tf_op jit(solution)/shard_map/ppermute | solution.py:237
  81.8 11.2 %collective-permute-start.21 = (bf16[64,2048]{1,0:T(8,128)(2,1)S(1)}, bf16[64,2048]{1,0:T(8,128)(2,1)S(1)}, u32[]{:S(2)}, u32[]{:S(2)}) collective-permute-start(bf16[64,2048]{1,0:T(8,128)(2,1)S(1)} %add_convert_fusion.7), channel_id=1, source_target_pairs={{4,0},{5,1},{8,4},{9,5},{12,8},{13,9},{14,12},{15,13},{10,14},{11,... | collective-permute-start | bytes 786440 | tf_op jit(solution)/shard_map/ppermute | solution.py:237
  83.5 11.2 %collective-permute-start.25 = (bf16[64,2048]{1,0:T(8,128)(2,1)S(1)}, bf16[64,2048]{1,0:T(8,128)(2,1)S(1)}, u32[]{:S(2)}, u32[]{:S(2)}) collective-permute-start(bf16[64,2048]{1,0:T(8,128)(2,1)S(1)} %add_convert_fusion.5), channel_id=1, source_target_pairs={{4,8},{5,9},{8,12},{9,13},{12,14},{13,15},{14,10},{15,11},{10,6},{... | collective-permute-start | bytes 786440 | tf_op jit(solution)/shard_map/ppermute | solution.py:237
  87.4 11.2 %collective-permute-start.29 = (bf16[64,2048]{1,0:T(8,128)(2,1)S(1)}, bf16[64,2048]{1,0:T(8,128)(2,1)S(1)}, u32[]{:S(2)}, u32[]{:S(2)}) collective-permute-start(bf16[64,2048]{1,0:T(8,128)(2,1)S(1)} %add_convert_fusion.3), channel_id=1, source_target_pairs={{4,0},{5,1},{8,4},{9,5},{12,8},{13,9},{14,12},{15,13},{10,14},{11,... | collective-permute-start | bytes 786440 | tf_op jit(solution)/shard_map/ppermute | solution.py:237
  89.1 11.2 %collective-permute-start.33 = (bf16[64,2048]{1,0:T(8,128)(2,1)S(1)}, bf16[64,2048]{1,0:T(8,128)(2,1)S(1)}, u32[]{:S(2)}, u32[]{:S(2)}) collective-permute-start(bf16[64,2048]{1,0:T(8,128)(2,1)S(1)} %add_convert_fusion.1), channel_id=1, source_target_pairs={{4,8},{5,9},{8,12},{9,13},{12,14},{13,15},{14,10},{15,11},{10,6},{... | collective-permute-start | bytes 786440 | tf_op jit(solution)/shard_map/ppermute | solution.py:237
  93.0 10.2 %collective-permute-start.22 = (bf16[64,2048]{1,0:T(8,128)(2,1)S(1)}, bf16[64,2048]{1,0:T(8,128)(2,1)S(1)}, u32[]{:S(2)}, u32[]{:S(2)}) collective-permute-start(bf16[64,2048]{1,0:T(8,128)(2,1)S(1)} %add_convert_fusion.6), channel_id=1, source_target_pairs={{4,0},{5,1},{8,4},{9,5},{12,8},{13,9},{14,12},{15,13},{10,14},{11,... | collective-permute-start | bytes 786440 | tf_op jit(solution)/shard_map/ppermute | solution.py:237
  94.7 9.6 %collective-permute-start.26 = (bf16[64,2048]{1,0:T(8,128)(2,1)S(1)}, bf16[64,2048]{1,0:T(8,128)(2,1)S(1)}, u32[]{:S(2)}, u32[]{:S(2)}) collective-permute-start(bf16[64,2048]{1,0:T(8,128)(2,1)S(1)} %add_convert_fusion.4), channel_id=1, source_target_pairs={{4,8},{5,9},{8,12},{9,13},{12,14},{13,15},{14,10},{15,11},{10,6},{... | collective-permute-start | bytes 786440 | tf_op jit(solution)/shard_map/ppermute | solution.py:237
  98.6 7.4 %collective-permute-start.30 = (bf16[64,2048]{1,0:T(8,128)(2,1)S(1)}, bf16[64,2048]{1,0:T(8,128)(2,1)S(1)}, u32[]{:S(2)}, u32[]{:S(2)}) collective-permute-start(bf16[64,2048]{1,0:T(8,128)(2,1)S(1)} %add_convert_fusion.2), channel_id=1, source_target_pairs={{4,0},{5,1},{8,4},{9,5},{12,8},{13,9},{14,12},{15,13},{10,14},{11,... | collective-permute-start | bytes 786440 | tf_op jit(solution)/shard_map/ppermute | solution.py:237
  (8 other events, 85.3 us)

commit v3 on v2

--- a/solution.py
+++ b/solution.py
@@ -246,8 +246,9 @@
         around = [(s, (s + 1) % sections) for s in range(sections)]
         arrived = [lax.ppermute(emitted[0, b], "section", around) for b in range(batches)]
         mine = (w_gate[0, 0], w_up[0, 0], w_down[0, 0])
-        down, arrived[0] = lax.optimization_barrier((mine[2], arrived[0]))
-        weights = mine + (swap(mine[0]), swap(mine[1]), swap(down))
+        gate_other, down_other = swap(mine[0]), swap(mine[2])
+        up_mine, gate_other = lax.optimization_barrier((mine[1], gate_other))
+        weights = (*mine, gate_other, swap(up_mine), down_other)
         room = min(tok_rows, 4 * tok_rows * expert_ids.shape[3] // (3 * experts))
         me = lax.axis_index("expert").astype(jnp.int32).reshape(1)
         mod_weight = w_mod[0]

time: 108 us -> 107 us (level)
  starting transfers between devices: 36.7 us -> 34.7 us
  local copies, waits for them, and re-layouts: 3.2 us -> 4.46 us
    ppermute x30, starting transfers between devices: 33.1 us -> 31.1 us  [hop(): return lax.ppermute(value, 'expert', pairs)]
    ppermute x30, waiting for transfers between devices: 34.5 us -> 33.2 us  [hop(): return lax.ppermute(value, 'expert', pairs)]
  transfers between devices with their start and end apart: 35 -> 35, of which waited for: 21 -> 19; matrix products, arithmetic and copies ran while one was open for 5% -> 7% of each run, Pallas kernels for 18% -> 19%
where the time goes in v3:
time: 107 us
  waiting for transfers between devices  38.4 us (36%)
  starting transfers between devices  34.7 us (32%)
  Pallas kernels  23.9 us (22%)
  local copies, waits for them, and re-layouts  4.46 us (4%)
  other arithmetic  3.84 us (4%)
    ppermute x30, waiting for transfers between devices, hop(): return lax.ppermute(value, 'expert', pairs)  33.2 us
    ppermute x30, starting transfers between devices, hop(): return lax.ppermute(value, 'expert', pairs)  31.1 us
    pallas_call x4, Pallas kernels, group_sums(): pl.pallas_call(kernel, out_shape=[pltpu.VMEM((size, features), jnp.bfloat...  17.4 us
    pallas_call x1, Pallas kernels, in_vmem(): pl.pallas_call(load_kernel, out_shape=[pltpu.VMEM(value.shape, value.dtyp...  6.49 us
    ppermute x2, waiting for transfers between devices, shards(): lax.ppermute(emitted[0, b], 'section', around)  5.13 us
    ppermute x2, starting transfers between devices, shards(): lax.ppermute(emitted[0, b], 'section', around)  2.5 us
  transfers between devices with their start and end apart: 35, of which 19 were waited for; matrix products, arithmetic and copies ran while one was open for 7% of the time, Pallas kernels for 19%

profile of v3, /device:TPU:0, one launch (start us, length us, event | category | flops | bytes accessed | tf_op | source)
XLA Modules:
  0.0 106.6 jit_solution(11064558612773379904)
XLA Ops:
  0.5 1.9 %slice_bitcast_fusion = (bf16[64,2048]{1,0:T(8,128)(2,1)S(1)}, bf16[64,2048]{1,0:T(8,128)(2,1)}) fusion(bf16[1,2,64,2048]{3,2,1,0:T(8,128)(2,1)} %param.8), kind=kLoop, calls=%fused_computation.47 | loop fusion | bytes 1048576 | tf_op jit(solution)/shard_map/squeeze | solution.py:247
  2.4 2.5 %collective-permute-start.3 = (bf16[64,2048]{1,0:T(8,128)(2,1)S(1)}, bf16[64,2048]{1,0:T(8,128)(2,1)S(1)}, u32[]{:S(2)}, u32[]{:S(2)}) collective-permute-start(bf16[64,2048]{1,0:T(8,128)(2,1)S(1)} %get-tuple-element.99), channel_id=1, source_target_pairs={{0,16},{16,0},{1,17},{17,1},{2,18},{18,2},{3,19},{19,3},{4,20},{20... | collective-permute-start | bytes 786440 | tf_op jit(solution)/shard_map/ppermute | solution.py:247
  9.7 2.3 %collective-permute-done.3 = bf16[64,2048]{1,0:T(8,128)(2,1)S(1)} collective-permute-done((bf16[64,2048]{1,0:T(8,128)(2,1)S(1)}, bf16[64,2048]{1,0:T(8,128)(2,1)S(1)}, u32[]{:S(2)}, u32[]{:S(2)}) %collective-permute-start.3) | collective-permute-done | bytes 262176 | tf_op jit(solution)/shard_map/ppermute | solution.py:247
  12.4 2.1 %collective-permute-start.4 = (bf16[64,2176]{1,0:T(8,128)(2,1)S(1)}, bf16[64,2176]{1,0:T(8,128)(2,1)S(1)}, u32[]{:S(2)}, u32[]{:S(2)}) collective-permute-start(bf16[64,2176]{1,0:T(8,128)(2,1)S(1)} %pad_maximum_fusion.1.refs_5_), channel_id=1, source_target_pairs={{4,8},{5,9},{8,12},{9,13},{12,14},{13,15},{14,10},{15,11},{10,6},{... | collective-permute-start | bytes 835592 | tf_op jit(solution)/shard_map/ppermute | solution.py:237
  14.5 2.8 %collective-permute-done = bf16[64,2048]{1,0:T(8,128)(2,1)S(1)} collective-permute-done((bf16[64,2048]{1,0:T(8,128)(2,1)}, bf16[64,2048]{1,0:T(8,128)(2,1)S(1)}, u32[]{:S(2)}, u32[]{:S(2)}) %collective-permute-start) | collective-permute-done | bytes 262176 | tf_op jit(solution)/shard_map/ppermute | solution.py:247
  18.2 1.9 %collective-permute-start.1 = (bf16[64,2176]{1,0:T(8,128)(2,1)S(1)}, bf16[64,2176]{1,0:T(8,128)(2,1)}, u32[]{:S(2)}, u32[]{:S(2)}) collective-permute-start(bf16[64,2176]{1,0:T(8,128)(2,1)S(1)} %pad_maximum_fusion.refs_4_), channel_id=1, source_target_pairs={{4,8},{5,9},{8,12},{9,13},{12,14},{13,15},{14,10},{15,11},{10,6},{... | collective-permute-start | bytes 835592 | tf_op jit(solution)/shard_map/ppermute | solution.py:237
  20.3 6.5 %shard_map.82 = (bf16[2048,768]{1,0:T(8,128)(2,1)S(1)}, bf16[2048,768]{1,0:T(8,128)(2,1)S(1)}, bf16[768,2048]{1,0:T(8,128)(2,1)S(1)}, bf16[2048,768]{1,0:T(8,128...) custom-call(bf16[2048,768]{1,0:T(8,128)(2,1)} %bitcast.32, bf16[2048,768]{1,0:T(8,128)(2,1)} %bitcast.34, ...), custom_call_target="tpu_custom_call" | custom-call | tf_op jit(solution)/shard_map/pallas_call | solution.py:175
  30.0 1.6 %collective-permute-start.11 = (bf16[64,2176]{1,0:T(8,128)(2,1)}, bf16[64,2176]{1,0:T(8,128)(2,1)S(1)}, u32[]{:S(2)}, u32[]{:S(2)}) collective-permute-start(bf16[64,2176]{1,0:T(8,128)(2,1)} %collective-permute-done.1.refs_0_), channel_id=1, source_target_pairs={{4,8},{5,9},{8,12},{9,13},{12,14},{13,15},{14,10},{15,11},{10,6},{... | collective-permute-start | bytes 835592 | tf_op jit(solution)/shard_map/ppermute | solution.py:237
  32.0 6.7 %shard_map.83 = (bf16[64,2048]{1,0:T(8,128)(2,1)S(1)}, bf16[64,2048]{1,0:T(8,128)(2,1)S(1)}, bf16[64,2048]{1,0:T(8,128)(2,1)S(1)}, bf16[64,2048]{1,0:T(8,128)(2,...) custom-call(s32[1]{0:T(128)} %bitcast.12.me_ref, bf16[64,2176]{1,0:T(8,128)(2,1)} %collective-permute-done.1.refs_0_, ...), custom_call_target="tpu_custom_call" | custom-call | flops 3623878656 | bytes 3145728 | tf_op jit(solution)/shard_map/pallas_call | solution.py:210
  39.8 2.1 %collective-permute-done.11.refs_0_ = bf16[64,2176]{1,0:T(8,128)(2,1)S(1)} collective-permute-done((bf16[64,2176]{1,0:T(8,128)(2,1)}, bf16[64,2176]{1,0:T(8,128)(2,1)S(1)}, u32[]{:S(2)}, u32[]{:S(2)}) %collective-permute-start.11) | collective-permute-done | bytes 278560 | tf_op jit(solution)/shard_map/ppermute | solution.py:237
  42.7 1.6 %collective-permute-start.16 = (bf16[64,2176]{1,0:T(8,128)(2,1)S(1)}, bf16[64,2176]{1,0:T(8,128)(2,1)S(1)}, u32[]{:S(2)}, u32[]{:S(2)}) collective-permute-start(bf16[64,2176]{1,0:T(8,128)(2,1)S(1)} %collective-permute-done.9.refs_2_), channel_id=1, source_target_pairs={{4,8},{5,9},{8,12},{9,13},{12,14},{13,15},{14,10},{15,11},{10,6},{... | collective-permute-start | bytes 835592 | tf_op jit(solution)/shard_map/ppermute | solution.py:237
  44.7 4.0 %shard_map.84 = (bf16[64,2048]{1,0:T(8,128)(2,1)S(1)}, bf16[64,2048]{1,0:T(8,128)(2,1)S(1)}, bf16[64,2048]{1,0:T(8,128)(2,1)S(1)}, bf16[64,2048]{1,0:T(8,128)(2,1)S(1)}) custom-call(s32[1]{0:T(128)} %bitcast.12.me_ref, bf16[64,2176]{1,0:T(8,128)(2,1)S(1)} %collective-permute-done.11.refs_0_, bf16[64,2176]{1,0:T(8,128)(2,1)S(1)} %collective-permute-done.14.refs_1_, ...), custom_call_target="tpu_custom_call" | custom-call | flops 2415919104 | bytes 2097152 | tf_op jit(solution)/shard_map/pallas_call | solution.py:210
  52.3 2.7 %shard_map.86 = (bf16[64,2048]{1,0:T(8,128)(2,1)S(1)}, bf16[64,2048]{1,0:T(8,128)(2,1)S(1)}) custom-call(s32[1]{0:T(128)} %bitcast.12.me_ref, bf16[64,2176]{1,0:T(8,128)(2,1)S(1)} %collective-permute-done.12.refs_0_, bf16[64,2176]{1,0:T(8,128)(2,1)S(1)} %collective-permute-done.17.refs_1_, bf16[2048,768]{1,0:T(8,128)(2,1)S(1)} %get-tuple-element.64.refs_6_.refs_4_.refs_2_, ...), custom_call_target="tpu_custom_call" | custom-call | flops 2415919104 | bytes 1048576 | tf_op jit(solution)/shard_map/pallas_call | solution.py:210
  55.0 2.2 %collective-permute-done.16.refs_2_ = bf16[64,2176]{1,0:T(8,128)(2,1)S(1)} collective-permute-done((bf16[64,2176]{1,0:T(8,128)(2,1)S(1)}, bf16[64,2176]{1,0:T(8,128)(2,1)S(1)}, u32[]{:S(2)}, u32[]{:S(2)}) %collective-permute-start.16) | collective-permute-done | bytes 278560 | tf_op jit(solution)/shard_map/ppermute | solution.py:237
  57.2 1.6 %collective-permute-done.18.refs_3_ = bf16[64,2176]{1,0:T(8,128)(2,1)S(1)} collective-permute-done((bf16[64,2176]{1,0:T(8,128)(2,1)S(1)}, bf16[64,2176]{1,0:T(8,128)(2,1)S(1)}, u32[]{:S(2)}, u32[]{:S(2)}) %collective-permute-start.18) | collective-permute-done | bytes 278560 | tf_op jit(solution)/shard_map/ppermute | solution.py:237
  60.2 4.0 %shard_map.85 = (bf16[64,2048]{1,0:T(8,128)(2,1)S(1)}, bf16[64,2048]{1,0:T(8,128)(2,1)S(1)}, bf16[64,2048]{1,0:T(8,128)(2,1)S(1)}, bf16[64,2048]{1,0:T(8,128)(2,1)S(1)}) custom-call(s32[1]{0:T(128)} %bitcast.12.me_ref, bf16[64,2176]{1,0:T(8,128)(2,1)S(1)} %collective-permute-done.13.refs_0_, bf16[64,2176]{1,0:T(8,128)(2,1)S(1)} %collective-permute-done.15.refs_1_, ...), custom_call_target="tpu_custom_call" | custom-call | flops 2415919104 | bytes 2097152 | tf_op jit(solution)/shard_map/pallas_call | solution.py:210
  64.2 1.6 %collective-permute-start.19 = (bf16[32,2048]{1,0:T(8,128)(2,1)S(1)}, bf16[32,2048]{1,0:T(8,128)(2,1)S(1)}, u32[]{:S(2)}, u32[]{:S(2)}) collective-permute-start(bf16[32,2048]{1,0:T(8,128)(2,1)S(1)} %get-tuple-element.101), channel_id=1, source_target_pairs={{4,0},{5,1},{8,4},{9,5},{12,8},{13,9},{14,12},{15,13},{10,14},{11,... | collective-permute-start | bytes 393224 | tf_op jit(solution)/shard_map/ppermute | solution.py:237
  66.3 1.7 %collective-permute-start.27 = (bf16[32,2048]{1,0:T(8,128)(2,1)S(1)}, bf16[32,2048]{1,0:T(8,128)(2,1)S(1)}, u32[]{:S(2)}, u32[]{:S(2)}) collective-permute-start(bf16[32,2048]{1,0:T(8,128)(2,1)S(1)} %get-tuple-element.103), channel_id=1, source_target_pairs={{4,0},{5,1},{8,4},{9,5},{12,8},{13,9},{14,12},{15,13},{10,14},{11,... | collective-permute-start | bytes 393224 | tf_op jit(solution)/shard_map/ppermute | solution.py:237
  68.5 2.1 %collective-permute-done.19 = bf16[32,2048]{1,0:T(8,128)(2,1)S(1)} collective-permute-done((bf16[32,2048]{1,0:T(8,128)(2,1)S(1)}, bf16[32,2048]{1,0:T(8,128)(2,1)S(1)}, u32[]{:S(2)}, u32[]{:S(2)}) %collective-permute-start.19) | collective-permute-done | bytes 131104 | tf_op jit(solution)/shard_map/ppermute | solution.py:237
  70.7 1.6 %collective-permute-start.20 = (bf16[64,2048]{1,0:T(8,128)(2,1)S(1)}, bf16[64,2048]{1,0:T(8,128)(2,1)S(1)}, u32[]{:S(2)}, u32[]{:S(2)}) collective-permute-start(bf16[64,2048]{1,0:T(8,128)(2,1)S(1)} %pad_maximum_fusion.2), channel_id=1, source_target_pairs={{4,0},{5,1},{8,4},{9,5},{12,8},{13,9},{14,12},{15,13},{10,14},{11,... | collective-permute-start | bytes 786440 | tf_op jit(solution)/shard_map/ppermute | solution.py:237
  73.5 1.6 %collective-permute-start.28 = (bf16[64,2048]{1,0:T(8,128)(2,1)S(1)}, bf16[64,2048]{1,0:T(8,128)(2,1)S(1)}, u32[]{:S(2)}, u32[]{:S(2)}) collective-permute-start(bf16[64,2048]{1,0:T(8,128)(2,1)S(1)} %pad_maximum_fusion.4), channel_id=1, source_target_pairs={{4,0},{5,1},{8,4},{9,5},{12,8},{13,9},{14,12},{15,13},{10,14},{11,... | collective-permute-start | bytes 786440 | tf_op jit(solution)/shard_map/ppermute | solution.py:237
  75.7 4.3 %collective-permute-done.20 = bf16[64,2048]{1,0:T(8,128)(2,1)S(1)} collective-permute-done((bf16[64,2048]{1,0:T(8,128)(2,1)S(1)}, bf16[64,2048]{1,0:T(8,128)(2,1)S(1)}, u32[]{:S(2)}, u32[]{:S(2)}) %collective-permute-start.20) | collective-permute-done | bytes 262176 | tf_op jit(solution)/shard_map/ppermute | solution.py:237
  80.1 1.6 %collective-permute-start.21 = (bf16[64,2048]{1,0:T(8,128)(2,1)S(1)}, bf16[64,2048]{1,0:T(8,128)(2,1)S(1)}, u32[]{:S(2)}, u32[]{:S(2)}) collective-permute-start(bf16[64,2048]{1,0:T(8,128)(2,1)S(1)} %add_convert_fusion.7), channel_id=1, source_target_pairs={{4,0},{5,1},{8,4},{9,5},{12,8},{13,9},{14,12},{15,13},{10,14},{11,... | collective-permute-start | bytes 786440 | tf_op jit(solution)/shard_map/ppermute | solution.py:237
  82.3 3.3 %collective-permute-done.28 = bf16[64,2048]{1,0:T(8,128)(2,1)S(1)} collective-permute-done((bf16[64,2048]{1,0:T(8,128)(2,1)S(1)}, bf16[64,2048]{1,0:T(8,128)(2,1)S(1)}, u32[]{:S(2)}, u32[]{:S(2)}) %collective-permute-start.28) | collective-permute-done | bytes 262176 | tf_op jit(solution)/shard_map/ppermute | solution.py:237
  85.7 1.6 %collective-permute-start.29 = (bf16[64,2048]{1,0:T(8,128)(2,1)S(1)}, bf16[64,2048]{1,0:T(8,128)(2,1)S(1)}, u32[]{:S(2)}, u32[]{:S(2)}) collective-permute-start(bf16[64,2048]{1,0:T(8,128)(2,1)S(1)} %add_convert_fusion.3), channel_id=1, source_target_pairs={{4,0},{5,1},{8,4},{9,5},{12,8},{13,9},{14,12},{15,13},{10,14},{11,... | collective-permute-start | bytes 786440 | tf_op jit(solution)/shard_map/ppermute | solution.py:237
  87.9 3.3 %collective-permute-done.21 = bf16[64,2048]{1,0:T(8,128)(2,1)S(1)} collective-permute-done((bf16[64,2048]{1,0:T(8,128)(2,1)S(1)}, bf16[64,2048]{1,0:T(8,128)(2,1)S(1)}, u32[]{:S(2)}, u32[]{:S(2)}) %collective-permute-start.21) | collective-permute-done | bytes 262176 | tf_op jit(solution)/shard_map/ppermute | solution.py:237
  91.3 1.6 %collective-permute-start.22 = (bf16[64,2048]{1,0:T(8,128)(2,1)S(1)}, bf16[64,2048]{1,0:T(8,128)(2,1)S(1)}, u32[]{:S(2)}, u32[]{:S(2)}) collective-permute-start(bf16[64,2048]{1,0:T(8,128)(2,1)S(1)} %add_convert_fusion.6), channel_id=1, source_target_pairs={{4,0},{5,1},{8,4},{9,5},{12,8},{13,9},{14,12},{15,13},{10,14},{11,... | collective-permute-start | bytes 786440 | tf_op jit(solution)/shard_map/ppermute | solution.py:237
  93.5 3.3 %collective-permute-done.29 = bf16[64,2048]{1,0:T(8,128)(2,1)S(1)} collective-permute-done((bf16[64,2048]{1,0:T(8,128)(2,1)S(1)}, bf16[64,2048]{1,0:T(8,128)(2,1)S(1)}, u32[]{:S(2)}, u32[]{:S(2)}) %collective-permute-start.29) | collective-permute-done | bytes 262176 | tf_op jit(solution)/shard_map/ppermute | solution.py:237
  96.9 1.6 %collective-permute-start.30 = (bf16[64,2048]{1,0:T(8,128)(2,1)S(1)}, bf16[64,2048]{1,0:T(8,128)(2,1)S(1)}, u32[]{:S(2)}, u32[]{:S(2)}) collective-permute-start(bf16[64,2048]{1,0:T(8,128)(2,1)S(1)} %add_convert_fusion.2), channel_id=1, source_target_pairs={{4,0},{5,1},{8,4},{9,5},{12,8},{13,9},{14,12},{15,13},{10,14},{11,... | collective-permute-start | bytes 786440 | tf_op jit(solution)/shard_map/ppermute | solution.py:237
  99.1 2.2 %collective-permute-done.22 = bf16[64,2048]{1,0:T(8,128)(2,1)S(1)} collective-permute-done((bf16[64,2048]{1,0:T(8,128)(2,1)S(1)}, bf16[64,2048]{1,0:T(8,128)(2,1)S(1)}, u32[]{:S(2)}, u32[]{:S(2)}) %collective-permute-start.22) | collective-permute-done | bytes 262176 | tf_op jit(solution)/shard_map/ppermute | solution.py:237
  101.4 1.4 %collective-permute-done.26 = bf16[64,2048]{1,0:T(8,128)(2,1)S(1)} collective-permute-done((bf16[64,2048]{1,0:T(8,128)(2,1)S(1)}, bf16[64,2048]{1,0:T(8,128)(2,1)S(1)}, u32[]{:S(2)}, u32[]{:S(2)}) %collective-permute-start.26) | collective-permute-done | bytes 262176 | tf_op jit(solution)/shard_map/ppermute | solution.py:237
  104.2 1.4 %collective-permute-done.34 = bf16[64,2048]{1,0:T(8,128)(2,1)S(1)} collective-permute-done((bf16[64,2048]{1,0:T(8,128)(2,1)S(1)}, bf16[64,2048]{1,0:T(8,128)(2,1)S(1)}, u32[]{:S(2)}, u32[]{:S(2)}) %collective-permute-start.34) | collective-permute-done | bytes 262176 | tf_op jit(solution)/shard_map/ppermute | solution.py:237
  (108 shorter events, 25.1 us)
Async XLA Ops:
  0.0 8.2 %collective-permute-start.6 = (bf16[2048,768]{1,0:T(8,128)(2,1)}, bf16[2048,768]{1,0:T(8,128)(2,1)}, u32[]{:S(2)}, u32[]{:S(2)}) collective-permute-start(bf16[2048,768]{1,0:T(8,128)(2,1)} %bitcast.31), channel_id=1, source_target_pairs={{0,1},{1,0},{2,3},{3,2},{4,5},{5,4},{6,7},{7,6},{8,9},{9,8},{10,11... | collective-permute-start | bytes 9437192 | tf_op jit(solution)/shard_map/ppermute | solution.py:240
  2.4 9.6 %collective-permute-start.3 = (bf16[64,2048]{1,0:T(8,128)(2,1)S(1)}, bf16[64,2048]{1,0:T(8,128)(2,1)S(1)}, u32[]{:S(2)}, u32[]{:S(2)}) collective-permute-start(bf16[64,2048]{1,0:T(8,128)(2,1)S(1)} %get-tuple-element.99), channel_id=1, source_target_pairs={{0,16},{16,0},{1,17},{17,1},{2,18},{18,2},{3,19},{19,3},{4,20},{20... | collective-permute-start | bytes 786440 | tf_op jit(solution)/shard_map/ppermute | solution.py:247
  4.9 12.4 %collective-permute-start = (bf16[64,2048]{1,0:T(8,128)(2,1)}, bf16[64,2048]{1,0:T(8,128)(2,1)S(1)}, u32[]{:S(2)}, u32[]{:S(2)}) collective-permute-start(bf16[64,2048]{1,0:T(8,128)(2,1)} %get-tuple-element.100), channel_id=1, source_target_pairs={{0,16},{16,0},{1,17},{17,1},{2,18},{18,2},{3,19},{19,3},{4,20},{20... | collective-permute-start | bytes 786440 | tf_op jit(solution)/shard_map/ppermute | solution.py:247
  4.9 15.2 %collective-permute-start.8 = (bf16[768,2048]{1,0:T(8,128)(2,1)}, bf16[768,2048]{1,0:T(8,128)(2,1)}, u32[]{:S(2)}, u32[]{:S(2)}) collective-permute-start(bf16[768,2048]{1,0:T(8,128)(2,1)} %bitcast.35), channel_id=1, source_target_pairs={{0,1},{1,0},{2,3},{3,2},{4,5},{5,4},{6,7},{7,6},{8,9},{9,8},{10,11... | collective-permute-start | bytes 9437192 | tf_op jit(solution)/shard_map/ppermute | solution.py:240
  8.2 12.1 %collective-permute-start.7 = (bf16[2048,768]{1,0:T(8,128)(2,1)}, bf16[2048,768]{1,0:T(8,128)(2,1)}, u32[]{:S(2)}, u32[]{:S(2)}) collective-permute-start(bf16[2048,768]{1,0:T(8,128)(2,1)} %bitcast.33), channel_id=1, source_target_pairs={{0,1},{1,0},{2,3},{3,2},{4,5},{5,4},{6,7},{7,6},{8,9},{9,8},{10,11... | collective-permute-start | bytes 9437192 | tf_op jit(solution)/shard_map/ppermute | solution.py:240
  12.4 14.4 %collective-permute-start.4 = (bf16[64,2176]{1,0:T(8,128)(2,1)S(1)}, bf16[64,2176]{1,0:T(8,128)(2,1)S(1)}, u32[]{:S(2)}, u32[]{:S(2)}) collective-permute-start(bf16[64,2176]{1,0:T(8,128)(2,1)S(1)} %pad_maximum_fusion.1.refs_5_), channel_id=1, source_target_pairs={{4,8},{5,9},{8,12},{9,13},{12,14},{13,15},{14,10},{15,11},{10,6},{... | collective-permute-start | bytes 835592 | tf_op jit(solution)/shard_map/ppermute | solution.py:237
  14.5 12.3 %collective-permute-start.5 = (bf16[64,2176]{1,0:T(8,128)(2,1)S(1)}, bf16[64,2176]{1,0:T(8,128)(2,1)S(1)}, u32[]{:S(2)}, u32[]{:S(2)}) collective-permute-start(bf16[64,2176]{1,0:T(8,128)(2,1)S(1)} %pad_maximum_fusion.1.refs_5_), channel_id=1, source_target_pairs={{4,0},{5,1},{8,4},{9,5},{12,8},{13,9},{14,12},{15,13},{10,14},{11,... | collective-permute-start | bytes 835592 | tf_op jit(solution)/shard_map/ppermute | solution.py:237
  18.2 8.6 %collective-permute-start.1 = (bf16[64,2176]{1,0:T(8,128)(2,1)S(1)}, bf16[64,2176]{1,0:T(8,128)(2,1)}, u32[]{:S(2)}, u32[]{:S(2)}) collective-permute-start(bf16[64,2176]{1,0:T(8,128)(2,1)S(1)} %pad_maximum_fusion.refs_4_), channel_id=1, source_target_pairs={{4,8},{5,9},{8,12},{9,13},{12,14},{13,15},{14,10},{15,11},{10,6},{... | collective-permute-start | bytes 835592 | tf_op jit(solution)/shard_map/ppermute | solution.py:237
  20.1 7.8 %collective-permute-start.2 = (bf16[64,2176]{1,0:T(8,128)(2,1)S(1)}, bf16[64,2176]{1,0:T(8,128)(2,1)S(1)}, u32[]{:S(2)}, u32[]{:S(2)}) collective-permute-start(bf16[64,2176]{1,0:T(8,128)(2,1)S(1)} %pad_maximum_fusion.refs_4_), channel_id=1, source_target_pairs={{4,0},{5,1},{8,4},{9,5},{12,8},{13,9},{14,12},{15,13},{10,14},{11,... | collective-permute-start | bytes 835592 | tf_op jit(solution)/shard_map/ppermute | solution.py:237
  27.9 10.8 %collective-permute-start.10 = (bf16[64,2176]{1,0:T(8,128)(2,1)S(1)}, bf16[64,2176]{1,0:T(8,128)(2,1)S(1)}, u32[]{:S(2)}, u32[]{:S(2)}) collective-permute-start(bf16[64,2176]{1,0:T(8,128)(2,1)S(1)} %collective-permute-done.5.refs_3_), channel_id=1, source_target_pairs={{4,0},{5,1},{8,4},{9,5},{12,8},{13,9},{14,12},{15,13},{10,14},{11,... | collective-permute-start | bytes 835592 | tf_op jit(solution)/shard_map/ppermute | solution.py:237
  28.7 10.1 %collective-permute-start.9 = (bf16[64,2176]{1,0:T(8,128)(2,1)S(1)}, bf16[64,2176]{1,0:T(8,128)(2,1)S(1)}, u32[]{:S(2)}, u32[]{:S(2)}) collective-permute-start(bf16[64,2176]{1,0:T(8,128)(2,1)S(1)} %collective-permute-done.4.refs_2_), channel_id=1, source_target_pairs={{4,8},{5,9},{8,12},{9,13},{12,14},{13,15},{14,10},{15,11},{10,6},{... | collective-permute-start | bytes 835592 | tf_op jit(solution)/shard_map/ppermute | solution.py:237
  30.0 11.9 %collective-permute-start.11 = (bf16[64,2176]{1,0:T(8,128)(2,1)}, bf16[64,2176]{1,0:T(8,128)(2,1)S(1)}, u32[]{:S(2)}, u32[]{:S(2)}) collective-permute-start(bf16[64,2176]{1,0:T(8,128)(2,1)} %collective-permute-done.1.refs_0_), channel_id=1, source_target_pairs={{4,8},{5,9},{8,12},{9,13},{12,14},{13,15},{14,10},{15,11},{10,6},{... | collective-permute-start | bytes 835592 | tf_op jit(solution)/shard_map/ppermute | solution.py:237
  31.5 12.8 %collective-permute-start.14 = (bf16[64,2176]{1,0:T(8,128)(2,1)S(1)}, bf16[64,2176]{1,0:T(8,128)(2,1)S(1)}, u32[]{:S(2)}, u32[]{:S(2)}) collective-permute-start(bf16[64,2176]{1,0:T(8,128)(2,1)S(1)} %collective-permute-done.2.refs_1_), channel_id=1, source_target_pairs={{4,0},{5,1},{8,4},{9,5},{12,8},{13,9},{14,12},{15,13},{10,14},{11,... | collective-permute-start | bytes 835592 | tf_op jit(solution)/shard_map/ppermute | solution.py:237
  38.7 10.2 %collective-permute-start.17 = (bf16[64,2176]{1,0:T(8,128)(2,1)S(1)}, bf16[64,2176]{1,0:T(8,128)(2,1)S(1)}, u32[]{:S(2)}, u32[]{:S(2)}) collective-permute-start(bf16[64,2176]{1,0:T(8,128)(2,1)S(1)} %collective-permute-done.10.refs_3_), channel_id=1, source_target_pairs={{4,0},{5,1},{8,4},{9,5},{12,8},{13,9},{14,12},{15,13},{10,14},{11,... | collective-permute-start | bytes 835592 | tf_op jit(solution)/shard_map/ppermute | solution.py:237
  41.9 9.6 %collective-permute-start.12 = (bf16[64,2176]{1,0:T(8,128)(2,1)S(1)}, bf16[64,2176]{1,0:T(8,128)(2,1)S(1)}, u32[]{:S(2)}, u32[]{:S(2)}) collective-permute-start(bf16[64,2176]{1,0:T(8,128)(2,1)S(1)} %collective-permute-done.11.refs_0_), channel_id=1, source_target_pairs={{4,8},{5,9},{8,12},{9,13},{12,14},{13,15},{14,10},{15,11},{10,6},{... | collective-permute-start | bytes 835592 | tf_op jit(solution)/shard_map/ppermute | solution.py:237
  42.7 14.5 %collective-permute-start.16 = (bf16[64,2176]{1,0:T(8,128)(2,1)S(1)}, bf16[64,2176]{1,0:T(8,128)(2,1)S(1)}, u32[]{:S(2)}, u32[]{:S(2)}) collective-permute-start(bf16[64,2176]{1,0:T(8,128)(2,1)S(1)} %collective-permute-done.9.refs_2_), channel_id=1, source_target_pairs={{4,8},{5,9},{8,12},{9,13},{12,14},{13,15},{14,10},{15,11},{10,6},{... | collective-permute-start | bytes 835592 | tf_op jit(solution)/shard_map/ppermute | solution.py:237
  44.3 12.9 %collective-permute-start.15 = (bf16[64,2176]{1,0:T(8,128)(2,1)S(1)}, bf16[64,2176]{1,0:T(8,128)(2,1)S(1)}, u32[]{:S(2)}, u32[]{:S(2)}) collective-permute-start(bf16[64,2176]{1,0:T(8,128)(2,1)S(1)} %collective-permute-done.14.refs_1_), channel_id=1, source_target_pairs={{4,0},{5,1},{8,4},{9,5},{12,8},{13,9},{14,12},{15,13},{10,14},{11,... | collective-permute-start | bytes 835592 | tf_op jit(solution)/shard_map/ppermute | solution.py:237
  49.0 9.8 %collective-permute-start.18 = (bf16[64,2176]{1,0:T(8,128)(2,1)S(1)}, bf16[64,2176]{1,0:T(8,128)(2,1)S(1)}, u32[]{:S(2)}, u32[]{:S(2)}) collective-permute-start(bf16[64,2176]{1,0:T(8,128)(2,1)S(1)} %collective-permute-done.17.refs_1_), channel_id=1, source_target_pairs={{4,0},{5,1},{8,4},{9,5},{12,8},{13,9},{14,12},{15,13},{10,14},{11,... | collective-permute-start | bytes 835592 | tf_op jit(solution)/shard_map/ppermute | solution.py:237
  51.5 8.7 %collective-permute-start.13 = (bf16[64,2176]{1,0:T(8,128)(2,1)S(1)}, bf16[64,2176]{1,0:T(8,128)(2,1)S(1)}, u32[]{:S(2)}, u32[]{:S(2)}) collective-permute-start(bf16[64,2176]{1,0:T(8,128)(2,1)S(1)} %collective-permute-done.12.refs_0_), channel_id=1, source_target_pairs={{4,8},{5,9},{8,12},{9,13},{12,14},{13,15},{14,10},{15,11},{10,6},{... | collective-permute-start | bytes 835592 | tf_op jit(solution)/shard_map/ppermute | solution.py:237
  66.3 7.1 %collective-permute-start.27 = (bf16[32,2048]{1,0:T(8,128)(2,1)S(1)}, bf16[32,2048]{1,0:T(8,128)(2,1)S(1)}, u32[]{:S(2)}, u32[]{:S(2)}) collective-permute-start(bf16[32,2048]{1,0:T(8,128)(2,1)S(1)} %get-tuple-element.103), channel_id=1, source_target_pairs={{4,0},{5,1},{8,4},{9,5},{12,8},{13,9},{14,12},{15,13},{10,14},{11,... | collective-permute-start | bytes 393224 | tf_op jit(solution)/shard_map/ppermute | solution.py:237
  68.0 7.1 %collective-permute-start.31 = (bf16[32,2048]{1,0:T(8,128)(2,1)S(1)}, bf16[32,2048]{1,0:T(8,128)(2,1)S(1)}, u32[]{:S(2)}, u32[]{:S(2)}) collective-permute-start(bf16[32,2048]{1,0:T(8,128)(2,1)S(1)} %get-tuple-element.104), channel_id=1, source_target_pairs={{4,8},{5,9},{8,12},{9,13},{12,14},{13,15},{14,10},{15,11},{10,6},{... | collective-permute-start | bytes 393224 | tf_op jit(solution)/shard_map/ppermute | solution.py:237
  70.7 9.3 %collective-permute-start.20 = (bf16[64,2048]{1,0:T(8,128)(2,1)S(1)}, bf16[64,2048]{1,0:T(8,128)(2,1)S(1)}, u32[]{:S(2)}, u32[]{:S(2)}) collective-permute-start(bf16[64,2048]{1,0:T(8,128)(2,1)S(1)} %pad_maximum_fusion.2), channel_id=1, source_target_pairs={{4,0},{5,1},{8,4},{9,5},{12,8},{13,9},{14,12},{15,13},{10,14},{11,... | collective-permute-start | bytes 786440 | tf_op jit(solution)/shard_map/ppermute | solution.py:237
  72.4 9.3 %collective-permute-start.24 = (bf16[64,2048]{1,0:T(8,128)(2,1)S(1)}, bf16[64,2048]{1,0:T(8,128)(2,1)S(1)}, u32[]{:S(2)}, u32[]{:S(2)}) collective-permute-start(bf16[64,2048]{1,0:T(8,128)(2,1)S(1)} %pad_maximum_fusion.3), channel_id=1, source_target_pairs={{4,8},{5,9},{8,12},{9,13},{12,14},{13,15},{14,10},{15,11},{10,6},{... | collective-permute-start | bytes 786440 | tf_op jit(solution)/shard_map/ppermute | solution.py:237
  73.5 12.1 %collective-permute-start.28 = (bf16[64,2048]{1,0:T(8,128)(2,1)S(1)}, bf16[64,2048]{1,0:T(8,128)(2,1)S(1)}, u32[]{:S(2)}, u32[]{:S(2)}) collective-permute-start(bf16[64,2048]{1,0:T(8,128)(2,1)S(1)} %pad_maximum_fusion.4), channel_id=1, source_target_pairs={{4,0},{5,1},{8,4},{9,5},{12,8},{13,9},{14,12},{15,13},{10,14},{11,... | collective-permute-start | bytes 786440 | tf_op jit(solution)/shard_map/ppermute | solution.py:237
  75.2 12.1 %collective-permute-start.32 = (bf16[64,2048]{1,0:T(8,128)(2,1)S(1)}, bf16[64,2048]{1,0:T(8,128)(2,1)S(1)}, u32[]{:S(2)}, u32[]{:S(2)}) collective-permute-start(bf16[64,2048]{1,0:T(8,128)(2,1)S(1)} %pad_maximum_fusion.5), channel_id=1, source_target_pairs={{4,8},{5,9},{8,12},{9,13},{12,14},{13,15},{14,10},{15,11},{10,6},{... | collective-permute-start | bytes 786440 | tf_op jit(solution)/shard_map/ppermute | solution.py:237
  80.1 11.2 %collective-permute-start.21 = (bf16[64,2048]{1,0:T(8,128)(2,1)S(1)}, bf16[64,2048]{1,0:T(8,128)(2,1)S(1)}, u32[]{:S(2)}, u32[]{:S(2)}) collective-permute-start(bf16[64,2048]{1,0:T(8,128)(2,1)S(1)} %add_convert_fusion.7), channel_id=1, source_target_pairs={{4,0},{5,1},{8,4},{9,5},{12,8},{13,9},{14,12},{15,13},{10,14},{11,... | collective-permute-start | bytes 786440 | tf_op jit(solution)/shard_map/ppermute | solution.py:237
  81.8 11.2 %collective-permute-start.25 = (bf16[64,2048]{1,0:T(8,128)(2,1)S(1)}, bf16[64,2048]{1,0:T(8,128)(2,1)S(1)}, u32[]{:S(2)}, u32[]{:S(2)}) collective-permute-start(bf16[64,2048]{1,0:T(8,128)(2,1)S(1)} %add_convert_fusion.5), channel_id=1, source_target_pairs={{4,8},{5,9},{8,12},{9,13},{12,14},{13,15},{14,10},{15,11},{10,6},{... | collective-permute-start | bytes 786440 | tf_op jit(solution)/shard_map/ppermute | solution.py:237
  85.7 11.2 %collective-permute-start.29 = (bf16[64,2048]{1,0:T(8,128)(2,1)S(1)}, bf16[64,2048]{1,0:T(8,128)(2,1)S(1)}, u32[]{:S(2)}, u32[]{:S(2)}) collective-permute-start(bf16[64,2048]{1,0:T(8,128)(2,1)S(1)} %add_convert_fusion.3), channel_id=1, source_target_pairs={{4,0},{5,1},{8,4},{9,5},{12,8},{13,9},{14,12},{15,13},{10,14},{11,... | collective-permute-start | bytes 786440 | tf_op jit(solution)/shard_map/ppermute | solution.py:237
  87.4 11.2 %collective-permute-start.33 = (bf16[64,2048]{1,0:T(8,128)(2,1)S(1)}, bf16[64,2048]{1,0:T(8,128)(2,1)S(1)}, u32[]{:S(2)}, u32[]{:S(2)}) collective-permute-start(bf16[64,2048]{1,0:T(8,128)(2,1)S(1)} %add_convert_fusion.1), channel_id=1, source_target_pairs={{4,8},{5,9},{8,12},{9,13},{12,14},{13,15},{14,10},{15,11},{10,6},{... | collective-permute-start | bytes 786440 | tf_op jit(solution)/shard_map/ppermute | solution.py:237
  91.3 10.1 %collective-permute-start.22 = (bf16[64,2048]{1,0:T(8,128)(2,1)S(1)}, bf16[64,2048]{1,0:T(8,128)(2,1)S(1)}, u32[]{:S(2)}, u32[]{:S(2)}) collective-permute-start(bf16[64,2048]{1,0:T(8,128)(2,1)S(1)} %add_convert_fusion.6), channel_id=1, source_target_pairs={{4,0},{5,1},{8,4},{9,5},{12,8},{13,9},{14,12},{15,13},{10,14},{11,... | collective-permute-start | bytes 786440 | tf_op jit(solution)/shard_map/ppermute | solution.py:237
  93.0 9.8 %collective-permute-start.26 = (bf16[64,2048]{1,0:T(8,128)(2,1)S(1)}, bf16[64,2048]{1,0:T(8,128)(2,1)S(1)}, u32[]{:S(2)}, u32[]{:S(2)}) collective-permute-start(bf16[64,2048]{1,0:T(8,128)(2,1)S(1)} %add_convert_fusion.4), channel_id=1, source_target_pairs={{4,8},{5,9},{8,12},{9,13},{12,14},{13,15},{14,10},{15,11},{10,6},{... | collective-permute-start | bytes 786440 | tf_op jit(solution)/shard_map/ppermute | solution.py:237
  96.9 7.3 %collective-permute-start.30 = (bf16[64,2048]{1,0:T(8,128)(2,1)S(1)}, bf16[64,2048]{1,0:T(8,128)(2,1)S(1)}, u32[]{:S(2)}, u32[]{:S(2)}) collective-permute-start(bf16[64,2048]{1,0:T(8,128)(2,1)S(1)} %add_convert_fusion.2), channel_id=1, source_target_pairs={{4,0},{5,1},{8,4},{9,5},{12,8},{13,9},{14,12},{15,13},{10,14},{11,... | collective-permute-start | bytes 786440 | tf_op jit(solution)/shard_map/ppermute | solution.py:237
  (8 other events, 88.8 us)

commit v4 on v3

--- a/solution.py
+++ b/solution.py
@@ -310,7 +310,9 @@
                 waiting += [(b, 1, 0) for b in range(batches)] if k == 2 else []
                 add_sums(waiting)
 
-        add_sums([(*chain, top[chain]) for chain in chains])
+        add_sums([(*chain, far) for chain in chains if top[chain] == far])
+        if halved:
+            add_sums([(*chain, far - 1) for chain in chains if top[chain] < far])
         total = {}
         for chain in chains:
             step = chain[1]

time: 107 us -> 106 us (level)
  waiting for transfers between devices: 38.4 us -> 35.7 us
  Pallas kernels: 23.9 us -> 25.4 us
    ppermute x30, waiting for transfers between devices: 33.2 us -> 30.6 us  [hop(): return lax.ppermute(value, 'expert', pairs)]
    pallas_call x4 -> x5, Pallas kernels: 17.4 us -> 18.9 us  [group_sums(): pl.pallas_call(kernel, out_shape=[pltpu.VMEM((size, features), jnp.bfloat...]
  transfers between devices with their start and end apart: 35 -> 35, of which waited for: 19 -> 18; matrix products, arithmetic and copies ran while one was open for 7% -> 7% of each run, Pallas kernels for 19% -> 22%
where the time goes in v4:
time: 106 us; the launch traced here: 105 us
  waiting for transfers between devices  35.7 us (34%)
  starting transfers between devices  34.6 us (33%)
  Pallas kernels  25.4 us (24%)
  local copies, waits for them, and re-layouts  4.46 us (4%)
  other arithmetic  3.84 us (4%)
    ppermute x30, starting transfers between devices, hop(): return lax.ppermute(value, 'expert', pairs)  31 us
    ppermute x30, waiting for transfers between devices, hop(): return lax.ppermute(value, 'expert', pairs)  30.6 us
    pallas_call x5, Pallas kernels, group_sums(): pl.pallas_call(kernel, out_shape=[pltpu.VMEM((size, features), jnp.bfloat...  18.9 us
    pallas_call x1, Pallas kernels, in_vmem(): pl.pallas_call(load_kernel, out_shape=[pltpu.VMEM(value.shape, value.dtyp...  6.49 us
    ppermute x2, waiting for transfers between devices, shards(): lax.ppermute(emitted[0, b], 'section', around)  5.13 us
    ppermute x2, starting transfers between devices, shards(): lax.ppermute(emitted[0, b], 'section', around)  2.5 us
  transfers between devices with their start and end apart: 35, of which 18 were waited for; matrix products, arithmetic and copies ran while one was open for 7% of the time, Pallas kernels for 22%

profile of v4, /device:TPU:0, one launch (start us, length us, event | category | flops | bytes accessed | tf_op | source)
XLA Modules:
  0.0 105.3 jit_solution(1301673897932115016)
XLA Ops:
  0.5 1.9 %slice_bitcast_fusion = (bf16[64,2048]{1,0:T(8,128)(2,1)S(1)}, bf16[64,2048]{1,0:T(8,128)(2,1)}) fusion(bf16[1,2,64,2048]{3,2,1,0:T(8,128)(2,1)} %param.8), kind=kLoop, calls=%fused_computation.47 | loop fusion | bytes 1048576 | tf_op jit(solution)/shard_map/squeeze | solution.py:247
  2.4 2.5 %collective-permute-start.3 = (bf16[64,2048]{1,0:T(8,128)(2,1)S(1)}, bf16[64,2048]{1,0:T(8,128)(2,1)S(1)}, u32[]{:S(2)}, u32[]{:S(2)}) collective-permute-start(bf16[64,2048]{1,0:T(8,128)(2,1)S(1)} %get-tuple-element.99), channel_id=1, source_target_pairs={{0,16},{16,0},{1,17},{17,1},{2,18},{18,2},{3,19},{19,3},{4,20},{20... | collective-permute-start | bytes 786440 | tf_op jit(solution)/shard_map/ppermute | solution.py:247
  9.7 2.3 %collective-permute-done.3 = bf16[64,2048]{1,0:T(8,128)(2,1)S(1)} collective-permute-done((bf16[64,2048]{1,0:T(8,128)(2,1)S(1)}, bf16[64,2048]{1,0:T(8,128)(2,1)S(1)}, u32[]{:S(2)}, u32[]{:S(2)}) %collective-permute-start.3) | collective-permute-done | bytes 262176 | tf_op jit(solution)/shard_map/ppermute | solution.py:247
  12.4 2.1 %collective-permute-start.4 = (bf16[64,2176]{1,0:T(8,128)(2,1)S(1)}, bf16[64,2176]{1,0:T(8,128)(2,1)S(1)}, u32[]{:S(2)}, u32[]{:S(2)}) collective-permute-start(bf16[64,2176]{1,0:T(8,128)(2,1)S(1)} %pad_maximum_fusion.1.refs_5_), channel_id=1, source_target_pairs={{4,8},{5,9},{8,12},{9,13},{12,14},{13,15},{14,10},{15,11},{10,6},{... | collective-permute-start | bytes 835592 | tf_op jit(solution)/shard_map/ppermute | solution.py:237
  14.5 2.8 %collective-permute-done = bf16[64,2048]{1,0:T(8,128)(2,1)S(1)} collective-permute-done((bf16[64,2048]{1,0:T(8,128)(2,1)}, bf16[64,2048]{1,0:T(8,128)(2,1)S(1)}, u32[]{:S(2)}, u32[]{:S(2)}) %collective-permute-start) | collective-permute-done | bytes 262176 | tf_op jit(solution)/shard_map/ppermute | solution.py:247
  18.2 1.9 %collective-permute-start.1 = (bf16[64,2176]{1,0:T(8,128)(2,1)S(1)}, bf16[64,2176]{1,0:T(8,128)(2,1)}, u32[]{:S(2)}, u32[]{:S(2)}) collective-permute-start(bf16[64,2176]{1,0:T(8,128)(2,1)S(1)} %pad_maximum_fusion.refs_4_), channel_id=1, source_target_pairs={{4,8},{5,9},{8,12},{9,13},{12,14},{13,15},{14,10},{15,11},{10,6},{... | collective-permute-start | bytes 835592 | tf_op jit(solution)/shard_map/ppermute | solution.py:237
  20.3 6.5 %shard_map.82 = (bf16[2048,768]{1,0:T(8,128)(2,1)S(1)}, bf16[2048,768]{1,0:T(8,128)(2,1)S(1)}, bf16[768,2048]{1,0:T(8,128)(2,1)S(1)}, bf16[2048,768]{1,0:T(8,128...) custom-call(bf16[2048,768]{1,0:T(8,128)(2,1)} %bitcast.32, bf16[2048,768]{1,0:T(8,128)(2,1)} %bitcast.34, ...), custom_call_target="tpu_custom_call" | custom-call | tf_op jit(solution)/shard_map/pallas_call | solution.py:175
  30.0 1.6 %collective-permute-start.11 = (bf16[64,2176]{1,0:T(8,128)(2,1)}, bf16[64,2176]{1,0:T(8,128)(2,1)S(1)}, u32[]{:S(2)}, u32[]{:S(2)}) collective-permute-start(bf16[64,2176]{1,0:T(8,128)(2,1)} %collective-permute-done.1.refs_0_), channel_id=1, source_target_pairs={{4,8},{5,9},{8,12},{9,13},{12,14},{13,15},{14,10},{15,11},{10,6},{... | collective-permute-start | bytes 835592 | tf_op jit(solution)/shard_map/ppermute | solution.py:237
  32.0 6.7 %shard_map.83 = (bf16[64,2048]{1,0:T(8,128)(2,1)S(1)}, bf16[64,2048]{1,0:T(8,128)(2,1)S(1)}, bf16[64,2048]{1,0:T(8,128)(2,1)S(1)}, bf16[64,2048]{1,0:T(8,128)(2,...) custom-call(s32[1]{0:T(128)} %bitcast.12.me_ref, bf16[64,2176]{1,0:T(8,128)(2,1)} %collective-permute-done.1.refs_0_, ...), custom_call_target="tpu_custom_call" | custom-call | flops 3623878656 | bytes 3145728 | tf_op jit(solution)/shard_map/pallas_call | solution.py:210
  39.8 2.1 %collective-permute-done.11.refs_0_ = bf16[64,2176]{1,0:T(8,128)(2,1)S(1)} collective-permute-done((bf16[64,2176]{1,0:T(8,128)(2,1)}, bf16[64,2176]{1,0:T(8,128)(2,1)S(1)}, u32[]{:S(2)}, u32[]{:S(2)}) %collective-permute-start.11) | collective-permute-done | bytes 278560 | tf_op jit(solution)/shard_map/ppermute | solution.py:237
  42.7 1.6 %collective-permute-start.22 = (bf16[64,2176]{1,0:T(8,128)(2,1)S(1)}, bf16[64,2176]{1,0:T(8,128)(2,1)S(1)}, u32[]{:S(2)}, u32[]{:S(2)}) collective-permute-start(bf16[64,2176]{1,0:T(8,128)(2,1)S(1)} %collective-permute-done.9.refs_2_), channel_id=1, source_target_pairs={{4,8},{5,9},{8,12},{9,13},{12,14},{13,15},{14,10},{15,11},{10,6},{... | collective-permute-start | bytes 835592 | tf_op jit(solution)/shard_map/ppermute | solution.py:237
  44.7 4.0 %shard_map.84 = (bf16[64,2048]{1,0:T(8,128)(2,1)S(1)}, bf16[64,2048]{1,0:T(8,128)(2,1)S(1)}, bf16[64,2048]{1,0:T(8,128)(2,1)S(1)}, bf16[64,2048]{1,0:T(8,128)(2,1)S(1)}) custom-call(s32[1]{0:T(128)} %bitcast.12.me_ref, bf16[64,2176]{1,0:T(8,128)(2,1)S(1)} %collective-permute-done.11.refs_0_, bf16[64,2176]{1,0:T(8,128)(2,1)S(1)} %collective-permute-done.15.refs_1_, ...), custom_call_target="tpu_custom_call" | custom-call | flops 2415919104 | bytes 2097152 | tf_op jit(solution)/shard_map/pallas_call | solution.py:210
  52.3 2.7 %shard_map.86 = (bf16[64,2048]{1,0:T(8,128)(2,1)S(1)}, bf16[64,2048]{1,0:T(8,128)(2,1)S(1)}) custom-call(s32[1]{0:T(128)} %bitcast.12.me_ref, bf16[64,2176]{1,0:T(8,128)(2,1)S(1)} %collective-permute-done.12.refs_0_, bf16[64,2176]{1,0:T(8,128)(2,1)S(1)} %collective-permute-done.14.refs_1_, bf16[2048,768]{1,0:T(8,128)(2,1)S(1)} %get-tuple-element.64.refs_6_.refs_4_.refs_2_, ...), custom_call_target="tpu_custom_call" | custom-call | flops 2415919104 | bytes 1048576 | tf_op jit(solution)/shard_map/pallas_call | solution.py:210
  55.0 2.2 %collective-permute-done.22.refs_1_ = bf16[64,2176]{1,0:T(8,128)(2,1)S(1)} collective-permute-done((bf16[64,2176]{1,0:T(8,128)(2,1)S(1)}, bf16[64,2176]{1,0:T(8,128)(2,1)S(1)}, u32[]{:S(2)}, u32[]{:S(2)}) %collective-permute-start.22) | collective-permute-done | bytes 278560 | tf_op jit(solution)/shard_map/ppermute | solution.py:237
  57.2 2.7 %shard_map.87 = (bf16[64,2048]{1,0:T(8,128)(2,1)S(1)}, bf16[64,2048]{1,0:T(8,128)(2,1)S(1)}) custom-call(s32[1]{0:T(128)} %bitcast.12.me_ref, bf16[64,2176]{1,0:T(8,128)(2,1)S(1)} %collective-permute-done.21.refs_0_, bf16[64,2176]{1,0:T(8,128)(2,1)S(1)} %collective-permute-done.22.refs_1_, bf16[2048,768]{1,0:T(8,128)(2,1)S(1)} %get-tuple-element.64.refs_6_.refs_4_.refs_2_, ...), custom_call_target="tpu_custom_call" | custom-call | flops 2415919104 | bytes 1048576 | tf_op jit(solution)/shard_map/pallas_call | solution.py:210
  60.2 2.7 %shard_map.85 = (bf16[64,2048]{1,0:T(8,128)(2,1)S(1)}, bf16[64,2048]{1,0:T(8,128)(2,1)S(1)}) custom-call(s32[1]{0:T(128)} %bitcast.12.me_ref, bf16[64,2176]{1,0:T(8,128)(2,1)S(1)} %collective-permute-done.13.refs_0_, bf16[64,2176]{1,0:T(8,128)(2,1)S(1)} %collective-permute-done.16.refs_1_, bf16[2048,768]{1,0:T(8,128)(2,1)S(1)} %get-tuple-element.64.refs_6_.refs_4_.refs_2_, ...), custom_call_target="tpu_custom_call" | custom-call | flops 2415919104 | bytes 1048576 | tf_op jit(solution)/shard_map/pallas_call | solution.py:210
  63.0 1.6 %collective-permute-start.17 = (bf16[32,2048]{1,0:T(8,128)(2,1)S(1)}, bf16[32,2048]{1,0:T(8,128)(2,1)S(1)}, u32[]{:S(2)}, u32[]{:S(2)}) collective-permute-start(bf16[32,2048]{1,0:T(8,128)(2,1)S(1)} %get-tuple-element.101), channel_id=1, source_target_pairs={{4,0},{5,1},{8,4},{9,5},{12,8},{13,9},{14,12},{15,13},{10,14},{11,... | collective-permute-start | bytes 393224 | tf_op jit(solution)/shard_map/ppermute | solution.py:237
  65.1 1.6 %collective-permute-start.27 = (bf16[32,2048]{1,0:T(8,128)(2,1)S(1)}, bf16[32,2048]{1,0:T(8,128)(2,1)S(1)}, u32[]{:S(2)}, u32[]{:S(2)}) collective-permute-start(bf16[32,2048]{1,0:T(8,128)(2,1)S(1)} %get-tuple-element.103), channel_id=1, source_target_pairs={{4,0},{5,1},{8,4},{9,5},{12,8},{13,9},{14,12},{15,13},{10,14},{11,... | collective-permute-start | bytes 393224 | tf_op jit(solution)/shard_map/ppermute | solution.py:237
  67.1 2.2 %collective-permute-done.17 = bf16[32,2048]{1,0:T(8,128)(2,1)S(1)} collective-permute-done((bf16[32,2048]{1,0:T(8,128)(2,1)S(1)}, bf16[32,2048]{1,0:T(8,128)(2,1)S(1)}, u32[]{:S(2)}, u32[]{:S(2)}) %collective-permute-start.17) | collective-permute-done | bytes 131104 | tf_op jit(solution)/shard_map/ppermute | solution.py:237
  69.4 1.6 %collective-permute-start.18 = (bf16[64,2048]{1,0:T(8,128)(2,1)S(1)}, bf16[64,2048]{1,0:T(8,128)(2,1)S(1)}, u32[]{:S(2)}, u32[]{:S(2)}) collective-permute-start(bf16[64,2048]{1,0:T(8,128)(2,1)S(1)} %pad_maximum_fusion.2), channel_id=1, source_target_pairs={{4,0},{5,1},{8,4},{9,5},{12,8},{13,9},{14,12},{15,13},{10,14},{11,... | collective-permute-start | bytes 786440 | tf_op jit(solution)/shard_map/ppermute | solution.py:237
  72.2 1.6 %collective-permute-start.28 = (bf16[64,2048]{1,0:T(8,128)(2,1)S(1)}, bf16[64,2048]{1,0:T(8,128)(2,1)S(1)}, u32[]{:S(2)}, u32[]{:S(2)}) collective-permute-start(bf16[64,2048]{1,0:T(8,128)(2,1)S(1)} %pad_maximum_fusion.4), channel_id=1, source_target_pairs={{4,0},{5,1},{8,4},{9,5},{12,8},{13,9},{14,12},{15,13},{10,14},{11,... | collective-permute-start | bytes 786440 | tf_op jit(solution)/shard_map/ppermute | solution.py:237
  74.5 4.3 %collective-permute-done.18 = bf16[64,2048]{1,0:T(8,128)(2,1)S(1)} collective-permute-done((bf16[64,2048]{1,0:T(8,128)(2,1)S(1)}, bf16[64,2048]{1,0:T(8,128)(2,1)S(1)}, u32[]{:S(2)}, u32[]{:S(2)}) %collective-permute-start.18) | collective-permute-done | bytes 262176 | tf_op jit(solution)/shard_map/ppermute | solution.py:237
  78.8 1.6 %collective-permute-start.19 = (bf16[64,2048]{1,0:T(8,128)(2,1)S(1)}, bf16[64,2048]{1,0:T(8,128)(2,1)S(1)}, u32[]{:S(2)}, u32[]{:S(2)}) collective-permute-start(bf16[64,2048]{1,0:T(8,128)(2,1)S(1)} %add_convert_fusion.7), channel_id=1, source_target_pairs={{4,0},{5,1},{8,4},{9,5},{12,8},{13,9},{14,12},{15,13},{10,14},{11,... | collective-permute-start | bytes 786440 | tf_op jit(solution)/shard_map/ppermute | solution.py:237
  81.0 3.3 %collective-permute-done.28 = bf16[64,2048]{1,0:T(8,128)(2,1)S(1)} collective-permute-done((bf16[64,2048]{1,0:T(8,128)(2,1)S(1)}, bf16[64,2048]{1,0:T(8,128)(2,1)S(1)}, u32[]{:S(2)}, u32[]{:S(2)}) %collective-permute-start.28) | collective-permute-done | bytes 262176 | tf_op jit(solution)/shard_map/ppermute | solution.py:237
  84.4 1.6 %collective-permute-start.29 = (bf16[64,2048]{1,0:T(8,128)(2,1)S(1)}, bf16[64,2048]{1,0:T(8,128)(2,1)S(1)}, u32[]{:S(2)}, u32[]{:S(2)}) collective-permute-start(bf16[64,2048]{1,0:T(8,128)(2,1)S(1)} %add_convert_fusion.3), channel_id=1, source_target_pairs={{4,0},{5,1},{8,4},{9,5},{12,8},{13,9},{14,12},{15,13},{10,14},{11,... | collective-permute-start | bytes 786440 | tf_op jit(solution)/shard_map/ppermute | solution.py:237
  86.6 3.3 %collective-permute-done.19 = bf16[64,2048]{1,0:T(8,128)(2,1)S(1)} collective-permute-done((bf16[64,2048]{1,0:T(8,128)(2,1)S(1)}, bf16[64,2048]{1,0:T(8,128)(2,1)S(1)}, u32[]{:S(2)}, u32[]{:S(2)}) %collective-permute-start.19) | collective-permute-done | bytes 262176 | tf_op jit(solution)/shard_map/ppermute | solution.py:237
  90.0 1.6 %collective-permute-start.20 = (bf16[64,2048]{1,0:T(8,128)(2,1)S(1)}, bf16[64,2048]{1,0:T(8,128)(2,1)S(1)}, u32[]{:S(2)}, u32[]{:S(2)}) collective-permute-start(bf16[64,2048]{1,0:T(8,128)(2,1)S(1)} %add_convert_fusion.6), channel_id=1, source_target_pairs={{4,0},{5,1},{8,4},{9,5},{12,8},{13,9},{14,12},{15,13},{10,14},{11,... | collective-permute-start | bytes 786440 | tf_op jit(solution)/shard_map/ppermute | solution.py:237
  92.2 3.3 %collective-permute-done.29 = bf16[64,2048]{1,0:T(8,128)(2,1)S(1)} collective-permute-done((bf16[64,2048]{1,0:T(8,128)(2,1)S(1)}, bf16[64,2048]{1,0:T(8,128)(2,1)S(1)}, u32[]{:S(2)}, u32[]{:S(2)}) %collective-permute-start.29) | collective-permute-done | bytes 262176 | tf_op jit(solution)/shard_map/ppermute | solution.py:237
  95.7 1.6 %collective-permute-start.30 = (bf16[64,2048]{1,0:T(8,128)(2,1)S(1)}, bf16[64,2048]{1,0:T(8,128)(2,1)S(1)}, u32[]{:S(2)}, u32[]{:S(2)}) collective-permute-start(bf16[64,2048]{1,0:T(8,128)(2,1)S(1)} %add_convert_fusion.2), channel_id=1, source_target_pairs={{4,0},{5,1},{8,4},{9,5},{12,8},{13,9},{14,12},{15,13},{10,14},{11,... | collective-permute-start | bytes 786440 | tf_op jit(solution)/shard_map/ppermute | solution.py:237
  97.9 2.2 %collective-permute-done.20 = bf16[64,2048]{1,0:T(8,128)(2,1)S(1)} collective-permute-done((bf16[64,2048]{1,0:T(8,128)(2,1)S(1)}, bf16[64,2048]{1,0:T(8,128)(2,1)S(1)}, u32[]{:S(2)}, u32[]{:S(2)}) %collective-permute-start.20) | collective-permute-done | bytes 262176 | tf_op jit(solution)/shard_map/ppermute | solution.py:237
  100.1 1.4 %collective-permute-done.26 = bf16[64,2048]{1,0:T(8,128)(2,1)S(1)} collective-permute-done((bf16[64,2048]{1,0:T(8,128)(2,1)S(1)}, bf16[64,2048]{1,0:T(8,128)(2,1)S(1)}, u32[]{:S(2)}, u32[]{:S(2)}) %collective-permute-start.26) | collective-permute-done | bytes 262176 | tf_op jit(solution)/shard_map/ppermute | solution.py:237
  102.9 1.4 %collective-permute-done.34 = bf16[64,2048]{1,0:T(8,128)(2,1)S(1)} collective-permute-done((bf16[64,2048]{1,0:T(8,128)(2,1)S(1)}, bf16[64,2048]{1,0:T(8,128)(2,1)S(1)}, u32[]{:S(2)}, u32[]{:S(2)}) %collective-permute-start.34) | collective-permute-done | bytes 262176 | tf_op jit(solution)/shard_map/ppermute | solution.py:237
  (109 shorter events, 24.0 us)
Async XLA Ops:
  0.0 8.2 %collective-permute-start.6 = (bf16[2048,768]{1,0:T(8,128)(2,1)}, bf16[2048,768]{1,0:T(8,128)(2,1)}, u32[]{:S(2)}, u32[]{:S(2)}) collective-permute-start(bf16[2048,768]{1,0:T(8,128)(2,1)} %bitcast.31), channel_id=1, source_target_pairs={{0,1},{1,0},{2,3},{3,2},{4,5},{5,4},{6,7},{7,6},{8,9},{9,8},{10,11... | collective-permute-start | bytes 9437192 | tf_op jit(solution)/shard_map/ppermute | solution.py:240
  2.4 9.6 %collective-permute-start.3 = (bf16[64,2048]{1,0:T(8,128)(2,1)S(1)}, bf16[64,2048]{1,0:T(8,128)(2,1)S(1)}, u32[]{:S(2)}, u32[]{:S(2)}) collective-permute-start(bf16[64,2048]{1,0:T(8,128)(2,1)S(1)} %get-tuple-element.99), channel_id=1, source_target_pairs={{0,16},{16,0},{1,17},{17,1},{2,18},{18,2},{3,19},{19,3},{4,20},{20... | collective-permute-start | bytes 786440 | tf_op jit(solution)/shard_map/ppermute | solution.py:247
  4.9 12.4 %collective-permute-start = (bf16[64,2048]{1,0:T(8,128)(2,1)}, bf16[64,2048]{1,0:T(8,128)(2,1)S(1)}, u32[]{:S(2)}, u32[]{:S(2)}) collective-permute-start(bf16[64,2048]{1,0:T(8,128)(2,1)} %get-tuple-element.100), channel_id=1, source_target_pairs={{0,16},{16,0},{1,17},{17,1},{2,18},{18,2},{3,19},{19,3},{4,20},{20... | collective-permute-start | bytes 786440 | tf_op jit(solution)/shard_map/ppermute | solution.py:247
  4.9 15.2 %collective-permute-start.8 = (bf16[768,2048]{1,0:T(8,128)(2,1)}, bf16[768,2048]{1,0:T(8,128)(2,1)}, u32[]{:S(2)}, u32[]{:S(2)}) collective-permute-start(bf16[768,2048]{1,0:T(8,128)(2,1)} %bitcast.35), channel_id=1, source_target_pairs={{0,1},{1,0},{2,3},{3,2},{4,5},{5,4},{6,7},{7,6},{8,9},{9,8},{10,11... | collective-permute-start | bytes 9437192 | tf_op jit(solution)/shard_map/ppermute | solution.py:240
  8.2 12.1 %collective-permute-start.7 = (bf16[2048,768]{1,0:T(8,128)(2,1)}, bf16[2048,768]{1,0:T(8,128)(2,1)}, u32[]{:S(2)}, u32[]{:S(2)}) collective-permute-start(bf16[2048,768]{1,0:T(8,128)(2,1)} %bitcast.33), channel_id=1, source_target_pairs={{0,1},{1,0},{2,3},{3,2},{4,5},{5,4},{6,7},{7,6},{8,9},{9,8},{10,11... | collective-permute-start | bytes 9437192 | tf_op jit(solution)/shard_map/ppermute | solution.py:240
  12.4 14.4 %collective-permute-start.4 = (bf16[64,2176]{1,0:T(8,128)(2,1)S(1)}, bf16[64,2176]{1,0:T(8,128)(2,1)S(1)}, u32[]{:S(2)}, u32[]{:S(2)}) collective-permute-start(bf16[64,2176]{1,0:T(8,128)(2,1)S(1)} %pad_maximum_fusion.1.refs_5_), channel_id=1, source_target_pairs={{4,8},{5,9},{8,12},{9,13},{12,14},{13,15},{14,10},{15,11},{10,6},{... | collective-permute-start | bytes 835592 | tf_op jit(solution)/shard_map/ppermute | solution.py:237
  14.5 12.3 %collective-permute-start.5 = (bf16[64,2176]{1,0:T(8,128)(2,1)S(1)}, bf16[64,2176]{1,0:T(8,128)(2,1)S(1)}, u32[]{:S(2)}, u32[]{:S(2)}) collective-permute-start(bf16[64,2176]{1,0:T(8,128)(2,1)S(1)} %pad_maximum_fusion.1.refs_5_), channel_id=1, source_target_pairs={{4,0},{5,1},{8,4},{9,5},{12,8},{13,9},{14,12},{15,13},{10,14},{11,... | collective-permute-start | bytes 835592 | tf_op jit(solution)/shard_map/ppermute | solution.py:237
  18.2 8.6 %collective-permute-start.1 = (bf16[64,2176]{1,0:T(8,128)(2,1)S(1)}, bf16[64,2176]{1,0:T(8,128)(2,1)}, u32[]{:S(2)}, u32[]{:S(2)}) collective-permute-start(bf16[64,2176]{1,0:T(8,128)(2,1)S(1)} %pad_maximum_fusion.refs_4_), channel_id=1, source_target_pairs={{4,8},{5,9},{8,12},{9,13},{12,14},{13,15},{14,10},{15,11},{10,6},{... | collective-permute-start | bytes 835592 | tf_op jit(solution)/shard_map/ppermute | solution.py:237
  20.1 7.8 %collective-permute-start.2 = (bf16[64,2176]{1,0:T(8,128)(2,1)S(1)}, bf16[64,2176]{1,0:T(8,128)(2,1)S(1)}, u32[]{:S(2)}, u32[]{:S(2)}) collective-permute-start(bf16[64,2176]{1,0:T(8,128)(2,1)S(1)} %pad_maximum_fusion.refs_4_), channel_id=1, source_target_pairs={{4,0},{5,1},{8,4},{9,5},{12,8},{13,9},{14,12},{15,13},{10,14},{11,... | collective-permute-start | bytes 835592 | tf_op jit(solution)/shard_map/ppermute | solution.py:237
  27.9 10.8 %collective-permute-start.10 = (bf16[64,2176]{1,0:T(8,128)(2,1)S(1)}, bf16[64,2176]{1,0:T(8,128)(2,1)S(1)}, u32[]{:S(2)}, u32[]{:S(2)}) collective-permute-start(bf16[64,2176]{1,0:T(8,128)(2,1)S(1)} %collective-permute-done.5.refs_3_), channel_id=1, source_target_pairs={{4,0},{5,1},{8,4},{9,5},{12,8},{13,9},{14,12},{15,13},{10,14},{11,... | collective-permute-start | bytes 835592 | tf_op jit(solution)/shard_map/ppermute | solution.py:237
  28.7 10.1 %collective-permute-start.9 = (bf16[64,2176]{1,0:T(8,128)(2,1)S(1)}, bf16[64,2176]{1,0:T(8,128)(2,1)S(1)}, u32[]{:S(2)}, u32[]{:S(2)}) collective-permute-start(bf16[64,2176]{1,0:T(8,128)(2,1)S(1)} %collective-permute-done.4.refs_2_), channel_id=1, source_target_pairs={{4,8},{5,9},{8,12},{9,13},{12,14},{13,15},{14,10},{15,11},{10,6},{... | collective-permute-start | bytes 835592 | tf_op jit(solution)/shard_map/ppermute | solution.py:237
  30.0 11.9 %collective-permute-start.11 = (bf16[64,2176]{1,0:T(8,128)(2,1)}, bf16[64,2176]{1,0:T(8,128)(2,1)S(1)}, u32[]{:S(2)}, u32[]{:S(2)}) collective-permute-start(bf16[64,2176]{1,0:T(8,128)(2,1)} %collective-permute-done.1.refs_0_), channel_id=1, source_target_pairs={{4,8},{5,9},{8,12},{9,13},{12,14},{13,15},{14,10},{15,11},{10,6},{... | collective-permute-start | bytes 835592 | tf_op jit(solution)/shard_map/ppermute | solution.py:237
  31.5 12.8 %collective-permute-start.15 = (bf16[64,2176]{1,0:T(8,128)(2,1)S(1)}, bf16[64,2176]{1,0:T(8,128)(2,1)S(1)}, u32[]{:S(2)}, u32[]{:S(2)}) collective-permute-start(bf16[64,2176]{1,0:T(8,128)(2,1)S(1)} %collective-permute-done.2.refs_1_), channel_id=1, source_target_pairs={{4,0},{5,1},{8,4},{9,5},{12,8},{13,9},{14,12},{15,13},{10,14},{11,... | collective-permute-start | bytes 835592 | tf_op jit(solution)/shard_map/ppermute | solution.py:237
  38.7 10.2 %collective-permute-start.14 = (bf16[64,2176]{1,0:T(8,128)(2,1)S(1)}, bf16[64,2176]{1,0:T(8,128)(2,1)S(1)}, u32[]{:S(2)}, u32[]{:S(2)}) collective-permute-start(bf16[64,2176]{1,0:T(8,128)(2,1)S(1)} %collective-permute-done.10.refs_3_), channel_id=1, source_target_pairs={{4,0},{5,1},{8,4},{9,5},{12,8},{13,9},{14,12},{15,13},{10,14},{11,... | collective-permute-start | bytes 835592 | tf_op jit(solution)/shard_map/ppermute | solution.py:237
  41.9 9.6 %collective-permute-start.12 = (bf16[64,2176]{1,0:T(8,128)(2,1)S(1)}, bf16[64,2176]{1,0:T(8,128)(2,1)S(1)}, u32[]{:S(2)}, u32[]{:S(2)}) collective-permute-start(bf16[64,2176]{1,0:T(8,128)(2,1)S(1)} %collective-permute-done.11.refs_0_), channel_id=1, source_target_pairs={{4,8},{5,9},{8,12},{9,13},{12,14},{13,15},{14,10},{15,11},{10,6},{... | collective-permute-start | bytes 835592 | tf_op jit(solution)/shard_map/ppermute | solution.py:237
  42.7 14.5 %collective-permute-start.22 = (bf16[64,2176]{1,0:T(8,128)(2,1)S(1)}, bf16[64,2176]{1,0:T(8,128)(2,1)S(1)}, u32[]{:S(2)}, u32[]{:S(2)}) collective-permute-start(bf16[64,2176]{1,0:T(8,128)(2,1)S(1)} %collective-permute-done.9.refs_2_), channel_id=1, source_target_pairs={{4,8},{5,9},{8,12},{9,13},{12,14},{13,15},{14,10},{15,11},{10,6},{... | collective-permute-start | bytes 835592 | tf_op jit(solution)/shard_map/ppermute | solution.py:237
  44.3 12.9 %collective-permute-start.21 = (bf16[64,2176]{1,0:T(8,128)(2,1)S(1)}, bf16[64,2176]{1,0:T(8,128)(2,1)S(1)}, u32[]{:S(2)}, u32[]{:S(2)}) collective-permute-start(bf16[64,2176]{1,0:T(8,128)(2,1)S(1)} %collective-permute-done.15.refs_1_), channel_id=1, source_target_pairs={{4,0},{5,1},{8,4},{9,5},{12,8},{13,9},{14,12},{15,13},{10,14},{11,... | collective-permute-start | bytes 835592 | tf_op jit(solution)/shard_map/ppermute | solution.py:237
  49.0 11.0 %collective-permute-start.16 = (bf16[64,2176]{1,0:T(8,128)(2,1)S(1)}, bf16[64,2176]{1,0:T(8,128)(2,1)S(1)}, u32[]{:S(2)}, u32[]{:S(2)}) collective-permute-start(bf16[64,2176]{1,0:T(8,128)(2,1)S(1)} %collective-permute-done.14.refs_1_), channel_id=1, source_target_pairs={{4,0},{5,1},{8,4},{9,5},{12,8},{13,9},{14,12},{15,13},{10,14},{11,... | collective-permute-start | bytes 835592 | tf_op jit(solution)/shard_map/ppermute | solution.py:237
  51.5 8.7 %collective-permute-start.13 = (bf16[64,2176]{1,0:T(8,128)(2,1)S(1)}, bf16[64,2176]{1,0:T(8,128)(2,1)S(1)}, u32[]{:S(2)}, u32[]{:S(2)}) collective-permute-start(bf16[64,2176]{1,0:T(8,128)(2,1)S(1)} %collective-permute-done.12.refs_0_), channel_id=1, source_target_pairs={{4,8},{5,9},{8,12},{9,13},{12,14},{13,15},{14,10},{15,11},{10,6},{... | collective-permute-start | bytes 835592 | tf_op jit(solution)/shard_map/ppermute | solution.py:237
  65.1 7.1 %collective-permute-start.27 = (bf16[32,2048]{1,0:T(8,128)(2,1)S(1)}, bf16[32,2048]{1,0:T(8,128)(2,1)S(1)}, u32[]{:S(2)}, u32[]{:S(2)}) collective-permute-start(bf16[32,2048]{1,0:T(8,128)(2,1)S(1)} %get-tuple-element.103), channel_id=1, source_target_pairs={{4,0},{5,1},{8,4},{9,5},{12,8},{13,9},{14,12},{15,13},{10,14},{11,... | collective-permute-start | bytes 393224 | tf_op jit(solution)/shard_map/ppermute | solution.py:237
  66.7 7.2 %collective-permute-start.31 = (bf16[32,2048]{1,0:T(8,128)(2,1)S(1)}, bf16[32,2048]{1,0:T(8,128)(2,1)S(1)}, u32[]{:S(2)}, u32[]{:S(2)}) collective-permute-start(bf16[32,2048]{1,0:T(8,128)(2,1)S(1)} %get-tuple-element.104), channel_id=1, source_target_pairs={{4,8},{5,9},{8,12},{9,13},{12,14},{13,15},{14,10},{15,11},{10,6},{... | collective-permute-start | bytes 393224 | tf_op jit(solution)/shard_map/ppermute | solution.py:237
  69.4 9.3 %collective-permute-start.18 = (bf16[64,2048]{1,0:T(8,128)(2,1)S(1)}, bf16[64,2048]{1,0:T(8,128)(2,1)S(1)}, u32[]{:S(2)}, u32[]{:S(2)}) collective-permute-start(bf16[64,2048]{1,0:T(8,128)(2,1)S(1)} %pad_maximum_fusion.2), channel_id=1, source_target_pairs={{4,0},{5,1},{8,4},{9,5},{12,8},{13,9},{14,12},{15,13},{10,14},{11,... | collective-permute-start | bytes 786440 | tf_op jit(solution)/shard_map/ppermute | solution.py:237
  71.1 9.3 %collective-permute-start.24 = (bf16[64,2048]{1,0:T(8,128)(2,1)S(1)}, bf16[64,2048]{1,0:T(8,128)(2,1)S(1)}, u32[]{:S(2)}, u32[]{:S(2)}) collective-permute-start(bf16[64,2048]{1,0:T(8,128)(2,1)S(1)} %pad_maximum_fusion.3), channel_id=1, source_target_pairs={{4,8},{5,9},{8,12},{9,13},{12,14},{13,15},{14,10},{15,11},{10,6},{... | collective-permute-start | bytes 786440 | tf_op jit(solution)/shard_map/ppermute | solution.py:237
  72.2 12.1 %collective-permute-start.28 = (bf16[64,2048]{1,0:T(8,128)(2,1)S(1)}, bf16[64,2048]{1,0:T(8,128)(2,1)S(1)}, u32[]{:S(2)}, u32[]{:S(2)}) collective-permute-start(bf16[64,2048]{1,0:T(8,128)(2,1)S(1)} %pad_maximum_fusion.4), channel_id=1, source_target_pairs={{4,0},{5,1},{8,4},{9,5},{12,8},{13,9},{14,12},{15,13},{10,14},{11,... | collective-permute-start | bytes 786440 | tf_op jit(solution)/shard_map/ppermute | solution.py:237
  73.9 12.1 %collective-permute-start.32 = (bf16[64,2048]{1,0:T(8,128)(2,1)S(1)}, bf16[64,2048]{1,0:T(8,128)(2,1)S(1)}, u32[]{:S(2)}, u32[]{:S(2)}) collective-permute-start(bf16[64,2048]{1,0:T(8,128)(2,1)S(1)} %pad_maximum_fusion.5), channel_id=1, source_target_pairs={{4,8},{5,9},{8,12},{9,13},{12,14},{13,15},{14,10},{15,11},{10,6},{... | collective-permute-start | bytes 786440 | tf_op jit(solution)/shard_map/ppermute | solution.py:237
  78.8 11.2 %collective-permute-start.19 = (bf16[64,2048]{1,0:T(8,128)(2,1)S(1)}, bf16[64,2048]{1,0:T(8,128)(2,1)S(1)}, u32[]{:S(2)}, u32[]{:S(2)}) collective-permute-start(bf16[64,2048]{1,0:T(8,128)(2,1)S(1)} %add_convert_fusion.7), channel_id=1, source_target_pairs={{4,0},{5,1},{8,4},{9,5},{12,8},{13,9},{14,12},{15,13},{10,14},{11,... | collective-permute-start | bytes 786440 | tf_op jit(solution)/shard_map/ppermute | solution.py:237
  80.5 11.2 %collective-permute-start.25 = (bf16[64,2048]{1,0:T(8,128)(2,1)S(1)}, bf16[64,2048]{1,0:T(8,128)(2,1)S(1)}, u32[]{:S(2)}, u32[]{:S(2)}) collective-permute-start(bf16[64,2048]{1,0:T(8,128)(2,1)S(1)} %add_convert_fusion.5), channel_id=1, source_target_pairs={{4,8},{5,9},{8,12},{9,13},{12,14},{13,15},{14,10},{15,11},{10,6},{... | collective-permute-start | bytes 786440 | tf_op jit(solution)/shard_map/ppermute | solution.py:237
  84.4 11.2 %collective-permute-start.29 = (bf16[64,2048]{1,0:T(8,128)(2,1)S(1)}, bf16[64,2048]{1,0:T(8,128)(2,1)S(1)}, u32[]{:S(2)}, u32[]{:S(2)}) collective-permute-start(bf16[64,2048]{1,0:T(8,128)(2,1)S(1)} %add_convert_fusion.3), channel_id=1, source_target_pairs={{4,0},{5,1},{8,4},{9,5},{12,8},{13,9},{14,12},{15,13},{10,14},{11,... | collective-permute-start | bytes 786440 | tf_op jit(solution)/shard_map/ppermute | solution.py:237
  86.1 11.2 %collective-permute-start.33 = (bf16[64,2048]{1,0:T(8,128)(2,1)S(1)}, bf16[64,2048]{1,0:T(8,128)(2,1)S(1)}, u32[]{:S(2)}, u32[]{:S(2)}) collective-permute-start(bf16[64,2048]{1,0:T(8,128)(2,1)S(1)} %add_convert_fusion.1), channel_id=1, source_target_pairs={{4,8},{5,9},{8,12},{9,13},{12,14},{13,15},{14,10},{15,11},{10,6},{... | collective-permute-start | bytes 786440 | tf_op jit(solution)/shard_map/ppermute | solution.py:237
  90.0 10.1 %collective-permute-start.20 = (bf16[64,2048]{1,0:T(8,128)(2,1)S(1)}, bf16[64,2048]{1,0:T(8,128)(2,1)S(1)}, u32[]{:S(2)}, u32[]{:S(2)}) collective-permute-start(bf16[64,2048]{1,0:T(8,128)(2,1)S(1)} %add_convert_fusion.6), channel_id=1, source_target_pairs={{4,0},{5,1},{8,4},{9,5},{12,8},{13,9},{14,12},{15,13},{10,14},{11,... | collective-permute-start | bytes 786440 | tf_op jit(solution)/shard_map/ppermute | solution.py:237
  91.7 9.8 %collective-permute-start.26 = (bf16[64,2048]{1,0:T(8,128)(2,1)S(1)}, bf16[64,2048]{1,0:T(8,128)(2,1)S(1)}, u32[]{:S(2)}, u32[]{:S(2)}) collective-permute-start(bf16[64,2048]{1,0:T(8,128)(2,1)S(1)} %add_convert_fusion.4), channel_id=1, source_target_pairs={{4,8},{5,9},{8,12},{9,13},{12,14},{13,15},{14,10},{15,11},{10,6},{... | collective-permute-start | bytes 786440 | tf_op jit(solution)/shard_map/ppermute | solution.py:237
  95.7 7.3 %collective-permute-start.30 = (bf16[64,2048]{1,0:T(8,128)(2,1)S(1)}, bf16[64,2048]{1,0:T(8,128)(2,1)S(1)}, u32[]{:S(2)}, u32[]{:S(2)}) collective-permute-start(bf16[64,2048]{1,0:T(8,128)(2,1)S(1)} %add_convert_fusion.2), channel_id=1, source_target_pairs={{4,0},{5,1},{8,4},{9,5},{12,8},{13,9},{14,12},{15,13},{10,14},{11,... | collective-permute-start | bytes 786440 | tf_op jit(solution)/shard_map/ppermute | solution.py:237
  (8 other events, 88.8 us)

commit v5 on v4

--- a/solution.py
+++ b/solution.py
@@ -12,7 +12,7 @@
 CORES = 2
 LANES = 128
 FF_CHUNK = 256
-OUT_CHUNK = 512
+OUT_CHUNK = 2048
 CHUNK_BLOCKS = 4
 VMEM_GRANT = 16 << 20
 

time: 106 us -> 106 us (level)
  transfers between devices with their start and end apart: 35 -> 35, of which waited for: 18 -> 18; matrix products, arithmetic and copies ran while one was open for 7% -> 7% of each run, Pallas kernels for 22% -> 21%
where the time goes in v5:
time: 106 us; the launch traced here: 105 us
  waiting for transfers between devices  36.7 us (35%)
  starting transfers between devices  34.5 us (33%)
  Pallas kernels  24.5 us (23%)
  local copies, waits for them, and re-layouts  4.46 us (4%)
  other arithmetic  3.84 us (4%)
    ppermute x30, waiting for transfers between devices, hop(): return lax.ppermute(value, 'expert', pairs)  31.5 us
    ppermute x30, starting transfers between devices, hop(): return lax.ppermute(value, 'expert', pairs)  31 us
    pallas_call x5, Pallas kernels, group_sums(): pl.pallas_call(kernel, out_shape=[pltpu.VMEM((size, features), jnp.bfloat...  18 us
    pallas_call x1, Pallas kernels, in_vmem(): pl.pallas_call(load_kernel, out_shape=[pltpu.VMEM(value.shape, value.dtyp...  6.49 us
    ppermute x2, waiting for transfers between devices, shards(): lax.ppermute(emitted[0, b], 'section', around)  5.13 us
    ppermute x2, starting transfers between devices, shards(): lax.ppermute(emitted[0, b], 'section', around)  2.5 us
  transfers between devices with their start and end apart: 35, of which 18 were waited for; matrix products, arithmetic and copies ran while one was open for 7% of the time, Pallas kernels for 21%

profile of v5, /device:TPU:0, one launch (start us, length us, event | category | flops | bytes accessed | tf_op | source)
XLA Modules:
  0.0 105.3 jit_solution(11138341041383873957)
XLA Ops:
  0.5 1.9 %slice_bitcast_fusion = (bf16[64,2048]{1,0:T(8,128)(2,1)S(1)}, bf16[64,2048]{1,0:T(8,128)(2,1)}) fusion(bf16[1,2,64,2048]{3,2,1,0:T(8,128)(2,1)} %param.8), kind=kLoop, calls=%fused_computation.47 | loop fusion | bytes 1048576 | tf_op jit(solution)/shard_map/squeeze | solution.py:247
  2.4 2.5 %collective-permute-start.3 = (bf16[64,2048]{1,0:T(8,128)(2,1)S(1)}, bf16[64,2048]{1,0:T(8,128)(2,1)S(1)}, u32[]{:S(2)}, u32[]{:S(2)}) collective-permute-start(bf16[64,2048]{1,0:T(8,128)(2,1)S(1)} %get-tuple-element.99), channel_id=1, source_target_pairs={{0,16},{16,0},{1,17},{17,1},{2,18},{18,2},{3,19},{19,3},{4,20},{20... | collective-permute-start | bytes 786440 | tf_op jit(solution)/shard_map/ppermute | solution.py:247
  9.7 2.3 %collective-permute-done.3 = bf16[64,2048]{1,0:T(8,128)(2,1)S(1)} collective-permute-done((bf16[64,2048]{1,0:T(8,128)(2,1)S(1)}, bf16[64,2048]{1,0:T(8,128)(2,1)S(1)}, u32[]{:S(2)}, u32[]{:S(2)}) %collective-permute-start.3) | collective-permute-done | bytes 262176 | tf_op jit(solution)/shard_map/ppermute | solution.py:247
  12.4 2.1 %collective-permute-start.4 = (bf16[64,2176]{1,0:T(8,128)(2,1)S(1)}, bf16[64,2176]{1,0:T(8,128)(2,1)S(1)}, u32[]{:S(2)}, u32[]{:S(2)}) collective-permute-start(bf16[64,2176]{1,0:T(8,128)(2,1)S(1)} %pad_maximum_fusion.1.refs_5_), channel_id=1, source_target_pairs={{4,8},{5,9},{8,12},{9,13},{12,14},{13,15},{14,10},{15,11},{10,6},{... | collective-permute-start | bytes 835592 | tf_op jit(solution)/shard_map/ppermute | solution.py:237
  14.5 2.8 %collective-permute-done = bf16[64,2048]{1,0:T(8,128)(2,1)S(1)} collective-permute-done((bf16[64,2048]{1,0:T(8,128)(2,1)}, bf16[64,2048]{1,0:T(8,128)(2,1)S(1)}, u32[]{:S(2)}, u32[]{:S(2)}) %collective-permute-start) | collective-permute-done | bytes 262176 | tf_op jit(solution)/shard_map/ppermute | solution.py:247
  18.2 1.9 %collective-permute-start.1 = (bf16[64,2176]{1,0:T(8,128)(2,1)S(1)}, bf16[64,2176]{1,0:T(8,128)(2,1)}, u32[]{:S(2)}, u32[]{:S(2)}) collective-permute-start(bf16[64,2176]{1,0:T(8,128)(2,1)S(1)} %pad_maximum_fusion.refs_4_), channel_id=1, source_target_pairs={{4,8},{5,9},{8,12},{9,13},{12,14},{13,15},{14,10},{15,11},{10,6},{... | collective-permute-start | bytes 835592 | tf_op jit(solution)/shard_map/ppermute | solution.py:237
  20.3 6.5 %shard_map.82 = (bf16[2048,768]{1,0:T(8,128)(2,1)S(1)}, bf16[2048,768]{1,0:T(8,128)(2,1)S(1)}, bf16[768,2048]{1,0:T(8,128)(2,1)S(1)}, bf16[2048,768]{1,0:T(8,128...) custom-call(bf16[2048,768]{1,0:T(8,128)(2,1)} %bitcast.32, bf16[2048,768]{1,0:T(8,128)(2,1)} %bitcast.34, ...), custom_call_target="tpu_custom_call" | custom-call | tf_op jit(solution)/shard_map/pallas_call | solution.py:175
  30.0 1.6 %collective-permute-start.11 = (bf16[64,2176]{1,0:T(8,128)(2,1)}, bf16[64,2176]{1,0:T(8,128)(2,1)S(1)}, u32[]{:S(2)}, u32[]{:S(2)}) collective-permute-start(bf16[64,2176]{1,0:T(8,128)(2,1)} %collective-permute-done.1.refs_0_), channel_id=1, source_target_pairs={{4,8},{5,9},{8,12},{9,13},{12,14},{13,15},{14,10},{15,11},{10,6},{... | collective-permute-start | bytes 835592 | tf_op jit(solution)/shard_map/ppermute | solution.py:237
  32.0 6.3 %shard_map.83 = (bf16[64,2048]{1,0:T(8,128)(2,1)S(1)}, bf16[64,2048]{1,0:T(8,128)(2,1)S(1)}, bf16[64,2048]{1,0:T(8,128)(2,1)S(1)}, bf16[64,2048]{1,0:T(8,128)(2,...) custom-call(s32[1]{0:T(128)} %bitcast.12.me_ref, bf16[64,2176]{1,0:T(8,128)(2,1)} %collective-permute-done.1.refs_0_, ...), custom_call_target="tpu_custom_call" | custom-call | flops 3623878656 | bytes 3145728 | tf_op jit(solution)/shard_map/pallas_call | solution.py:210
  38.3 1.5 %collective-permute-start.14 = (bf16[64,2176]{1,0:T(8,128)(2,1)S(1)}, bf16[64,2176]{1,0:T(8,128)(2,1)S(1)}, u32[]{:S(2)}, u32[]{:S(2)}) collective-permute-start(bf16[64,2176]{1,0:T(8,128)(2,1)S(1)} %collective-permute-done.10.refs_3_), channel_id=1, source_target_pairs={{4,0},{5,1},{8,4},{9,5},{12,8},{13,9},{14,12},{15,13},{10,14},{11,... | collective-permute-start | bytes 835592 | tf_op jit(solution)/shard_map/ppermute | solution.py:237
  39.8 2.1 %collective-permute-done.11.refs_0_ = bf16[64,2176]{1,0:T(8,128)(2,1)S(1)} collective-permute-done((bf16[64,2176]{1,0:T(8,128)(2,1)}, bf16[64,2176]{1,0:T(8,128)(2,1)S(1)}, u32[]{:S(2)}, u32[]{:S(2)}) %collective-permute-start.11) | collective-permute-done | bytes 278560 | tf_op jit(solution)/shard_map/ppermute | solution.py:237
  42.7 1.6 %collective-permute-start.22 = (bf16[64,2176]{1,0:T(8,128)(2,1)S(1)}, bf16[64,2176]{1,0:T(8,128)(2,1)S(1)}, u32[]{:S(2)}, u32[]{:S(2)}) collective-permute-start(bf16[64,2176]{1,0:T(8,128)(2,1)S(1)} %collective-permute-done.9.refs_2_), channel_id=1, source_target_pairs={{4,8},{5,9},{8,12},{9,13},{12,14},{13,15},{14,10},{15,11},{10,6},{... | collective-permute-start | bytes 835592 | tf_op jit(solution)/shard_map/ppermute | solution.py:237
  44.7 3.5 %shard_map.84 = (bf16[64,2048]{1,0:T(8,128)(2,1)S(1)}, bf16[64,2048]{1,0:T(8,128)(2,1)S(1)}, bf16[64,2048]{1,0:T(8,128)(2,1)S(1)}, bf16[64,2048]{1,0:T(8,128)(2,1)S(1)}) custom-call(s32[1]{0:T(128)} %bitcast.12.me_ref, bf16[64,2176]{1,0:T(8,128)(2,1)S(1)} %collective-permute-done.11.refs_0_, bf16[64,2176]{1,0:T(8,128)(2,1)S(1)} %collective-permute-done.15.refs_1_, ...), custom_call_target="tpu_custom_call" | custom-call | flops 2415919104 | bytes 2097152 | tf_op jit(solution)/shard_map/pallas_call | solution.py:210
  52.3 2.7 %shard_map.86 = (bf16[64,2048]{1,0:T(8,128)(2,1)S(1)}, bf16[64,2048]{1,0:T(8,128)(2,1)S(1)}) custom-call(s32[1]{0:T(128)} %bitcast.12.me_ref, bf16[64,2176]{1,0:T(8,128)(2,1)S(1)} %collective-permute-done.12.refs_0_, bf16[64,2176]{1,0:T(8,128)(2,1)S(1)} %collective-permute-done.14.refs_1_, bf16[2048,768]{1,0:T(8,128)(2,1)S(1)} %get-tuple-element.64.refs_6_.refs_4_.refs_2_, ...), custom_call_target="tpu_custom_call" | custom-call | flops 2415919104 | bytes 1048576 | tf_op jit(solution)/shard_map/pallas_call | solution.py:210
  55.0 2.2 %collective-permute-done.22.refs_1_ = bf16[64,2176]{1,0:T(8,128)(2,1)S(1)} collective-permute-done((bf16[64,2176]{1,0:T(8,128)(2,1)S(1)}, bf16[64,2176]{1,0:T(8,128)(2,1)S(1)}, u32[]{:S(2)}, u32[]{:S(2)}) %collective-permute-start.22) | collective-permute-done | bytes 278560 | tf_op jit(solution)/shard_map/ppermute | solution.py:237
  57.2 2.7 %shard_map.87 = (bf16[64,2048]{1,0:T(8,128)(2,1)S(1)}, bf16[64,2048]{1,0:T(8,128)(2,1)S(1)}) custom-call(s32[1]{0:T(128)} %bitcast.12.me_ref, bf16[64,2176]{1,0:T(8,128)(2,1)S(1)} %collective-permute-done.21.refs_0_, bf16[64,2176]{1,0:T(8,128)(2,1)S(1)} %collective-permute-done.22.refs_1_, bf16[2048,768]{1,0:T(8,128)(2,1)S(1)} %get-tuple-element.64.refs_6_.refs_4_.refs_2_, ...), custom_call_target="tpu_custom_call" | custom-call | flops 2415919104 | bytes 1048576 | tf_op jit(solution)/shard_map/pallas_call | solution.py:210
  60.2 2.7 %shard_map.85 = (bf16[64,2048]{1,0:T(8,128)(2,1)S(1)}, bf16[64,2048]{1,0:T(8,128)(2,1)S(1)}) custom-call(s32[1]{0:T(128)} %bitcast.12.me_ref, bf16[64,2176]{1,0:T(8,128)(2,1)S(1)} %collective-permute-done.13.refs_0_, bf16[64,2176]{1,0:T(8,128)(2,1)S(1)} %collective-permute-done.16.refs_1_, bf16[2048,768]{1,0:T(8,128)(2,1)S(1)} %get-tuple-element.64.refs_6_.refs_4_.refs_2_, ...), custom_call_target="tpu_custom_call" | custom-call | flops 2415919104 | bytes 1048576 | tf_op jit(solution)/shard_map/pallas_call | solution.py:210
  63.0 1.6 %collective-permute-start.17 = (bf16[32,2048]{1,0:T(8,128)(2,1)S(1)}, bf16[32,2048]{1,0:T(8,128)(2,1)S(1)}, u32[]{:S(2)}, u32[]{:S(2)}) collective-permute-start(bf16[32,2048]{1,0:T(8,128)(2,1)S(1)} %get-tuple-element.101), channel_id=1, source_target_pairs={{4,0},{5,1},{8,4},{9,5},{12,8},{13,9},{14,12},{15,13},{10,14},{11,... | collective-permute-start | bytes 393224 | tf_op jit(solution)/shard_map/ppermute | solution.py:237
  65.0 1.6 %collective-permute-start.27 = (bf16[32,2048]{1,0:T(8,128)(2,1)S(1)}, bf16[32,2048]{1,0:T(8,128)(2,1)S(1)}, u32[]{:S(2)}, u32[]{:S(2)}) collective-permute-start(bf16[32,2048]{1,0:T(8,128)(2,1)S(1)} %get-tuple-element.103), channel_id=1, source_target_pairs={{4,0},{5,1},{8,4},{9,5},{12,8},{13,9},{14,12},{15,13},{10,14},{11,... | collective-permute-start | bytes 393224 | tf_op jit(solution)/shard_map/ppermute | solution.py:237
  67.1 2.2 %collective-permute-done.17 = bf16[32,2048]{1,0:T(8,128)(2,1)S(1)} collective-permute-done((bf16[32,2048]{1,0:T(8,128)(2,1)S(1)}, bf16[32,2048]{1,0:T(8,128)(2,1)S(1)}, u32[]{:S(2)}, u32[]{:S(2)}) %collective-permute-start.17) | collective-permute-done | bytes 131104 | tf_op jit(solution)/shard_map/ppermute | solution.py:237
  69.4 1.6 %collective-permute-start.18 = (bf16[64,2048]{1,0:T(8,128)(2,1)S(1)}, bf16[64,2048]{1,0:T(8,128)(2,1)S(1)}, u32[]{:S(2)}, u32[]{:S(2)}) collective-permute-start(bf16[64,2048]{1,0:T(8,128)(2,1)S(1)} %pad_maximum_fusion.2), channel_id=1, source_target_pairs={{4,0},{5,1},{8,4},{9,5},{12,8},{13,9},{14,12},{15,13},{10,14},{11,... | collective-permute-start | bytes 786440 | tf_op jit(solution)/shard_map/ppermute | solution.py:237
  72.2 1.6 %collective-permute-start.28 = (bf16[64,2048]{1,0:T(8,128)(2,1)S(1)}, bf16[64,2048]{1,0:T(8,128)(2,1)S(1)}, u32[]{:S(2)}, u32[]{:S(2)}) collective-permute-start(bf16[64,2048]{1,0:T(8,128)(2,1)S(1)} %pad_maximum_fusion.4), channel_id=1, source_target_pairs={{4,0},{5,1},{8,4},{9,5},{12,8},{13,9},{14,12},{15,13},{10,14},{11,... | collective-permute-start | bytes 786440 | tf_op jit(solution)/shard_map/ppermute | solution.py:237
  74.5 4.3 %collective-permute-done.18 = bf16[64,2048]{1,0:T(8,128)(2,1)S(1)} collective-permute-done((bf16[64,2048]{1,0:T(8,128)(2,1)S(1)}, bf16[64,2048]{1,0:T(8,128)(2,1)S(1)}, u32[]{:S(2)}, u32[]{:S(2)}) %collective-permute-start.18) | collective-permute-done | bytes 262176 | tf_op jit(solution)/shard_map/ppermute | solution.py:237
  78.8 1.6 %collective-permute-start.19 = (bf16[64,2048]{1,0:T(8,128)(2,1)S(1)}, bf16[64,2048]{1,0:T(8,128)(2,1)S(1)}, u32[]{:S(2)}, u32[]{:S(2)}) collective-permute-start(bf16[64,2048]{1,0:T(8,128)(2,1)S(1)} %add_convert_fusion.7), channel_id=1, source_target_pairs={{4,0},{5,1},{8,4},{9,5},{12,8},{13,9},{14,12},{15,13},{10,14},{11,... | collective-permute-start | bytes 786440 | tf_op jit(solution)/shard_map/ppermute | solution.py:237
  81.0 3.3 %collective-permute-done.28 = bf16[64,2048]{1,0:T(8,128)(2,1)S(1)} collective-permute-done((bf16[64,2048]{1,0:T(8,128)(2,1)S(1)}, bf16[64,2048]{1,0:T(8,128)(2,1)S(1)}, u32[]{:S(2)}, u32[]{:S(2)}) %collective-permute-start.28) | collective-permute-done | bytes 262176 | tf_op jit(solution)/shard_map/ppermute | solution.py:237
  84.4 1.6 %collective-permute-start.29 = (bf16[64,2048]{1,0:T(8,128)(2,1)S(1)}, bf16[64,2048]{1,0:T(8,128)(2,1)S(1)}, u32[]{:S(2)}, u32[]{:S(2)}) collective-permute-start(bf16[64,2048]{1,0:T(8,128)(2,1)S(1)} %add_convert_fusion.3), channel_id=1, source_target_pairs={{4,0},{5,1},{8,4},{9,5},{12,8},{13,9},{14,12},{15,13},{10,14},{11,... | collective-permute-start | bytes 786440 | tf_op jit(solution)/shard_map/ppermute | solution.py:237
  86.6 3.3 %collective-permute-done.19 = bf16[64,2048]{1,0:T(8,128)(2,1)S(1)} collective-permute-done((bf16[64,2048]{1,0:T(8,128)(2,1)S(1)}, bf16[64,2048]{1,0:T(8,128)(2,1)S(1)}, u32[]{:S(2)}, u32[]{:S(2)}) %collective-permute-start.19) | collective-permute-done | bytes 262176 | tf_op jit(solution)/shard_map/ppermute | solution.py:237
  90.0 1.6 %collective-permute-start.20 = (bf16[64,2048]{1,0:T(8,128)(2,1)S(1)}, bf16[64,2048]{1,0:T(8,128)(2,1)S(1)}, u32[]{:S(2)}, u32[]{:S(2)}) collective-permute-start(bf16[64,2048]{1,0:T(8,128)(2,1)S(1)} %add_convert_fusion.6), channel_id=1, source_target_pairs={{4,0},{5,1},{8,4},{9,5},{12,8},{13,9},{14,12},{15,13},{10,14},{11,... | collective-permute-start | bytes 786440 | tf_op jit(solution)/shard_map/ppermute | solution.py:237
  92.2 3.3 %collective-permute-done.29 = bf16[64,2048]{1,0:T(8,128)(2,1)S(1)} collective-permute-done((bf16[64,2048]{1,0:T(8,128)(2,1)S(1)}, bf16[64,2048]{1,0:T(8,128)(2,1)S(1)}, u32[]{:S(2)}, u32[]{:S(2)}) %collective-permute-start.29) | collective-permute-done | bytes 262176 | tf_op jit(solution)/shard_map/ppermute | solution.py:237
  95.7 1.6 %collective-permute-start.30 = (bf16[64,2048]{1,0:T(8,128)(2,1)S(1)}, bf16[64,2048]{1,0:T(8,128)(2,1)S(1)}, u32[]{:S(2)}, u32[]{:S(2)}) collective-permute-start(bf16[64,2048]{1,0:T(8,128)(2,1)S(1)} %add_convert_fusion.2), channel_id=1, source_target_pairs={{4,0},{5,1},{8,4},{9,5},{12,8},{13,9},{14,12},{15,13},{10,14},{11,... | collective-permute-start | bytes 786440 | tf_op jit(solution)/shard_map/ppermute | solution.py:237
  97.9 2.2 %collective-permute-done.20 = bf16[64,2048]{1,0:T(8,128)(2,1)S(1)} collective-permute-done((bf16[64,2048]{1,0:T(8,128)(2,1)S(1)}, bf16[64,2048]{1,0:T(8,128)(2,1)S(1)}, u32[]{:S(2)}, u32[]{:S(2)}) %collective-permute-start.20) | collective-permute-done | bytes 262176 | tf_op jit(solution)/shard_map/ppermute | solution.py:237
  102.9 1.4 %collective-permute-done.34 = bf16[64,2048]{1,0:T(8,128)(2,1)S(1)} collective-permute-done((bf16[64,2048]{1,0:T(8,128)(2,1)S(1)}, bf16[64,2048]{1,0:T(8,128)(2,1)S(1)}, u32[]{:S(2)}, u32[]{:S(2)}) %collective-permute-start.34) | collective-permute-done | bytes 262176 | tf_op jit(solution)/shard_map/ppermute | solution.py:237
  (109 shorter events, 24.8 us)
Async XLA Ops:
  0.0 8.2 %collective-permute-start.6 = (bf16[2048,768]{1,0:T(8,128)(2,1)}, bf16[2048,768]{1,0:T(8,128)(2,1)}, u32[]{:S(2)}, u32[]{:S(2)}) collective-permute-start(bf16[2048,768]{1,0:T(8,128)(2,1)} %bitcast.31), channel_id=1, source_target_pairs={{0,1},{1,0},{2,3},{3,2},{4,5},{5,4},{6,7},{7,6},{8,9},{9,8},{10,11... | collective-permute-start | bytes 9437192 | tf_op jit(solution)/shard_map/ppermute | solution.py:240
  2.4 9.6 %collective-permute-start.3 = (bf16[64,2048]{1,0:T(8,128)(2,1)S(1)}, bf16[64,2048]{1,0:T(8,128)(2,1)S(1)}, u32[]{:S(2)}, u32[]{:S(2)}) collective-permute-start(bf16[64,2048]{1,0:T(8,128)(2,1)S(1)} %get-tuple-element.99), channel_id=1, source_target_pairs={{0,16},{16,0},{1,17},{17,1},{2,18},{18,2},{3,19},{19,3},{4,20},{20... | collective-permute-start | bytes 786440 | tf_op jit(solution)/shard_map/ppermute | solution.py:247
  4.9 12.4 %collective-permute-start = (bf16[64,2048]{1,0:T(8,128)(2,1)}, bf16[64,2048]{1,0:T(8,128)(2,1)S(1)}, u32[]{:S(2)}, u32[]{:S(2)}) collective-permute-start(bf16[64,2048]{1,0:T(8,128)(2,1)} %get-tuple-element.100), channel_id=1, source_target_pairs={{0,16},{16,0},{1,17},{17,1},{2,18},{18,2},{3,19},{19,3},{4,20},{20... | collective-permute-start | bytes 786440 | tf_op jit(solution)/shard_map/ppermute | solution.py:247
  4.9 15.2 %collective-permute-start.8 = (bf16[768,2048]{1,0:T(8,128)(2,1)}, bf16[768,2048]{1,0:T(8,128)(2,1)}, u32[]{:S(2)}, u32[]{:S(2)}) collective-permute-start(bf16[768,2048]{1,0:T(8,128)(2,1)} %bitcast.35), channel_id=1, source_target_pairs={{0,1},{1,0},{2,3},{3,2},{4,5},{5,4},{6,7},{7,6},{8,9},{9,8},{10,11... | collective-permute-start | bytes 9437192 | tf_op jit(solution)/shard_map/ppermute | solution.py:240
  8.2 12.1 %collective-permute-start.7 = (bf16[2048,768]{1,0:T(8,128)(2,1)}, bf16[2048,768]{1,0:T(8,128)(2,1)}, u32[]{:S(2)}, u32[]{:S(2)}) collective-permute-start(bf16[2048,768]{1,0:T(8,128)(2,1)} %bitcast.33), channel_id=1, source_target_pairs={{0,1},{1,0},{2,3},{3,2},{4,5},{5,4},{6,7},{7,6},{8,9},{9,8},{10,11... | collective-permute-start | bytes 9437192 | tf_op jit(solution)/shard_map/ppermute | solution.py:240
  12.4 14.4 %collective-permute-start.4 = (bf16[64,2176]{1,0:T(8,128)(2,1)S(1)}, bf16[64,2176]{1,0:T(8,128)(2,1)S(1)}, u32[]{:S(2)}, u32[]{:S(2)}) collective-permute-start(bf16[64,2176]{1,0:T(8,128)(2,1)S(1)} %pad_maximum_fusion.1.refs_5_), channel_id=1, source_target_pairs={{4,8},{5,9},{8,12},{9,13},{12,14},{13,15},{14,10},{15,11},{10,6},{... | collective-permute-start | bytes 835592 | tf_op jit(solution)/shard_map/ppermute | solution.py:237
  14.5 12.3 %collective-permute-start.5 = (bf16[64,2176]{1,0:T(8,128)(2,1)S(1)}, bf16[64,2176]{1,0:T(8,128)(2,1)S(1)}, u32[]{:S(2)}, u32[]{:S(2)}) collective-permute-start(bf16[64,2176]{1,0:T(8,128)(2,1)S(1)} %pad_maximum_fusion.1.refs_5_), channel_id=1, source_target_pairs={{4,0},{5,1},{8,4},{9,5},{12,8},{13,9},{14,12},{15,13},{10,14},{11,... | collective-permute-start | bytes 835592 | tf_op jit(solution)/shard_map/ppermute | solution.py:237
  18.2 8.6 %collective-permute-start.1 = (bf16[64,2176]{1,0:T(8,128)(2,1)S(1)}, bf16[64,2176]{1,0:T(8,128)(2,1)}, u32[]{:S(2)}, u32[]{:S(2)}) collective-permute-start(bf16[64,2176]{1,0:T(8,128)(2,1)S(1)} %pad_maximum_fusion.refs_4_), channel_id=1, source_target_pairs={{4,8},{5,9},{8,12},{9,13},{12,14},{13,15},{14,10},{15,11},{10,6},{... | collective-permute-start | bytes 835592 | tf_op jit(solution)/shard_map/ppermute | solution.py:237
  20.1 7.8 %collective-permute-start.2 = (bf16[64,2176]{1,0:T(8,128)(2,1)S(1)}, bf16[64,2176]{1,0:T(8,128)(2,1)S(1)}, u32[]{:S(2)}, u32[]{:S(2)}) collective-permute-start(bf16[64,2176]{1,0:T(8,128)(2,1)S(1)} %pad_maximum_fusion.refs_4_), channel_id=1, source_target_pairs={{4,0},{5,1},{8,4},{9,5},{12,8},{13,9},{14,12},{15,13},{10,14},{11,... | collective-permute-start | bytes 835592 | tf_op jit(solution)/shard_map/ppermute | solution.py:237
  27.9 10.4 %collective-permute-start.10 = (bf16[64,2176]{1,0:T(8,128)(2,1)S(1)}, bf16[64,2176]{1,0:T(8,128)(2,1)S(1)}, u32[]{:S(2)}, u32[]{:S(2)}) collective-permute-start(bf16[64,2176]{1,0:T(8,128)(2,1)S(1)} %collective-permute-done.5.refs_3_), channel_id=1, source_target_pairs={{4,0},{5,1},{8,4},{9,5},{12,8},{13,9},{14,12},{15,13},{10,14},{11,... | collective-permute-start | bytes 835592 | tf_op jit(solution)/shard_map/ppermute | solution.py:237
  28.7 9.7 %collective-permute-start.9 = (bf16[64,2176]{1,0:T(8,128)(2,1)S(1)}, bf16[64,2176]{1,0:T(8,128)(2,1)S(1)}, u32[]{:S(2)}, u32[]{:S(2)}) collective-permute-start(bf16[64,2176]{1,0:T(8,128)(2,1)S(1)} %collective-permute-done.4.refs_2_), channel_id=1, source_target_pairs={{4,8},{5,9},{8,12},{9,13},{12,14},{13,15},{14,10},{15,11},{10,6},{... | collective-permute-start | bytes 835592 | tf_op jit(solution)/shard_map/ppermute | solution.py:237
  30.0 11.9 %collective-permute-start.11 = (bf16[64,2176]{1,0:T(8,128)(2,1)}, bf16[64,2176]{1,0:T(8,128)(2,1)S(1)}, u32[]{:S(2)}, u32[]{:S(2)}) collective-permute-start(bf16[64,2176]{1,0:T(8,128)(2,1)} %collective-permute-done.1.refs_0_), channel_id=1, source_target_pairs={{4,8},{5,9},{8,12},{9,13},{12,14},{13,15},{14,10},{15,11},{10,6},{... | collective-permute-start | bytes 835592 | tf_op jit(solution)/shard_map/ppermute | solution.py:237
  31.5 12.8 %collective-permute-start.15 = (bf16[64,2176]{1,0:T(8,128)(2,1)S(1)}, bf16[64,2176]{1,0:T(8,128)(2,1)S(1)}, u32[]{:S(2)}, u32[]{:S(2)}) collective-permute-start(bf16[64,2176]{1,0:T(8,128)(2,1)S(1)} %collective-permute-done.2.refs_1_), channel_id=1, source_target_pairs={{4,0},{5,1},{8,4},{9,5},{12,8},{13,9},{14,12},{15,13},{10,14},{11,... | collective-permute-start | bytes 835592 | tf_op jit(solution)/shard_map/ppermute | solution.py:237
  38.3 11.1 %collective-permute-start.14 = (bf16[64,2176]{1,0:T(8,128)(2,1)S(1)}, bf16[64,2176]{1,0:T(8,128)(2,1)S(1)}, u32[]{:S(2)}, u32[]{:S(2)}) collective-permute-start(bf16[64,2176]{1,0:T(8,128)(2,1)S(1)} %collective-permute-done.10.refs_3_), channel_id=1, source_target_pairs={{4,0},{5,1},{8,4},{9,5},{12,8},{13,9},{14,12},{15,13},{10,14},{11,... | collective-permute-start | bytes 835592 | tf_op jit(solution)/shard_map/ppermute | solution.py:237
  41.9 9.6 %collective-permute-start.12 = (bf16[64,2176]{1,0:T(8,128)(2,1)S(1)}, bf16[64,2176]{1,0:T(8,128)(2,1)S(1)}, u32[]{:S(2)}, u32[]{:S(2)}) collective-permute-start(bf16[64,2176]{1,0:T(8,128)(2,1)S(1)} %collective-permute-done.11.refs_0_), channel_id=1, source_target_pairs={{4,8},{5,9},{8,12},{9,13},{12,14},{13,15},{14,10},{15,11},{10,6},{... | collective-permute-start | bytes 835592 | tf_op jit(solution)/shard_map/ppermute | solution.py:237
  42.7 14.5 %collective-permute-start.22 = (bf16[64,2176]{1,0:T(8,128)(2,1)S(1)}, bf16[64,2176]{1,0:T(8,128)(2,1)S(1)}, u32[]{:S(2)}, u32[]{:S(2)}) collective-permute-start(bf16[64,2176]{1,0:T(8,128)(2,1)S(1)} %collective-permute-done.9.refs_2_), channel_id=1, source_target_pairs={{4,8},{5,9},{8,12},{9,13},{12,14},{13,15},{14,10},{15,11},{10,6},{... | collective-permute-start | bytes 835592 | tf_op jit(solution)/shard_map/ppermute | solution.py:237
  44.3 12.9 %collective-permute-start.21 = (bf16[64,2176]{1,0:T(8,128)(2,1)S(1)}, bf16[64,2176]{1,0:T(8,128)(2,1)S(1)}, u32[]{:S(2)}, u32[]{:S(2)}) collective-permute-start(bf16[64,2176]{1,0:T(8,128)(2,1)S(1)} %collective-permute-done.15.refs_1_), channel_id=1, source_target_pairs={{4,0},{5,1},{8,4},{9,5},{12,8},{13,9},{14,12},{15,13},{10,14},{11,... | collective-permute-start | bytes 835592 | tf_op jit(solution)/shard_map/ppermute | solution.py:237
  49.5 10.5 %collective-permute-start.16 = (bf16[64,2176]{1,0:T(8,128)(2,1)S(1)}, bf16[64,2176]{1,0:T(8,128)(2,1)S(1)}, u32[]{:S(2)}, u32[]{:S(2)}) collective-permute-start(bf16[64,2176]{1,0:T(8,128)(2,1)S(1)} %collective-permute-done.14.refs_1_), channel_id=1, source_target_pairs={{4,0},{5,1},{8,4},{9,5},{12,8},{13,9},{14,12},{15,13},{10,14},{11,... | collective-permute-start | bytes 835592 | tf_op jit(solution)/shard_map/ppermute | solution.py:237
  51.5 8.7 %collective-permute-start.13 = (bf16[64,2176]{1,0:T(8,128)(2,1)S(1)}, bf16[64,2176]{1,0:T(8,128)(2,1)S(1)}, u32[]{:S(2)}, u32[]{:S(2)}) collective-permute-start(bf16[64,2176]{1,0:T(8,128)(2,1)S(1)} %collective-permute-done.12.refs_0_), channel_id=1, source_target_pairs={{4,8},{5,9},{8,12},{9,13},{12,14},{13,15},{14,10},{15,11},{10,6},{... | collective-permute-start | bytes 835592 | tf_op jit(solution)/shard_map/ppermute | solution.py:237
  65.0 7.1 %collective-permute-start.27 = (bf16[32,2048]{1,0:T(8,128)(2,1)S(1)}, bf16[32,2048]{1,0:T(8,128)(2,1)S(1)}, u32[]{:S(2)}, u32[]{:S(2)}) collective-permute-start(bf16[32,2048]{1,0:T(8,128)(2,1)S(1)} %get-tuple-element.103), channel_id=1, source_target_pairs={{4,0},{5,1},{8,4},{9,5},{12,8},{13,9},{14,12},{15,13},{10,14},{11,... | collective-permute-start | bytes 393224 | tf_op jit(solution)/shard_map/ppermute | solution.py:237
  66.7 7.2 %collective-permute-start.31 = (bf16[32,2048]{1,0:T(8,128)(2,1)S(1)}, bf16[32,2048]{1,0:T(8,128)(2,1)S(1)}, u32[]{:S(2)}, u32[]{:S(2)}) collective-permute-start(bf16[32,2048]{1,0:T(8,128)(2,1)S(1)} %get-tuple-element.104), channel_id=1, source_target_pairs={{4,8},{5,9},{8,12},{9,13},{12,14},{13,15},{14,10},{15,11},{10,6},{... | collective-permute-start | bytes 393224 | tf_op jit(solution)/shard_map/ppermute | solution.py:237
  69.4 9.3 %collective-permute-start.18 = (bf16[64,2048]{1,0:T(8,128)(2,1)S(1)}, bf16[64,2048]{1,0:T(8,128)(2,1)S(1)}, u32[]{:S(2)}, u32[]{:S(2)}) collective-permute-start(bf16[64,2048]{1,0:T(8,128)(2,1)S(1)} %pad_maximum_fusion.2), channel_id=1, source_target_pairs={{4,0},{5,1},{8,4},{9,5},{12,8},{13,9},{14,12},{15,13},{10,14},{11,... | collective-permute-start | bytes 786440 | tf_op jit(solution)/shard_map/ppermute | solution.py:237
  71.1 9.3 %collective-permute-start.24 = (bf16[64,2048]{1,0:T(8,128)(2,1)S(1)}, bf16[64,2048]{1,0:T(8,128)(2,1)S(1)}, u32[]{:S(2)}, u32[]{:S(2)}) collective-permute-start(bf16[64,2048]{1,0:T(8,128)(2,1)S(1)} %pad_maximum_fusion.3), channel_id=1, source_target_pairs={{4,8},{5,9},{8,12},{9,13},{12,14},{13,15},{14,10},{15,11},{10,6},{... | collective-permute-start | bytes 786440 | tf_op jit(solution)/shard_map/ppermute | solution.py:237
  72.2 12.1 %collective-permute-start.28 = (bf16[64,2048]{1,0:T(8,128)(2,1)S(1)}, bf16[64,2048]{1,0:T(8,128)(2,1)S(1)}, u32[]{:S(2)}, u32[]{:S(2)}) collective-permute-start(bf16[64,2048]{1,0:T(8,128)(2,1)S(1)} %pad_maximum_fusion.4), channel_id=1, source_target_pairs={{4,0},{5,1},{8,4},{9,5},{12,8},{13,9},{14,12},{15,13},{10,14},{11,... | collective-permute-start | bytes 786440 | tf_op jit(solution)/shard_map/ppermute | solution.py:237
  73.9 12.1 %collective-permute-start.32 = (bf16[64,2048]{1,0:T(8,128)(2,1)S(1)}, bf16[64,2048]{1,0:T(8,128)(2,1)S(1)}, u32[]{:S(2)}, u32[]{:S(2)}) collective-permute-start(bf16[64,2048]{1,0:T(8,128)(2,1)S(1)} %pad_maximum_fusion.5), channel_id=1, source_target_pairs={{4,8},{5,9},{8,12},{9,13},{12,14},{13,15},{14,10},{15,11},{10,6},{... | collective-permute-start | bytes 786440 | tf_op jit(solution)/shard_map/ppermute | solution.py:237
  78.8 11.2 %collective-permute-start.19 = (bf16[64,2048]{1,0:T(8,128)(2,1)S(1)}, bf16[64,2048]{1,0:T(8,128)(2,1)S(1)}, u32[]{:S(2)}, u32[]{:S(2)}) collective-permute-start(bf16[64,2048]{1,0:T(8,128)(2,1)S(1)} %add_convert_fusion.7), channel_id=1, source_target_pairs={{4,0},{5,1},{8,4},{9,5},{12,8},{13,9},{14,12},{15,13},{10,14},{11,... | collective-permute-start | bytes 786440 | tf_op jit(solution)/shard_map/ppermute | solution.py:237
  80.5 11.2 %collective-permute-start.25 = (bf16[64,2048]{1,0:T(8,128)(2,1)S(1)}, bf16[64,2048]{1,0:T(8,128)(2,1)S(1)}, u32[]{:S(2)}, u32[]{:S(2)}) collective-permute-start(bf16[64,2048]{1,0:T(8,128)(2,1)S(1)} %add_convert_fusion.5), channel_id=1, source_target_pairs={{4,8},{5,9},{8,12},{9,13},{12,14},{13,15},{14,10},{15,11},{10,6},{... | collective-permute-start | bytes 786440 | tf_op jit(solution)/shard_map/ppermute | solution.py:237
  84.4 11.2 %collective-permute-start.29 = (bf16[64,2048]{1,0:T(8,128)(2,1)S(1)}, bf16[64,2048]{1,0:T(8,128)(2,1)S(1)}, u32[]{:S(2)}, u32[]{:S(2)}) collective-permute-start(bf16[64,2048]{1,0:T(8,128)(2,1)S(1)} %add_convert_fusion.3), channel_id=1, source_target_pairs={{4,0},{5,1},{8,4},{9,5},{12,8},{13,9},{14,12},{15,13},{10,14},{11,... | collective-permute-start | bytes 786440 | tf_op jit(solution)/shard_map/ppermute | solution.py:237
  86.1 11.2 %collective-permute-start.33 = (bf16[64,2048]{1,0:T(8,128)(2,1)S(1)}, bf16[64,2048]{1,0:T(8,128)(2,1)S(1)}, u32[]{:S(2)}, u32[]{:S(2)}) collective-permute-start(bf16[64,2048]{1,0:T(8,128)(2,1)S(1)} %add_convert_fusion.1), channel_id=1, source_target_pairs={{4,8},{5,9},{8,12},{9,13},{12,14},{13,15},{14,10},{15,11},{10,6},{... | collective-permute-start | bytes 786440 | tf_op jit(solution)/shard_map/ppermute | solution.py:237
  90.0 10.1 %collective-permute-start.20 = (bf16[64,2048]{1,0:T(8,128)(2,1)S(1)}, bf16[64,2048]{1,0:T(8,128)(2,1)S(1)}, u32[]{:S(2)}, u32[]{:S(2)}) collective-permute-start(bf16[64,2048]{1,0:T(8,128)(2,1)S(1)} %add_convert_fusion.6), channel_id=1, source_target_pairs={{4,0},{5,1},{8,4},{9,5},{12,8},{13,9},{14,12},{15,13},{10,14},{11,... | collective-permute-start | bytes 786440 | tf_op jit(solution)/shard_map/ppermute | solution.py:237
  91.7 9.8 %collective-permute-start.26 = (bf16[64,2048]{1,0:T(8,128)(2,1)S(1)}, bf16[64,2048]{1,0:T(8,128)(2,1)S(1)}, u32[]{:S(2)}, u32[]{:S(2)}) collective-permute-start(bf16[64,2048]{1,0:T(8,128)(2,1)S(1)} %add_convert_fusion.4), channel_id=1, source_target_pairs={{4,8},{5,9},{8,12},{9,13},{12,14},{13,15},{14,10},{15,11},{10,6},{... | collective-permute-start | bytes 786440 | tf_op jit(solution)/shard_map/ppermute | solution.py:237
  95.7 7.3 %collective-permute-start.30 = (bf16[64,2048]{1,0:T(8,128)(2,1)S(1)}, bf16[64,2048]{1,0:T(8,128)(2,1)S(1)}, u32[]{:S(2)}, u32[]{:S(2)}) collective-permute-start(bf16[64,2048]{1,0:T(8,128)(2,1)S(1)} %add_convert_fusion.2), channel_id=1, source_target_pairs={{4,0},{5,1},{8,4},{9,5},{12,8},{13,9},{14,12},{15,13},{10,14},{11,... | collective-permute-start | bytes 786440 | tf_op jit(solution)/shard_map/ppermute | solution.py:237
  (8 other events, 88.8 us)

commit v6 on v5

--- a/solution.py
+++ b/solution.py
@@ -222,6 +222,40 @@
     )(me, *operands)
 
 
+def final_kernel(count, *refs):
+    out, made, sems = refs[-3:]
+    copies = []
+    rows = made.shape[1]
+    size = rows // 2 if rows % 32 == 0 else rows
+    for b in range(count):
+        for first in range(0, rows, size):
+            part = slice(first, first + size)
+            total = sum(ref[part, :].astype(jnp.float32) for ref in refs[b * 4 : b * 4 + 4])
+            made[b, part, :] = total.astype(jnp.bfloat16)
+            copies.append(
+                pltpu.make_async_copy(made.at[b, part, :], out.at[b, part, :], sems.at[len(copies)])
+            )
+            copies[-1].start()
+    for copy in copies:
+        copy.wait()
+
+
+def final_sums(parts):
+    count, (rows, features) = len(parts), parts[0][0].shape
+    near = pl.BlockSpec(memory_space=pltpu.VMEM)
+    return pl.pallas_call(
+        functools.partial(final_kernel, count),
+        out_shape=jax.ShapeDtypeStruct((count, rows, features), jnp.bfloat16),
+        in_specs=[near] * (4 * count),
+        out_specs=pl.BlockSpec(memory_space=pl.ANY),
+        scratch_shapes=[
+            pltpu.VMEM((count, rows, features), jnp.bfloat16),
+            pltpu.SemaphoreType.DMA((2 * count,)),
+        ],
+        compiler_params=pltpu.CompilerParams(vmem_limit_bytes=VMEM_GRANT),
+    )(*[value for part in parts for value in part])
+
+
 def build(cycle):
     chips = len(cycle)
     experts = chips * CORES
@@ -331,13 +365,10 @@
                 elif place:
                     value = added(value, near)
             total[chain] = value
-        results = []
-        for b in range(batches):
-            value = arrived[b].astype(jnp.float32) + sums[(b, 1, 0)].astype(jnp.float32)
-            for step in (1, -1):
-                value += total[b, step].astype(jnp.float32)
-            results.append(value.astype(jnp.bfloat16))
-        return jnp.stack(results)[None]
+        parts = [
+            (arrived[b], sums[b, 1, 0], total[b, 1], total[b, -1]) for b in range(batches)
+        ]
+        return final_sums(parts)[None]
 
     return shards
 

time: 106 us -> 105 us (level)
  local copies, waits for them, and re-layouts: 4.46 us -> 3.2 us
  Pallas kernels: 24.5 us -> 25.7 us
  other arithmetic: 3.84 us -> 2.73 us
where the time goes in v6:
time: 105 us; the launch traced here: 104 us
  waiting for transfers between devices  36.4 us (35%)
  starting transfers between devices  34.9 us (33%)
  Pallas kernels  25.7 us (24%)
  local copies, waits for them, and re-layouts  3.2 us (3%)
  other arithmetic  2.73 us (3%)
    ppermute x30, waiting for transfers between devices, hop(): return lax.ppermute(value, 'expert', pairs)  31.3 us
    ppermute x30, starting transfers between devices, hop(): return lax.ppermute(value, 'expert', pairs)  31.3 us
    pallas_call x5, Pallas kernels, group_sums(): pl.pallas_call(kernel, out_shape=[pltpu.VMEM((size, features), jnp.bfloat...  18.3 us
    pallas_call x1, Pallas kernels, in_vmem(): pl.pallas_call(load_kernel, out_shape=[pltpu.VMEM(value.shape, value.dtyp...  6.49 us
    ppermute x2, waiting for transfers between devices, shards(): lax.ppermute(emitted[0, b], 'section', around)  5.09 us
    ppermute x2, starting transfers between devices, shards(): lax.ppermute(emitted[0, b], 'section', around)  2.61 us
  transfers between devices with their start and end apart: 35, of which 18 were waited for; matrix products, arithmetic and copies ran while one was open for 7% of the time, Pallas kernels for 21%

profile of v6, /device:TPU:0, one launch (start us, length us, event | category | flops | bytes accessed | tf_op | source)
XLA Modules:
  0.0 104.4 jit_solution(11480945869996502286)
XLA Ops:
  1.7 2.5 %collective-permute-start.3 = (bf16[64,2048]{1,0:T(8,128)(2,1)S(1)}, bf16[64,2048]{1,0:T(8,128)(2,1)S(1)}, u32[]{:S(2)}, u32[]{:S(2)}) collective-permute-start(bf16[64,2048]{1,0:T(8,128)(2,1)S(1)} %get-tuple-element.99), channel_id=1, source_target_pairs={{0,16},{16,0},{1,17},{17,1},{2,18},{18,2},{3,19},{19,3},{4,20},{20... | collective-permute-start | bytes 786440 | tf_op jit(solution)/shard_map/ppermute | solution.py:281
  9.1 2.3 %collective-permute-done.3.refs_4_ = bf16[64,2048]{1,0:T(8,128)(2,1)S(1)} collective-permute-done((bf16[64,2048]{1,0:T(8,128)(2,1)S(1)}, bf16[64,2048]{1,0:T(8,128)(2,1)S(1)}, u32[]{:S(2)}, u32[]{:S(2)}) %collective-permute-start.3) | collective-permute-done | bytes 262176 | tf_op jit(solution)/shard_map/ppermute | solution.py:281
  11.8 2.1 %collective-permute-start.4 = (bf16[64,2176]{1,0:T(8,128)(2,1)S(1)}, bf16[64,2176]{1,0:T(8,128)(2,1)S(1)}, u32[]{:S(2)}, u32[]{:S(2)}) collective-permute-start(bf16[64,2176]{1,0:T(8,128)(2,1)S(1)} %pad_maximum_fusion.1.refs_5_), channel_id=1, source_target_pairs={{4,8},{5,9},{8,12},{9,13},{12,14},{13,15},{14,10},{15,11},{10,6},{... | collective-permute-start | bytes 835592 | tf_op jit(solution)/shard_map/ppermute | solution.py:271
  13.9 2.8 %collective-permute-done.refs_0_ = bf16[64,2048]{1,0:T(8,128)(2,1)S(1)} collective-permute-done((bf16[64,2048]{1,0:T(8,128)(2,1)S(1)}, bf16[64,2048]{1,0:T(8,128)(2,1)S(1)}, u32[]{:S(2)}, u32[]{:S(2)}) %collective-permute-start) | collective-permute-done | bytes 262176 | tf_op jit(solution)/shard_map/ppermute | solution.py:281
  17.0 1.9 %collective-permute-start.1 = (bf16[64,2176]{1,0:T(8,128)(2,1)S(1)}, bf16[64,2176]{1,0:T(8,128)(2,1)}, u32[]{:S(2)}, u32[]{:S(2)}) collective-permute-start(bf16[64,2176]{1,0:T(8,128)(2,1)S(1)} %pad_maximum_fusion.refs_4_), channel_id=1, source_target_pairs={{4,8},{5,9},{8,12},{9,13},{12,14},{13,15},{14,10},{15,11},{10,6},{... | collective-permute-start | bytes 835592 | tf_op jit(solution)/shard_map/ppermute | solution.py:271
  19.1 6.5 %shard_map.82 = (bf16[2048,768]{1,0:T(8,128)(2,1)S(1)}, bf16[2048,768]{1,0:T(8,128)(2,1)S(1)}, bf16[768,2048]{1,0:T(8,128)(2,1)S(1)}, bf16[2048,768]{1,0:T(8,128...) custom-call(bf16[2048,768]{1,0:T(8,128)(2,1)} %bitcast.27, bf16[2048,768]{1,0:T(8,128)(2,1)} %bitcast.29, ...), custom_call_target="tpu_custom_call" | custom-call | tf_op jit(solution)/shard_map/pallas_call | solution.py:175
  27.6 1.6 %collective-permute-start.11 = (bf16[64,2176]{1,0:T(8,128)(2,1)}, bf16[64,2176]{1,0:T(8,128)(2,1)S(1)}, u32[]{:S(2)}, u32[]{:S(2)}) collective-permute-start(bf16[64,2176]{1,0:T(8,128)(2,1)} %collective-permute-done.1.refs_0_), channel_id=1, source_target_pairs={{4,8},{5,9},{8,12},{9,13},{12,14},{13,15},{14,10},{15,11},{10,6},{... | collective-permute-start | bytes 835592 | tf_op jit(solution)/shard_map/ppermute | solution.py:271
  29.7 1.6 %collective-permute-start.9 = (bf16[64,2176]{1,0:T(8,128)(2,1)S(1)}, bf16[64,2176]{1,0:T(8,128)(2,1)S(1)}, u32[]{:S(2)}, u32[]{:S(2)}) collective-permute-start(bf16[64,2176]{1,0:T(8,128)(2,1)S(1)} %collective-permute-done.4.refs_2_), channel_id=1, source_target_pairs={{4,8},{5,9},{8,12},{9,13},{12,14},{13,15},{14,10},{15,11},{10,6},{... | collective-permute-start | bytes 835592 | tf_op jit(solution)/shard_map/ppermute | solution.py:271
  31.3 6.5 %shard_map.83 = (bf16[64,2048]{1,0:T(8,128)(2,1)S(1)}, bf16[64,2048]{1,0:T(8,128)(2,1)S(1)}, bf16[64,2048]{1,0:T(8,128)(2,1)S(1)}, bf16[64,2048]{1,0:T(8,128)(2,...) custom-call(s32[1]{0:T(128)} %bitcast.12.me_ref, bf16[64,2176]{1,0:T(8,128)(2,1)} %collective-permute-done.1.refs_0_, ...), custom_call_target="tpu_custom_call" | custom-call | flops 3623878656 | bytes 3145728 | tf_op jit(solution)/shard_map/pallas_call | solution.py:210
  37.8 3.3 %collective-permute-done.9.refs_2_ = bf16[64,2176]{1,0:T(8,128)(2,1)S(1)} collective-permute-done((bf16[64,2176]{1,0:T(8,128)(2,1)S(1)}, bf16[64,2176]{1,0:T(8,128)(2,1)S(1)}, u32[]{:S(2)}, u32[]{:S(2)}) %collective-permute-start.9) | collective-permute-done | bytes 278560 | tf_op jit(solution)/shard_map/ppermute | solution.py:271
  41.1 1.5 %collective-permute-start.14 = (bf16[64,2176]{1,0:T(8,128)(2,1)S(1)}, bf16[64,2176]{1,0:T(8,128)(2,1)S(1)}, u32[]{:S(2)}, u32[]{:S(2)}) collective-permute-start(bf16[64,2176]{1,0:T(8,128)(2,1)S(1)} %collective-permute-done.10.refs_3_), channel_id=1, source_target_pairs={{4,0},{5,1},{8,4},{9,5},{12,8},{13,9},{14,12},{15,13},{10,14},{11,... | collective-permute-start | bytes 835592 | tf_op jit(solution)/shard_map/ppermute | solution.py:271
  45.1 3.6 %shard_map.84 = (bf16[64,2048]{1,0:T(8,128)(2,1)S(1)}, bf16[64,2048]{1,0:T(8,128)(2,1)S(1)}, bf16[64,2048]{1,0:T(8,128)(2,1)S(1)}, bf16[64,2048]{1,0:T(8,128)(2,1)S(1)}) custom-call(s32[1]{0:T(128)} %bitcast.12.me_ref, bf16[64,2176]{1,0:T(8,128)(2,1)S(1)} %collective-permute-done.11.refs_0_, bf16[64,2176]{1,0:T(8,128)(2,1)S(1)} %collective-permute-done.15.refs_1_, ...), custom_call_target="tpu_custom_call" | custom-call | flops 2415919104 | bytes 2097152 | tf_op jit(solution)/shard_map/pallas_call | solution.py:210
  48.7 2.0 %collective-permute-done.14.refs_1_ = bf16[64,2176]{1,0:T(8,128)(2,1)S(1)} collective-permute-done((bf16[64,2176]{1,0:T(8,128)(2,1)S(1)}, bf16[64,2176]{1,0:T(8,128)(2,1)S(1)}, u32[]{:S(2)}, u32[]{:S(2)}) %collective-permute-start.14) | collective-permute-done | bytes 278560 | tf_op jit(solution)/shard_map/ppermute | solution.py:271
  50.6 1.5 %collective-permute-start.16 = (bf16[64,2176]{1,0:T(8,128)(2,1)S(1)}, bf16[64,2176]{1,0:T(8,128)(2,1)S(1)}, u32[]{:S(2)}, u32[]{:S(2)}) collective-permute-start(bf16[64,2176]{1,0:T(8,128)(2,1)S(1)} %collective-permute-done.14.refs_1_), channel_id=1, source_target_pairs={{4,0},{5,1},{8,4},{9,5},{12,8},{13,9},{14,12},{15,13},{10,14},{11,... | collective-permute-start | bytes 835592 | tf_op jit(solution)/shard_map/ppermute | solution.py:271
  52.7 2.7 %shard_map.86 = (bf16[64,2048]{1,0:T(8,128)(2,1)S(1)}, bf16[64,2048]{1,0:T(8,128)(2,1)S(1)}) custom-call(s32[1]{0:T(128)} %bitcast.12.me_ref, bf16[64,2176]{1,0:T(8,128)(2,1)S(1)} %collective-permute-done.12.refs_0_, bf16[64,2176]{1,0:T(8,128)(2,1)S(1)} %collective-permute-done.14.refs_1_, bf16[2048,768]{1,0:T(8,128)(2,1)S(1)} %get-tuple-element.64.refs_6_.refs_4_.refs_2_, ...), custom_call_target="tpu_custom_call" | custom-call | flops 2415919104 | bytes 1048576 | tf_op jit(solution)/shard_map/pallas_call | solution.py:210
  55.4 2.0 %collective-permute-done.22.refs_1_ = bf16[64,2176]{1,0:T(8,128)(2,1)S(1)} collective-permute-done((bf16[64,2176]{1,0:T(8,128)(2,1)S(1)}, bf16[64,2176]{1,0:T(8,128)(2,1)S(1)}, u32[]{:S(2)}, u32[]{:S(2)}) %collective-permute-start.22) | collective-permute-done | bytes 278560 | tf_op jit(solution)/shard_map/ppermute | solution.py:271
  57.4 2.8 %shard_map.87 = (bf16[64,2048]{1,0:T(8,128)(2,1)S(1)}, bf16[64,2048]{1,0:T(8,128)(2,1)S(1)}) custom-call(s32[1]{0:T(128)} %bitcast.12.me_ref, bf16[64,2176]{1,0:T(8,128)(2,1)S(1)} %collective-permute-done.21.refs_0_, bf16[64,2176]{1,0:T(8,128)(2,1)S(1)} %collective-permute-done.22.refs_1_, bf16[2048,768]{1,0:T(8,128)(2,1)S(1)} %get-tuple-element.64.refs_6_.refs_4_.refs_2_, ...), custom_call_target="tpu_custom_call" | custom-call | flops 2415919104 | bytes 1048576 | tf_op jit(solution)/shard_map/pallas_call | solution.py:210
  60.4 2.7 %shard_map.85 = (bf16[64,2048]{1,0:T(8,128)(2,1)S(1)}, bf16[64,2048]{1,0:T(8,128)(2,1)S(1)}) custom-call(s32[1]{0:T(128)} %bitcast.12.me_ref, bf16[64,2176]{1,0:T(8,128)(2,1)S(1)} %collective-permute-done.13.refs_0_, bf16[64,2176]{1,0:T(8,128)(2,1)S(1)} %collective-permute-done.16.refs_1_, bf16[2048,768]{1,0:T(8,128)(2,1)S(1)} %get-tuple-element.64.refs_6_.refs_4_.refs_2_, ...), custom_call_target="tpu_custom_call" | custom-call | flops 2415919104 | bytes 1048576 | tf_op jit(solution)/shard_map/pallas_call | solution.py:210
  63.9 1.4 %collective-permute-start.27 = (bf16[32,2048]{1,0:T(8,128)(2,1)S(1)}, bf16[32,2048]{1,0:T(8,128)(2,1)S(1)}, u32[]{:S(2)}, u32[]{:S(2)}) collective-permute-start(bf16[32,2048]{1,0:T(8,128)(2,1)S(1)} %get-tuple-element.102), channel_id=1, source_target_pairs={{4,0},{5,1},{8,4},{9,5},{12,8},{13,9},{14,12},{15,13},{10,14},{11,... | collective-permute-start | bytes 393224 | tf_op jit(solution)/shard_map/ppermute | solution.py:271
  67.4 2.2 %collective-permute-done.31 = bf16[32,2048]{1,0:T(8,128)(2,1)S(1)} collective-permute-done((bf16[32,2048]{1,0:T(8,128)(2,1)S(1)}, bf16[32,2048]{1,0:T(8,128)(2,1)S(1)}, u32[]{:S(2)}, u32[]{:S(2)}) %collective-permute-start.31) | collective-permute-done | bytes 131104 | tf_op jit(solution)/shard_map/ppermute | solution.py:271
  70.4 1.4 %collective-permute-start.28 = (bf16[64,2048]{1,0:T(8,128)(2,1)S(1)}, bf16[64,2048]{1,0:T(8,128)(2,1)S(1)}, u32[]{:S(2)}, u32[]{:S(2)}) collective-permute-start(bf16[64,2048]{1,0:T(8,128)(2,1)S(1)} %pad_maximum_fusion.4), channel_id=1, source_target_pairs={{4,0},{5,1},{8,4},{9,5},{12,8},{13,9},{14,12},{15,13},{10,14},{11,... | collective-permute-start | bytes 786440 | tf_op jit(solution)/shard_map/ppermute | solution.py:271
  73.2 1.4 %collective-permute-start.18 = (bf16[64,2048]{1,0:T(8,128)(2,1)S(1)}, bf16[64,2048]{1,0:T(8,128)(2,1)S(1)}, u32[]{:S(2)}, u32[]{:S(2)}) collective-permute-start(bf16[64,2048]{1,0:T(8,128)(2,1)S(1)} %pad_maximum_fusion.2), channel_id=1, source_target_pairs={{4,0},{5,1},{8,4},{9,5},{12,8},{13,9},{14,12},{15,13},{10,14},{11,... | collective-permute-start | bytes 786440 | tf_op jit(solution)/shard_map/ppermute | solution.py:271
  74.6 4.3 %collective-permute-done.32 = bf16[64,2048]{1,0:T(8,128)(2,1)S(1)} collective-permute-done((bf16[64,2048]{1,0:T(8,128)(2,1)S(1)}, bf16[64,2048]{1,0:T(8,128)(2,1)S(1)}, u32[]{:S(2)}, u32[]{:S(2)}) %collective-permute-start.32) | collective-permute-done | bytes 262176 | tf_op jit(solution)/shard_map/ppermute | solution.py:271
  79.7 1.4 %collective-permute-start.29 = (bf16[64,2048]{1,0:T(8,128)(2,1)S(1)}, bf16[64,2048]{1,0:T(8,128)(2,1)S(1)}, u32[]{:S(2)}, u32[]{:S(2)}) collective-permute-start(bf16[64,2048]{1,0:T(8,128)(2,1)S(1)} %add_convert_fusion.3), channel_id=1, source_target_pairs={{4,0},{5,1},{8,4},{9,5},{12,8},{13,9},{14,12},{15,13},{10,14},{11,... | collective-permute-start | bytes 786440 | tf_op jit(solution)/shard_map/ppermute | solution.py:271
  81.2 3.3 %collective-permute-done.24 = bf16[64,2048]{1,0:T(8,128)(2,1)S(1)} collective-permute-done((bf16[64,2048]{1,0:T(8,128)(2,1)S(1)}, bf16[64,2048]{1,0:T(8,128)(2,1)S(1)}, u32[]{:S(2)}, u32[]{:S(2)}) %collective-permute-start.24) | collective-permute-done | bytes 262176 | tf_op jit(solution)/shard_map/ppermute | solution.py:271
  85.3 1.4 %collective-permute-start.19 = (bf16[64,2048]{1,0:T(8,128)(2,1)S(1)}, bf16[64,2048]{1,0:T(8,128)(2,1)S(1)}, u32[]{:S(2)}, u32[]{:S(2)}) collective-permute-start(bf16[64,2048]{1,0:T(8,128)(2,1)S(1)} %add_convert_fusion.7), channel_id=1, source_target_pairs={{4,0},{5,1},{8,4},{9,5},{12,8},{13,9},{14,12},{15,13},{10,14},{11,... | collective-permute-start | bytes 786440 | tf_op jit(solution)/shard_map/ppermute | solution.py:271
  86.8 3.3 %collective-permute-done.33 = bf16[64,2048]{1,0:T(8,128)(2,1)S(1)} collective-permute-done((bf16[64,2048]{1,0:T(8,128)(2,1)S(1)}, bf16[64,2048]{1,0:T(8,128)(2,1)S(1)}, u32[]{:S(2)}, u32[]{:S(2)}) %collective-permute-start.33) | collective-permute-done | bytes 262176 | tf_op jit(solution)/shard_map/ppermute | solution.py:271
  91.0 1.4 %collective-permute-start.30 = (bf16[64,2048]{1,0:T(8,128)(2,1)S(1)}, bf16[64,2048]{1,0:T(8,128)(2,1)S(1)}, u32[]{:S(2)}, u32[]{:S(2)}) collective-permute-start(bf16[64,2048]{1,0:T(8,128)(2,1)S(1)} %add_convert_fusion.2), channel_id=1, source_target_pairs={{4,0},{5,1},{8,4},{9,5},{12,8},{13,9},{14,12},{15,13},{10,14},{11,... | collective-permute-start | bytes 786440 | tf_op jit(solution)/shard_map/ppermute | solution.py:271
  92.4 3.3 %collective-permute-done.25 = bf16[64,2048]{1,0:T(8,128)(2,1)S(1)} collective-permute-done((bf16[64,2048]{1,0:T(8,128)(2,1)S(1)}, bf16[64,2048]{1,0:T(8,128)(2,1)S(1)}, u32[]{:S(2)}, u32[]{:S(2)}) %collective-permute-start.25) | collective-permute-done | bytes 262176 | tf_op jit(solution)/shard_map/ppermute | solution.py:271
  96.6 1.4 %collective-permute-start.20 = (bf16[64,2048]{1,0:T(8,128)(2,1)S(1)}, bf16[64,2048]{1,0:T(8,128)(2,1)S(1)}, u32[]{:S(2)}, u32[]{:S(2)}) collective-permute-start(bf16[64,2048]{1,0:T(8,128)(2,1)S(1)} %add_convert_fusion.6), channel_id=1, source_target_pairs={{4,0},{5,1},{8,4},{9,5},{12,8},{13,9},{14,12},{15,13},{10,14},{11,... | collective-permute-start | bytes 786440 | tf_op jit(solution)/shard_map/ppermute | solution.py:271
  98.0 1.9 %collective-permute-done.34.refs_7_ = bf16[64,2048]{1,0:T(8,128)(2,1)S(1)} collective-permute-done((bf16[64,2048]{1,0:T(8,128)(2,1)S(1)}, bf16[64,2048]{1,0:T(8,128)(2,1)S(1)}, u32[]{:S(2)}, u32[]{:S(2)}) %collective-permute-start.34) | collective-permute-done | bytes 262176 | tf_op jit(solution)/shard_map/ppermute | solution.py:271
  100.5 2.3 %collective-permute-done.26.refs_3_ = bf16[64,2048]{1,0:T(8,128)(2,1)S(1)} collective-permute-done((bf16[64,2048]{1,0:T(8,128)(2,1)S(1)}, bf16[64,2048]{1,0:T(8,128)(2,1)S(1)}, u32[]{:S(2)}, u32[]{:S(2)}) %collective-permute-start.26) | collective-permute-done | bytes 262176 | tf_op jit(solution)/shard_map/ppermute | solution.py:271
  (99 shorter events, 23.4 us)
Async XLA Ops:
  0.0 7.6 %collective-permute-start.6 = (bf16[2048,768]{1,0:T(8,128)(2,1)}, bf16[2048,768]{1,0:T(8,128)(2,1)}, u32[]{:S(2)}, u32[]{:S(2)}) collective-permute-start(bf16[2048,768]{1,0:T(8,128)(2,1)} %bitcast.26), channel_id=1, source_target_pairs={{0,1},{1,0},{2,3},{3,2},{4,5},{5,4},{6,7},{7,6},{8,9},{9,8},{10,11... | collective-permute-start | bytes 9437192 | tf_op jit(solution)/shard_map/ppermute | solution.py:274
  1.7 9.7 %collective-permute-start.3 = (bf16[64,2048]{1,0:T(8,128)(2,1)S(1)}, bf16[64,2048]{1,0:T(8,128)(2,1)S(1)}, u32[]{:S(2)}, u32[]{:S(2)}) collective-permute-start(bf16[64,2048]{1,0:T(8,128)(2,1)S(1)} %get-tuple-element.99), channel_id=1, source_target_pairs={{0,16},{16,0},{1,17},{17,1},{2,18},{18,2},{3,19},{19,3},{4,20},{20... | collective-permute-start | bytes 786440 | tf_op jit(solution)/shard_map/ppermute | solution.py:281
  4.2 12.4 %collective-permute-start = (bf16[64,2048]{1,0:T(8,128)(2,1)S(1)}, bf16[64,2048]{1,0:T(8,128)(2,1)S(1)}, u32[]{:S(2)}, u32[]{:S(2)}) collective-permute-start(bf16[64,2048]{1,0:T(8,128)(2,1)S(1)} %get-tuple-element.100), channel_id=1, source_target_pairs={{0,16},{16,0},{1,17},{17,1},{2,18},{18,2},{3,19},{19,3},{4,20},{20... | collective-permute-start | bytes 786440 | tf_op jit(solution)/shard_map/ppermute | solution.py:281
  4.3 14.6 %collective-permute-start.8 = (bf16[768,2048]{1,0:T(8,128)(2,1)}, bf16[768,2048]{1,0:T(8,128)(2,1)}, u32[]{:S(2)}, u32[]{:S(2)}) collective-permute-start(bf16[768,2048]{1,0:T(8,128)(2,1)} %bitcast.30), channel_id=1, source_target_pairs={{0,1},{1,0},{2,3},{3,2},{4,5},{5,4},{6,7},{7,6},{8,9},{9,8},{10,11... | collective-permute-start | bytes 9437192 | tf_op jit(solution)/shard_map/ppermute | solution.py:274
  7.6 11.5 %collective-permute-start.7 = (bf16[2048,768]{1,0:T(8,128)(2,1)}, bf16[2048,768]{1,0:T(8,128)(2,1)}, u32[]{:S(2)}, u32[]{:S(2)}) collective-permute-start(bf16[2048,768]{1,0:T(8,128)(2,1)} %bitcast.28), channel_id=1, source_target_pairs={{0,1},{1,0},{2,3},{3,2},{4,5},{5,4},{6,7},{7,6},{8,9},{9,8},{10,11... | collective-permute-start | bytes 9437192 | tf_op jit(solution)/shard_map/ppermute | solution.py:274
  11.8 13.9 %collective-permute-start.4 = (bf16[64,2176]{1,0:T(8,128)(2,1)S(1)}, bf16[64,2176]{1,0:T(8,128)(2,1)S(1)}, u32[]{:S(2)}, u32[]{:S(2)}) collective-permute-start(bf16[64,2176]{1,0:T(8,128)(2,1)S(1)} %pad_maximum_fusion.1.refs_5_), channel_id=1, source_target_pairs={{4,8},{5,9},{8,12},{9,13},{12,14},{13,15},{14,10},{15,11},{10,6},{... | collective-permute-start | bytes 835592 | tf_op jit(solution)/shard_map/ppermute | solution.py:271
  13.9 11.8 %collective-permute-start.5 = (bf16[64,2176]{1,0:T(8,128)(2,1)S(1)}, bf16[64,2176]{1,0:T(8,128)(2,1)}, u32[]{:S(2)}, u32[]{:S(2)}) collective-permute-start(bf16[64,2176]{1,0:T(8,128)(2,1)S(1)} %pad_maximum_fusion.1.refs_5_), channel_id=1, source_target_pairs={{4,0},{5,1},{8,4},{9,5},{12,8},{13,9},{14,12},{15,13},{10,14},{11,... | collective-permute-start | bytes 835592 | tf_op jit(solution)/shard_map/ppermute | solution.py:271
  17.0 8.8 %collective-permute-start.1 = (bf16[64,2176]{1,0:T(8,128)(2,1)S(1)}, bf16[64,2176]{1,0:T(8,128)(2,1)}, u32[]{:S(2)}, u32[]{:S(2)}) collective-permute-start(bf16[64,2176]{1,0:T(8,128)(2,1)S(1)} %pad_maximum_fusion.refs_4_), channel_id=1, source_target_pairs={{4,8},{5,9},{8,12},{9,13},{12,14},{13,15},{14,10},{15,11},{10,6},{... | collective-permute-start | bytes 835592 | tf_op jit(solution)/shard_map/ppermute | solution.py:271
  18.9 8.3 %collective-permute-start.2 = (bf16[64,2176]{1,0:T(8,128)(2,1)S(1)}, bf16[64,2176]{1,0:T(8,128)(2,1)}, u32[]{:S(2)}, u32[]{:S(2)}) collective-permute-start(bf16[64,2176]{1,0:T(8,128)(2,1)S(1)} %pad_maximum_fusion.refs_4_), channel_id=1, source_target_pairs={{4,0},{5,1},{8,4},{9,5},{12,8},{13,9},{14,12},{15,13},{10,14},{11,... | collective-permute-start | bytes 835592 | tf_op jit(solution)/shard_map/ppermute | solution.py:271
  27.2 10.6 %collective-permute-start.10 = (bf16[64,2176]{1,0:T(8,128)(2,1)}, bf16[64,2176]{1,0:T(8,128)(2,1)S(1)}, u32[]{:S(2)}, u32[]{:S(2)}) collective-permute-start(bf16[64,2176]{1,0:T(8,128)(2,1)} %collective-permute-done.5.refs_3_), channel_id=1, source_target_pairs={{4,0},{5,1},{8,4},{9,5},{12,8},{13,9},{14,12},{15,13},{10,14},{11,... | collective-permute-start | bytes 835592 | tf_op jit(solution)/shard_map/ppermute | solution.py:271
  27.6 14.9 %collective-permute-start.11 = (bf16[64,2176]{1,0:T(8,128)(2,1)}, bf16[64,2176]{1,0:T(8,128)(2,1)S(1)}, u32[]{:S(2)}, u32[]{:S(2)}) collective-permute-start(bf16[64,2176]{1,0:T(8,128)(2,1)} %collective-permute-done.1.refs_0_), channel_id=1, source_target_pairs={{4,8},{5,9},{8,12},{9,13},{12,14},{13,15},{14,10},{15,11},{10,6},{... | collective-permute-start | bytes 835592 | tf_op jit(solution)/shard_map/ppermute | solution.py:271
  29.2 15.2 %collective-permute-start.15 = (bf16[64,2176]{1,0:T(8,128)(2,1)}, bf16[64,2176]{1,0:T(8,128)(2,1)S(1)}, u32[]{:S(2)}, u32[]{:S(2)}) collective-permute-start(bf16[64,2176]{1,0:T(8,128)(2,1)} %collective-permute-done.2.refs_1_), channel_id=1, source_target_pairs={{4,0},{5,1},{8,4},{9,5},{12,8},{13,9},{14,12},{15,13},{10,14},{11,... | collective-permute-start | bytes 835592 | tf_op jit(solution)/shard_map/ppermute | solution.py:271
  29.7 11.4 %collective-permute-start.9 = (bf16[64,2176]{1,0:T(8,128)(2,1)S(1)}, bf16[64,2176]{1,0:T(8,128)(2,1)S(1)}, u32[]{:S(2)}, u32[]{:S(2)}) collective-permute-start(bf16[64,2176]{1,0:T(8,128)(2,1)S(1)} %collective-permute-done.4.refs_2_), channel_id=1, source_target_pairs={{4,8},{5,9},{8,12},{9,13},{12,14},{13,15},{14,10},{15,11},{10,6},{... | collective-permute-start | bytes 835592 | tf_op jit(solution)/shard_map/ppermute | solution.py:271
  41.1 9.6 %collective-permute-start.14 = (bf16[64,2176]{1,0:T(8,128)(2,1)S(1)}, bf16[64,2176]{1,0:T(8,128)(2,1)S(1)}, u32[]{:S(2)}, u32[]{:S(2)}) collective-permute-start(bf16[64,2176]{1,0:T(8,128)(2,1)S(1)} %collective-permute-done.10.refs_3_), channel_id=1, source_target_pairs={{4,0},{5,1},{8,4},{9,5},{12,8},{13,9},{14,12},{15,13},{10,14},{11,... | collective-permute-start | bytes 835592 | tf_op jit(solution)/shard_map/ppermute | solution.py:271
  42.5 9.6 %collective-permute-start.12 = (bf16[64,2176]{1,0:T(8,128)(2,1)S(1)}, bf16[64,2176]{1,0:T(8,128)(2,1)S(1)}, u32[]{:S(2)}, u32[]{:S(2)}) collective-permute-start(bf16[64,2176]{1,0:T(8,128)(2,1)S(1)} %collective-permute-done.11.refs_0_), channel_id=1, source_target_pairs={{4,8},{5,9},{8,12},{9,13},{12,14},{13,15},{14,10},{15,11},{10,6},{... | collective-permute-start | bytes 835592 | tf_op jit(solution)/shard_map/ppermute | solution.py:271
  43.1 14.4 %collective-permute-start.22 = (bf16[64,2176]{1,0:T(8,128)(2,1)S(1)}, bf16[64,2176]{1,0:T(8,128)(2,1)S(1)}, u32[]{:S(2)}, u32[]{:S(2)}) collective-permute-start(bf16[64,2176]{1,0:T(8,128)(2,1)S(1)} %collective-permute-done.9.refs_2_), channel_id=1, source_target_pairs={{4,8},{5,9},{8,12},{9,13},{12,14},{13,15},{14,10},{15,11},{10,6},{... | collective-permute-start | bytes 835592 | tf_op jit(solution)/shard_map/ppermute | solution.py:271
  44.4 13.0 %collective-permute-start.21 = (bf16[64,2176]{1,0:T(8,128)(2,1)S(1)}, bf16[64,2176]{1,0:T(8,128)(2,1)S(1)}, u32[]{:S(2)}, u32[]{:S(2)}) collective-permute-start(bf16[64,2176]{1,0:T(8,128)(2,1)S(1)} %collective-permute-done.15.refs_1_), channel_id=1, source_target_pairs={{4,0},{5,1},{8,4},{9,5},{12,8},{13,9},{14,12},{15,13},{10,14},{11,... | collective-permute-start | bytes 835592 | tf_op jit(solution)/shard_map/ppermute | solution.py:271
  50.6 9.6 %collective-permute-start.16 = (bf16[64,2176]{1,0:T(8,128)(2,1)S(1)}, bf16[64,2176]{1,0:T(8,128)(2,1)S(1)}, u32[]{:S(2)}, u32[]{:S(2)}) collective-permute-start(bf16[64,2176]{1,0:T(8,128)(2,1)S(1)} %collective-permute-done.14.refs_1_), channel_id=1, source_target_pairs={{4,0},{5,1},{8,4},{9,5},{12,8},{13,9},{14,12},{15,13},{10,14},{11,... | collective-permute-start | bytes 835592 | tf_op jit(solution)/shard_map/ppermute | solution.py:271
  52.1 8.3 %collective-permute-start.13 = (bf16[64,2176]{1,0:T(8,128)(2,1)S(1)}, bf16[64,2176]{1,0:T(8,128)(2,1)S(1)}, u32[]{:S(2)}, u32[]{:S(2)}) collective-permute-start(bf16[64,2176]{1,0:T(8,128)(2,1)S(1)} %collective-permute-done.12.refs_0_), channel_id=1, source_target_pairs={{4,8},{5,9},{8,12},{9,13},{12,14},{13,15},{14,10},{15,11},{10,6},{... | collective-permute-start | bytes 835592 | tf_op jit(solution)/shard_map/ppermute | solution.py:271
  65.3 7.1 %collective-permute-start.23 = (bf16[32,2048]{1,0:T(8,128)(2,1)S(1)}, bf16[32,2048]{1,0:T(8,128)(2,1)S(1)}, u32[]{:S(2)}, u32[]{:S(2)}) collective-permute-start(bf16[32,2048]{1,0:T(8,128)(2,1)S(1)} %get-tuple-element.103), channel_id=1, source_target_pairs={{4,8},{5,9},{8,12},{9,13},{12,14},{13,15},{14,10},{15,11},{10,6},{... | collective-permute-start | bytes 393224 | tf_op jit(solution)/shard_map/ppermute | solution.py:271
  66.0 7.1 %collective-permute-start.17 = (bf16[32,2048]{1,0:T(8,128)(2,1)S(1)}, bf16[32,2048]{1,0:T(8,128)(2,1)S(1)}, u32[]{:S(2)}, u32[]{:S(2)}) collective-permute-start(bf16[32,2048]{1,0:T(8,128)(2,1)S(1)} %get-tuple-element.104), channel_id=1, source_target_pairs={{4,0},{5,1},{8,4},{9,5},{12,8},{13,9},{14,12},{15,13},{10,14},{11,... | collective-permute-start | bytes 393224 | tf_op jit(solution)/shard_map/ppermute | solution.py:271
  69.6 9.3 %collective-permute-start.32 = (bf16[64,2048]{1,0:T(8,128)(2,1)S(1)}, bf16[64,2048]{1,0:T(8,128)(2,1)S(1)}, u32[]{:S(2)}, u32[]{:S(2)}) collective-permute-start(bf16[64,2048]{1,0:T(8,128)(2,1)S(1)} %pad_maximum_fusion.5), channel_id=1, source_target_pairs={{4,8},{5,9},{8,12},{9,13},{12,14},{13,15},{14,10},{15,11},{10,6},{... | collective-permute-start | bytes 786440 | tf_op jit(solution)/shard_map/ppermute | solution.py:271
  70.4 9.3 %collective-permute-start.28 = (bf16[64,2048]{1,0:T(8,128)(2,1)S(1)}, bf16[64,2048]{1,0:T(8,128)(2,1)S(1)}, u32[]{:S(2)}, u32[]{:S(2)}) collective-permute-start(bf16[64,2048]{1,0:T(8,128)(2,1)S(1)} %pad_maximum_fusion.4), channel_id=1, source_target_pairs={{4,0},{5,1},{8,4},{9,5},{12,8},{13,9},{14,12},{15,13},{10,14},{11,... | collective-permute-start | bytes 786440 | tf_op jit(solution)/shard_map/ppermute | solution.py:271
  72.4 12.1 %collective-permute-start.24 = (bf16[64,2048]{1,0:T(8,128)(2,1)S(1)}, bf16[64,2048]{1,0:T(8,128)(2,1)S(1)}, u32[]{:S(2)}, u32[]{:S(2)}) collective-permute-start(bf16[64,2048]{1,0:T(8,128)(2,1)S(1)} %pad_maximum_fusion.3), channel_id=1, source_target_pairs={{4,8},{5,9},{8,12},{9,13},{12,14},{13,15},{14,10},{15,11},{10,6},{... | collective-permute-start | bytes 786440 | tf_op jit(solution)/shard_map/ppermute | solution.py:271
  73.2 12.1 %collective-permute-start.18 = (bf16[64,2048]{1,0:T(8,128)(2,1)S(1)}, bf16[64,2048]{1,0:T(8,128)(2,1)S(1)}, u32[]{:S(2)}, u32[]{:S(2)}) collective-permute-start(bf16[64,2048]{1,0:T(8,128)(2,1)S(1)} %pad_maximum_fusion.2), channel_id=1, source_target_pairs={{4,0},{5,1},{8,4},{9,5},{12,8},{13,9},{14,12},{15,13},{10,14},{11,... | collective-permute-start | bytes 786440 | tf_op jit(solution)/shard_map/ppermute | solution.py:271
  79.0 11.2 %collective-permute-start.33 = (bf16[64,2048]{1,0:T(8,128)(2,1)S(1)}, bf16[64,2048]{1,0:T(8,128)(2,1)S(1)}, u32[]{:S(2)}, u32[]{:S(2)}) collective-permute-start(bf16[64,2048]{1,0:T(8,128)(2,1)S(1)} %add_convert_fusion.1), channel_id=1, source_target_pairs={{4,8},{5,9},{8,12},{9,13},{12,14},{13,15},{14,10},{15,11},{10,6},{... | collective-permute-start | bytes 786440 | tf_op jit(solution)/shard_map/ppermute | solution.py:271
  79.7 11.2 %collective-permute-start.29 = (bf16[64,2048]{1,0:T(8,128)(2,1)S(1)}, bf16[64,2048]{1,0:T(8,128)(2,1)S(1)}, u32[]{:S(2)}, u32[]{:S(2)}) collective-permute-start(bf16[64,2048]{1,0:T(8,128)(2,1)S(1)} %add_convert_fusion.3), channel_id=1, source_target_pairs={{4,0},{5,1},{8,4},{9,5},{12,8},{13,9},{14,12},{15,13},{10,14},{11,... | collective-permute-start | bytes 786440 | tf_op jit(solution)/shard_map/ppermute | solution.py:271
  84.6 11.2 %collective-permute-start.25 = (bf16[64,2048]{1,0:T(8,128)(2,1)S(1)}, bf16[64,2048]{1,0:T(8,128)(2,1)S(1)}, u32[]{:S(2)}, u32[]{:S(2)}) collective-permute-start(bf16[64,2048]{1,0:T(8,128)(2,1)S(1)} %add_convert_fusion.5), channel_id=1, source_target_pairs={{4,8},{5,9},{8,12},{9,13},{12,14},{13,15},{14,10},{15,11},{10,6},{... | collective-permute-start | bytes 786440 | tf_op jit(solution)/shard_map/ppermute | solution.py:271
  85.3 11.2 %collective-permute-start.19 = (bf16[64,2048]{1,0:T(8,128)(2,1)S(1)}, bf16[64,2048]{1,0:T(8,128)(2,1)S(1)}, u32[]{:S(2)}, u32[]{:S(2)}) collective-permute-start(bf16[64,2048]{1,0:T(8,128)(2,1)S(1)} %add_convert_fusion.7), channel_id=1, source_target_pairs={{4,0},{5,1},{8,4},{9,5},{12,8},{13,9},{14,12},{15,13},{10,14},{11,... | collective-permute-start | bytes 786440 | tf_op jit(solution)/shard_map/ppermute | solution.py:271
  90.2 9.8 %collective-permute-start.34 = (bf16[64,2048]{1,0:T(8,128)(2,1)S(1)}, bf16[64,2048]{1,0:T(8,128)(2,1)S(1)}, u32[]{:S(2)}, u32[]{:S(2)}) collective-permute-start(bf16[64,2048]{1,0:T(8,128)(2,1)S(1)} %add_convert_fusion), channel_id=1, source_target_pairs={{4,8},{5,9},{8,12},{9,13},{12,14},{13,15},{14,10},{15,11},{10,6},{... | collective-permute-start | bytes 786440 | tf_op jit(solution)/shard_map/ppermute | solution.py:271
  91.0 9.6 %collective-permute-start.30 = (bf16[64,2048]{1,0:T(8,128)(2,1)S(1)}, bf16[64,2048]{1,0:T(8,128)(2,1)S(1)}, u32[]{:S(2)}, u32[]{:S(2)}) collective-permute-start(bf16[64,2048]{1,0:T(8,128)(2,1)S(1)} %add_convert_fusion.2), channel_id=1, source_target_pairs={{4,0},{5,1},{8,4},{9,5},{12,8},{13,9},{14,12},{15,13},{10,14},{11,... | collective-permute-start | bytes 786440 | tf_op jit(solution)/shard_map/ppermute | solution.py:271
  95.8 7.0 %collective-permute-start.26 = (bf16[64,2048]{1,0:T(8,128)(2,1)S(1)}, bf16[64,2048]{1,0:T(8,128)(2,1)S(1)}, u32[]{:S(2)}, u32[]{:S(2)}) collective-permute-start(bf16[64,2048]{1,0:T(8,128)(2,1)S(1)} %add_convert_fusion.4), channel_id=1, source_target_pairs={{4,8},{5,9},{8,12},{9,13},{12,14},{13,15},{14,10},{15,11},{10,6},{... | collective-permute-start | bytes 786440 | tf_op jit(solution)/shard_map/ppermute | solution.py:271
  (4 other events, 27.6 us)

commit v7 on v6

--- a/solution.py
+++ b/solution.py
@@ -280,9 +280,9 @@
         around = [(s, (s + 1) % sections) for s in range(sections)]
         arrived = [lax.ppermute(emitted[0, b], "section", around) for b in range(batches)]
         mine = (w_gate[0, 0], w_up[0, 0], w_down[0, 0])
-        gate_other, down_other = swap(mine[0]), swap(mine[2])
-        up_mine, gate_other = lax.optimization_barrier((mine[1], gate_other))
-        weights = (*mine, gate_other, swap(up_mine), down_other)
+        gate_other, up_other = swap(mine[0]), swap(mine[1])
+        down_mine, gate_other = lax.optimization_barrier((mine[2], gate_other))
+        weights = (*mine, gate_other, up_other, swap(down_mine))
         room = min(tok_rows, 4 * tok_rows * expert_ids.shape[3] // (3 * experts))
         me = lax.axis_index("expert").astype(jnp.int32).reshape(1)
         mod_weight = w_mod[0]

time: 105 us -> 105 us (level)
  no operation moved by 1% of the time
where the time goes in v7:
time: 105 us; the launch traced here: 104 us
  waiting for transfers between devices  36.4 us (35%)
  starting transfers between devices  34.9 us (33%)
  Pallas kernels  25.7 us (24%)
  local copies, waits for them, and re-layouts  3.2 us (3%)
  other arithmetic  2.73 us (3%)
    ppermute x30, waiting for transfers between devices, hop(): return lax.ppermute(value, 'expert', pairs)  31.3 us
    ppermute x30, starting transfers between devices, hop(): return lax.ppermute(value, 'expert', pairs)  31.3 us
    pallas_call x5, Pallas kernels, group_sums(): pl.pallas_call(kernel, out_shape=[pltpu.VMEM((size, features), jnp.bfloat...  18.3 us
    pallas_call x1, Pallas kernels, in_vmem(): pl.pallas_call(load_kernel, out_shape=[pltpu.VMEM(value.shape, value.dtyp...  6.49 us
    ppermute x2, waiting for transfers between devices, shards(): lax.ppermute(emitted[0, b], 'section', around)  5.09 us
    ppermute x2, starting transfers between devices, shards(): lax.ppermute(emitted[0, b], 'section', around)  2.61 us
  transfers between devices with their start and end apart: 35, of which 18 were waited for; matrix products, arithmetic and copies ran while one was open for 7% of the time, Pallas kernels for 21%

profile of v7, /device:TPU:0, one launch (start us, length us, event | category | flops | bytes accessed | tf_op | source)
XLA Modules:
  0.0 104.4 jit_solution(4402782204184643154)
XLA Ops:
  1.7 2.5 %collective-permute-start.3 = (bf16[64,2048]{1,0:T(8,128)(2,1)S(1)}, bf16[64,2048]{1,0:T(8,128)(2,1)S(1)}, u32[]{:S(2)}, u32[]{:S(2)}) collective-permute-start(bf16[64,2048]{1,0:T(8,128)(2,1)S(1)} %get-tuple-element.99), channel_id=1, source_target_pairs={{0,16},{16,0},{1,17},{17,1},{2,18},{18,2},{3,19},{19,3},{4,20},{20... | collective-permute-start | bytes 786440 | tf_op jit(solution)/shard_map/ppermute | solution.py:281
  9.1 2.3 %collective-permute-done.3.refs_4_ = bf16[64,2048]{1,0:T(8,128)(2,1)S(1)} collective-permute-done((bf16[64,2048]{1,0:T(8,128)(2,1)S(1)}, bf16[64,2048]{1,0:T(8,128)(2,1)S(1)}, u32[]{:S(2)}, u32[]{:S(2)}) %collective-permute-start.3) | collective-permute-done | bytes 262176 | tf_op jit(solution)/shard_map/ppermute | solution.py:281
  11.8 2.1 %collective-permute-start.4 = (bf16[64,2176]{1,0:T(8,128)(2,1)S(1)}, bf16[64,2176]{1,0:T(8,128)(2,1)S(1)}, u32[]{:S(2)}, u32[]{:S(2)}) collective-permute-start(bf16[64,2176]{1,0:T(8,128)(2,1)S(1)} %pad_maximum_fusion.1.refs_5_), channel_id=1, source_target_pairs={{4,8},{5,9},{8,12},{9,13},{12,14},{13,15},{14,10},{15,11},{10,6},{... | collective-permute-start | bytes 835592 | tf_op jit(solution)/shard_map/ppermute | solution.py:271
  13.9 2.8 %collective-permute-done.refs_0_ = bf16[64,2048]{1,0:T(8,128)(2,1)S(1)} collective-permute-done((bf16[64,2048]{1,0:T(8,128)(2,1)S(1)}, bf16[64,2048]{1,0:T(8,128)(2,1)S(1)}, u32[]{:S(2)}, u32[]{:S(2)}) %collective-permute-start) | collective-permute-done | bytes 262176 | tf_op jit(solution)/shard_map/ppermute | solution.py:281
  17.0 1.9 %collective-permute-start.1 = (bf16[64,2176]{1,0:T(8,128)(2,1)S(1)}, bf16[64,2176]{1,0:T(8,128)(2,1)}, u32[]{:S(2)}, u32[]{:S(2)}) collective-permute-start(bf16[64,2176]{1,0:T(8,128)(2,1)S(1)} %pad_maximum_fusion.refs_4_), channel_id=1, source_target_pairs={{4,8},{5,9},{8,12},{9,13},{12,14},{13,15},{14,10},{15,11},{10,6},{... | collective-permute-start | bytes 835592 | tf_op jit(solution)/shard_map/ppermute | solution.py:271
  19.1 6.5 %shard_map.82 = (bf16[2048,768]{1,0:T(8,128)(2,1)S(1)}, bf16[2048,768]{1,0:T(8,128)(2,1)S(1)}, bf16[768,2048]{1,0:T(8,128)(2,1)S(1)}, bf16[2048,768]{1,0:T(8,128...) custom-call(bf16[2048,768]{1,0:T(8,128)(2,1)} %bitcast.27, bf16[2048,768]{1,0:T(8,128)(2,1)} %bitcast.29, ...), custom_call_target="tpu_custom_call" | custom-call | tf_op jit(solution)/shard_map/pallas_call | solution.py:175
  27.6 1.6 %collective-permute-start.11 = (bf16[64,2176]{1,0:T(8,128)(2,1)}, bf16[64,2176]{1,0:T(8,128)(2,1)S(1)}, u32[]{:S(2)}, u32[]{:S(2)}) collective-permute-start(bf16[64,2176]{1,0:T(8,128)(2,1)} %collective-permute-done.1.refs_0_), channel_id=1, source_target_pairs={{4,8},{5,9},{8,12},{9,13},{12,14},{13,15},{14,10},{15,11},{10,6},{... | collective-permute-start | bytes 835592 | tf_op jit(solution)/shard_map/ppermute | solution.py:271
  29.7 1.6 %collective-permute-start.9 = (bf16[64,2176]{1,0:T(8,128)(2,1)S(1)}, bf16[64,2176]{1,0:T(8,128)(2,1)S(1)}, u32[]{:S(2)}, u32[]{:S(2)}) collective-permute-start(bf16[64,2176]{1,0:T(8,128)(2,1)S(1)} %collective-permute-done.4.refs_2_), channel_id=1, source_target_pairs={{4,8},{5,9},{8,12},{9,13},{12,14},{13,15},{14,10},{15,11},{10,6},{... | collective-permute-start | bytes 835592 | tf_op jit(solution)/shard_map/ppermute | solution.py:271
  31.3 6.5 %shard_map.83 = (bf16[64,2048]{1,0:T(8,128)(2,1)S(1)}, bf16[64,2048]{1,0:T(8,128)(2,1)S(1)}, bf16[64,2048]{1,0:T(8,128)(2,1)S(1)}, bf16[64,2048]{1,0:T(8,128)(2,...) custom-call(s32[1]{0:T(128)} %bitcast.12.me_ref, bf16[64,2176]{1,0:T(8,128)(2,1)} %collective-permute-done.1.refs_0_, ...), custom_call_target="tpu_custom_call" | custom-call | flops 3623878656 | bytes 3145728 | tf_op jit(solution)/shard_map/pallas_call | solution.py:210
  37.8 3.3 %collective-permute-done.9.refs_2_ = bf16[64,2176]{1,0:T(8,128)(2,1)S(1)} collective-permute-done((bf16[64,2176]{1,0:T(8,128)(2,1)S(1)}, bf16[64,2176]{1,0:T(8,128)(2,1)S(1)}, u32[]{:S(2)}, u32[]{:S(2)}) %collective-permute-start.9) | collective-permute-done | bytes 278560 | tf_op jit(solution)/shard_map/ppermute | solution.py:271
  41.1 1.5 %collective-permute-start.14 = (bf16[64,2176]{1,0:T(8,128)(2,1)S(1)}, bf16[64,2176]{1,0:T(8,128)(2,1)S(1)}, u32[]{:S(2)}, u32[]{:S(2)}) collective-permute-start(bf16[64,2176]{1,0:T(8,128)(2,1)S(1)} %collective-permute-done.10.refs_3_), channel_id=1, source_target_pairs={{4,0},{5,1},{8,4},{9,5},{12,8},{13,9},{14,12},{15,13},{10,14},{11,... | collective-permute-start | bytes 835592 | tf_op jit(solution)/shard_map/ppermute | solution.py:271
  45.1 3.6 %shard_map.84 = (bf16[64,2048]{1,0:T(8,128)(2,1)S(1)}, bf16[64,2048]{1,0:T(8,128)(2,1)S(1)}, bf16[64,2048]{1,0:T(8,128)(2,1)S(1)}, bf16[64,2048]{1,0:T(8,128)(2,1)S(1)}) custom-call(s32[1]{0:T(128)} %bitcast.12.me_ref, bf16[64,2176]{1,0:T(8,128)(2,1)S(1)} %collective-permute-done.11.refs_0_, bf16[64,2176]{1,0:T(8,128)(2,1)S(1)} %collective-permute-done.15.refs_1_, ...), custom_call_target="tpu_custom_call" | custom-call | flops 2415919104 | bytes 2097152 | tf_op jit(solution)/shard_map/pallas_call | solution.py:210
  48.7 2.0 %collective-permute-done.14.refs_1_ = bf16[64,2176]{1,0:T(8,128)(2,1)S(1)} collective-permute-done((bf16[64,2176]{1,0:T(8,128)(2,1)S(1)}, bf16[64,2176]{1,0:T(8,128)(2,1)S(1)}, u32[]{:S(2)}, u32[]{:S(2)}) %collective-permute-start.14) | collective-permute-done | bytes 278560 | tf_op jit(solution)/shard_map/ppermute | solution.py:271
  50.6 1.5 %collective-permute-start.16 = (bf16[64,2176]{1,0:T(8,128)(2,1)S(1)}, bf16[64,2176]{1,0:T(8,128)(2,1)S(1)}, u32[]{:S(2)}, u32[]{:S(2)}) collective-permute-start(bf16[64,2176]{1,0:T(8,128)(2,1)S(1)} %collective-permute-done.14.refs_1_), channel_id=1, source_target_pairs={{4,0},{5,1},{8,4},{9,5},{12,8},{13,9},{14,12},{15,13},{10,14},{11,... | collective-permute-start | bytes 835592 | tf_op jit(solution)/shard_map/ppermute | solution.py:271
  52.7 2.7 %shard_map.86 = (bf16[64,2048]{1,0:T(8,128)(2,1)S(1)}, bf16[64,2048]{1,0:T(8,128)(2,1)S(1)}) custom-call(s32[1]{0:T(128)} %bitcast.12.me_ref, bf16[64,2176]{1,0:T(8,128)(2,1)S(1)} %collective-permute-done.12.refs_0_, bf16[64,2176]{1,0:T(8,128)(2,1)S(1)} %collective-permute-done.14.refs_1_, bf16[2048,768]{1,0:T(8,128)(2,1)S(1)} %get-tuple-element.64.refs_6_.refs_4_.refs_2_, ...), custom_call_target="tpu_custom_call" | custom-call | flops 2415919104 | bytes 1048576 | tf_op jit(solution)/shard_map/pallas_call | solution.py:210
  55.4 2.0 %collective-permute-done.22.refs_1_ = bf16[64,2176]{1,0:T(8,128)(2,1)S(1)} collective-permute-done((bf16[64,2176]{1,0:T(8,128)(2,1)S(1)}, bf16[64,2176]{1,0:T(8,128)(2,1)S(1)}, u32[]{:S(2)}, u32[]{:S(2)}) %collective-permute-start.22) | collective-permute-done | bytes 278560 | tf_op jit(solution)/shard_map/ppermute | solution.py:271
  57.4 2.8 %shard_map.87 = (bf16[64,2048]{1,0:T(8,128)(2,1)S(1)}, bf16[64,2048]{1,0:T(8,128)(2,1)S(1)}) custom-call(s32[1]{0:T(128)} %bitcast.12.me_ref, bf16[64,2176]{1,0:T(8,128)(2,1)S(1)} %collective-permute-done.21.refs_0_, bf16[64,2176]{1,0:T(8,128)(2,1)S(1)} %collective-permute-done.22.refs_1_, bf16[2048,768]{1,0:T(8,128)(2,1)S(1)} %get-tuple-element.64.refs_6_.refs_4_.refs_2_, ...), custom_call_target="tpu_custom_call" | custom-call | flops 2415919104 | bytes 1048576 | tf_op jit(solution)/shard_map/pallas_call | solution.py:210
  60.4 2.7 %shard_map.85 = (bf16[64,2048]{1,0:T(8,128)(2,1)S(1)}, bf16[64,2048]{1,0:T(8,128)(2,1)S(1)}) custom-call(s32[1]{0:T(128)} %bitcast.12.me_ref, bf16[64,2176]{1,0:T(8,128)(2,1)S(1)} %collective-permute-done.13.refs_0_, bf16[64,2176]{1,0:T(8,128)(2,1)S(1)} %collective-permute-done.16.refs_1_, bf16[2048,768]{1,0:T(8,128)(2,1)S(1)} %get-tuple-element.64.refs_6_.refs_4_.refs_2_, ...), custom_call_target="tpu_custom_call" | custom-call | flops 2415919104 | bytes 1048576 | tf_op jit(solution)/shard_map/pallas_call | solution.py:210
  63.9 1.4 %collective-permute-start.27 = (bf16[32,2048]{1,0:T(8,128)(2,1)S(1)}, bf16[32,2048]{1,0:T(8,128)(2,1)S(1)}, u32[]{:S(2)}, u32[]{:S(2)}) collective-permute-start(bf16[32,2048]{1,0:T(8,128)(2,1)S(1)} %get-tuple-element.102), channel_id=1, source_target_pairs={{4,0},{5,1},{8,4},{9,5},{12,8},{13,9},{14,12},{15,13},{10,14},{11,... | collective-permute-start | bytes 393224 | tf_op jit(solution)/shard_map/ppermute | solution.py:271
  67.4 2.2 %collective-permute-done.31 = bf16[32,2048]{1,0:T(8,128)(2,1)S(1)} collective-permute-done((bf16[32,2048]{1,0:T(8,128)(2,1)S(1)}, bf16[32,2048]{1,0:T(8,128)(2,1)S(1)}, u32[]{:S(2)}, u32[]{:S(2)}) %collective-permute-start.31) | collective-permute-done | bytes 131104 | tf_op jit(solution)/shard_map/ppermute | solution.py:271
  70.4 1.4 %collective-permute-start.28 = (bf16[64,2048]{1,0:T(8,128)(2,1)S(1)}, bf16[64,2048]{1,0:T(8,128)(2,1)S(1)}, u32[]{:S(2)}, u32[]{:S(2)}) collective-permute-start(bf16[64,2048]{1,0:T(8,128)(2,1)S(1)} %pad_maximum_fusion.4), channel_id=1, source_target_pairs={{4,0},{5,1},{8,4},{9,5},{12,8},{13,9},{14,12},{15,13},{10,14},{11,... | collective-permute-start | bytes 786440 | tf_op jit(solution)/shard_map/ppermute | solution.py:271
  73.2 1.4 %collective-permute-start.18 = (bf16[64,2048]{1,0:T(8,128)(2,1)S(1)}, bf16[64,2048]{1,0:T(8,128)(2,1)S(1)}, u32[]{:S(2)}, u32[]{:S(2)}) collective-permute-start(bf16[64,2048]{1,0:T(8,128)(2,1)S(1)} %pad_maximum_fusion.2), channel_id=1, source_target_pairs={{4,0},{5,1},{8,4},{9,5},{12,8},{13,9},{14,12},{15,13},{10,14},{11,... | collective-permute-start | bytes 786440 | tf_op jit(solution)/shard_map/ppermute | solution.py:271
  74.6 4.3 %collective-permute-done.32 = bf16[64,2048]{1,0:T(8,128)(2,1)S(1)} collective-permute-done((bf16[64,2048]{1,0:T(8,128)(2,1)S(1)}, bf16[64,2048]{1,0:T(8,128)(2,1)S(1)}, u32[]{:S(2)}, u32[]{:S(2)}) %collective-permute-start.32) | collective-permute-done | bytes 262176 | tf_op jit(solution)/shard_map/ppermute | solution.py:271
  79.7 1.4 %collective-permute-start.29 = (bf16[64,2048]{1,0:T(8,128)(2,1)S(1)}, bf16[64,2048]{1,0:T(8,128)(2,1)S(1)}, u32[]{:S(2)}, u32[]{:S(2)}) collective-permute-start(bf16[64,2048]{1,0:T(8,128)(2,1)S(1)} %add_convert_fusion.3), channel_id=1, source_target_pairs={{4,0},{5,1},{8,4},{9,5},{12,8},{13,9},{14,12},{15,13},{10,14},{11,... | collective-permute-start | bytes 786440 | tf_op jit(solution)/shard_map/ppermute | solution.py:271
  81.2 3.3 %collective-permute-done.24 = bf16[64,2048]{1,0:T(8,128)(2,1)S(1)} collective-permute-done((bf16[64,2048]{1,0:T(8,128)(2,1)S(1)}, bf16[64,2048]{1,0:T(8,128)(2,1)S(1)}, u32[]{:S(2)}, u32[]{:S(2)}) %collective-permute-start.24) | collective-permute-done | bytes 262176 | tf_op jit(solution)/shard_map/ppermute | solution.py:271
  85.3 1.4 %collective-permute-start.19 = (bf16[64,2048]{1,0:T(8,128)(2,1)S(1)}, bf16[64,2048]{1,0:T(8,128)(2,1)S(1)}, u32[]{:S(2)}, u32[]{:S(2)}) collective-permute-start(bf16[64,2048]{1,0:T(8,128)(2,1)S(1)} %add_convert_fusion.7), channel_id=1, source_target_pairs={{4,0},{5,1},{8,4},{9,5},{12,8},{13,9},{14,12},{15,13},{10,14},{11,... | collective-permute-start | bytes 786440 | tf_op jit(solution)/shard_map/ppermute | solution.py:271
  86.8 3.3 %collective-permute-done.33 = bf16[64,2048]{1,0:T(8,128)(2,1)S(1)} collective-permute-done((bf16[64,2048]{1,0:T(8,128)(2,1)S(1)}, bf16[64,2048]{1,0:T(8,128)(2,1)S(1)}, u32[]{:S(2)}, u32[]{:S(2)}) %collective-permute-start.33) | collective-permute-done | bytes 262176 | tf_op jit(solution)/shard_map/ppermute | solution.py:271
  91.0 1.4 %collective-permute-start.30 = (bf16[64,2048]{1,0:T(8,128)(2,1)S(1)}, bf16[64,2048]{1,0:T(8,128)(2,1)S(1)}, u32[]{:S(2)}, u32[]{:S(2)}) collective-permute-start(bf16[64,2048]{1,0:T(8,128)(2,1)S(1)} %add_convert_fusion.2), channel_id=1, source_target_pairs={{4,0},{5,1},{8,4},{9,5},{12,8},{13,9},{14,12},{15,13},{10,14},{11,... | collective-permute-start | bytes 786440 | tf_op jit(solution)/shard_map/ppermute | solution.py:271
  92.4 3.3 %collective-permute-done.25 = bf16[64,2048]{1,0:T(8,128)(2,1)S(1)} collective-permute-done((bf16[64,2048]{1,0:T(8,128)(2,1)S(1)}, bf16[64,2048]{1,0:T(8,128)(2,1)S(1)}, u32[]{:S(2)}, u32[]{:S(2)}) %collective-permute-start.25) | collective-permute-done | bytes 262176 | tf_op jit(solution)/shard_map/ppermute | solution.py:271
  96.6 1.4 %collective-permute-start.20 = (bf16[64,2048]{1,0:T(8,128)(2,1)S(1)}, bf16[64,2048]{1,0:T(8,128)(2,1)S(1)}, u32[]{:S(2)}, u32[]{:S(2)}) collective-permute-start(bf16[64,2048]{1,0:T(8,128)(2,1)S(1)} %add_convert_fusion.6), channel_id=1, source_target_pairs={{4,0},{5,1},{8,4},{9,5},{12,8},{13,9},{14,12},{15,13},{10,14},{11,... | collective-permute-start | bytes 786440 | tf_op jit(solution)/shard_map/ppermute | solution.py:271
  98.0 1.9 %collective-permute-done.34.refs_7_ = bf16[64,2048]{1,0:T(8,128)(2,1)S(1)} collective-permute-done((bf16[64,2048]{1,0:T(8,128)(2,1)S(1)}, bf16[64,2048]{1,0:T(8,128)(2,1)S(1)}, u32[]{:S(2)}, u32[]{:S(2)}) %collective-permute-start.34) | collective-permute-done | bytes 262176 | tf_op jit(solution)/shard_map/ppermute | solution.py:271
  100.5 2.3 %collective-permute-done.26.refs_3_ = bf16[64,2048]{1,0:T(8,128)(2,1)S(1)} collective-permute-done((bf16[64,2048]{1,0:T(8,128)(2,1)S(1)}, bf16[64,2048]{1,0:T(8,128)(2,1)S(1)}, u32[]{:S(2)}, u32[]{:S(2)}) %collective-permute-start.26) | collective-permute-done | bytes 262176 | tf_op jit(solution)/shard_map/ppermute | solution.py:271
  (99 shorter events, 23.4 us)
Async XLA Ops:
  0.0 7.6 %collective-permute-start.6 = (bf16[2048,768]{1,0:T(8,128)(2,1)}, bf16[2048,768]{1,0:T(8,128)(2,1)}, u32[]{:S(2)}, u32[]{:S(2)}) collective-permute-start(bf16[2048,768]{1,0:T(8,128)(2,1)} %bitcast.26), channel_id=1, source_target_pairs={{0,1},{1,0},{2,3},{3,2},{4,5},{5,4},{6,7},{7,6},{8,9},{9,8},{10,11... | collective-permute-start | bytes 9437192 | tf_op jit(solution)/shard_map/ppermute | solution.py:274
  1.7 9.7 %collective-permute-start.3 = (bf16[64,2048]{1,0:T(8,128)(2,1)S(1)}, bf16[64,2048]{1,0:T(8,128)(2,1)S(1)}, u32[]{:S(2)}, u32[]{:S(2)}) collective-permute-start(bf16[64,2048]{1,0:T(8,128)(2,1)S(1)} %get-tuple-element.99), channel_id=1, source_target_pairs={{0,16},{16,0},{1,17},{17,1},{2,18},{18,2},{3,19},{19,3},{4,20},{20... | collective-permute-start | bytes 786440 | tf_op jit(solution)/shard_map/ppermute | solution.py:281
  4.2 12.4 %collective-permute-start = (bf16[64,2048]{1,0:T(8,128)(2,1)S(1)}, bf16[64,2048]{1,0:T(8,128)(2,1)S(1)}, u32[]{:S(2)}, u32[]{:S(2)}) collective-permute-start(bf16[64,2048]{1,0:T(8,128)(2,1)S(1)} %get-tuple-element.100), channel_id=1, source_target_pairs={{0,16},{16,0},{1,17},{17,1},{2,18},{18,2},{3,19},{19,3},{4,20},{20... | collective-permute-start | bytes 786440 | tf_op jit(solution)/shard_map/ppermute | solution.py:281
  4.3 14.6 %collective-permute-start.7 = (bf16[2048,768]{1,0:T(8,128)(2,1)}, bf16[2048,768]{1,0:T(8,128)(2,1)}, u32[]{:S(2)}, u32[]{:S(2)}) collective-permute-start(bf16[2048,768]{1,0:T(8,128)(2,1)} %bitcast.28), channel_id=1, source_target_pairs={{0,1},{1,0},{2,3},{3,2},{4,5},{5,4},{6,7},{7,6},{8,9},{9,8},{10,11... | collective-permute-start | bytes 9437192 | tf_op jit(solution)/shard_map/ppermute | solution.py:274
  7.6 11.5 %collective-permute-start.8 = (bf16[768,2048]{1,0:T(8,128)(2,1)}, bf16[768,2048]{1,0:T(8,128)(2,1)}, u32[]{:S(2)}, u32[]{:S(2)}) collective-permute-start(bf16[768,2048]{1,0:T(8,128)(2,1)} %bitcast.30), channel_id=1, source_target_pairs={{0,1},{1,0},{2,3},{3,2},{4,5},{5,4},{6,7},{7,6},{8,9},{9,8},{10,11... | collective-permute-start | bytes 9437192 | tf_op jit(solution)/shard_map/ppermute | solution.py:274
  11.8 13.9 %collective-permute-start.4 = (bf16[64,2176]{1,0:T(8,128)(2,1)S(1)}, bf16[64,2176]{1,0:T(8,128)(2,1)S(1)}, u32[]{:S(2)}, u32[]{:S(2)}) collective-permute-start(bf16[64,2176]{1,0:T(8,128)(2,1)S(1)} %pad_maximum_fusion.1.refs_5_), channel_id=1, source_target_pairs={{4,8},{5,9},{8,12},{9,13},{12,14},{13,15},{14,10},{15,11},{10,6},{... | collective-permute-start | bytes 835592 | tf_op jit(solution)/shard_map/ppermute | solution.py:271
  13.9 11.8 %collective-permute-start.5 = (bf16[64,2176]{1,0:T(8,128)(2,1)S(1)}, bf16[64,2176]{1,0:T(8,128)(2,1)}, u32[]{:S(2)}, u32[]{:S(2)}) collective-permute-start(bf16[64,2176]{1,0:T(8,128)(2,1)S(1)} %pad_maximum_fusion.1.refs_5_), channel_id=1, source_target_pairs={{4,0},{5,1},{8,4},{9,5},{12,8},{13,9},{14,12},{15,13},{10,14},{11,... | collective-permute-start | bytes 835592 | tf_op jit(solution)/shard_map/ppermute | solution.py:271
  17.0 8.8 %collective-permute-start.1 = (bf16[64,2176]{1,0:T(8,128)(2,1)S(1)}, bf16[64,2176]{1,0:T(8,128)(2,1)}, u32[]{:S(2)}, u32[]{:S(2)}) collective-permute-start(bf16[64,2176]{1,0:T(8,128)(2,1)S(1)} %pad_maximum_fusion.refs_4_), channel_id=1, source_target_pairs={{4,8},{5,9},{8,12},{9,13},{12,14},{13,15},{14,10},{15,11},{10,6},{... | collective-permute-start | bytes 835592 | tf_op jit(solution)/shard_map/ppermute | solution.py:271
  18.9 8.3 %collective-permute-start.2 = (bf16[64,2176]{1,0:T(8,128)(2,1)S(1)}, bf16[64,2176]{1,0:T(8,128)(2,1)}, u32[]{:S(2)}, u32[]{:S(2)}) collective-permute-start(bf16[64,2176]{1,0:T(8,128)(2,1)S(1)} %pad_maximum_fusion.refs_4_), channel_id=1, source_target_pairs={{4,0},{5,1},{8,4},{9,5},{12,8},{13,9},{14,12},{15,13},{10,14},{11,... | collective-permute-start | bytes 835592 | tf_op jit(solution)/shard_map/ppermute | solution.py:271
  27.2 10.6 %collective-permute-start.10 = (bf16[64,2176]{1,0:T(8,128)(2,1)}, bf16[64,2176]{1,0:T(8,128)(2,1)S(1)}, u32[]{:S(2)}, u32[]{:S(2)}) collective-permute-start(bf16[64,2176]{1,0:T(8,128)(2,1)} %collective-permute-done.5.refs_3_), channel_id=1, source_target_pairs={{4,0},{5,1},{8,4},{9,5},{12,8},{13,9},{14,12},{15,13},{10,14},{11,... | collective-permute-start | bytes 835592 | tf_op jit(solution)/shard_map/ppermute | solution.py:271
  27.6 14.9 %collective-permute-start.11 = (bf16[64,2176]{1,0:T(8,128)(2,1)}, bf16[64,2176]{1,0:T(8,128)(2,1)S(1)}, u32[]{:S(2)}, u32[]{:S(2)}) collective-permute-start(bf16[64,2176]{1,0:T(8,128)(2,1)} %collective-permute-done.1.refs_0_), channel_id=1, source_target_pairs={{4,8},{5,9},{8,12},{9,13},{12,14},{13,15},{14,10},{15,11},{10,6},{... | collective-permute-start | bytes 835592 | tf_op jit(solution)/shard_map/ppermute | solution.py:271
  29.2 15.2 %collective-permute-start.15 = (bf16[64,2176]{1,0:T(8,128)(2,1)}, bf16[64,2176]{1,0:T(8,128)(2,1)S(1)}, u32[]{:S(2)}, u32[]{:S(2)}) collective-permute-start(bf16[64,2176]{1,0:T(8,128)(2,1)} %collective-permute-done.2.refs_1_), channel_id=1, source_target_pairs={{4,0},{5,1},{8,4},{9,5},{12,8},{13,9},{14,12},{15,13},{10,14},{11,... | collective-permute-start | bytes 835592 | tf_op jit(solution)/shard_map/ppermute | solution.py:271
  29.7 11.4 %collective-permute-start.9 = (bf16[64,2176]{1,0:T(8,128)(2,1)S(1)}, bf16[64,2176]{1,0:T(8,128)(2,1)S(1)}, u32[]{:S(2)}, u32[]{:S(2)}) collective-permute-start(bf16[64,2176]{1,0:T(8,128)(2,1)S(1)} %collective-permute-done.4.refs_2_), channel_id=1, source_target_pairs={{4,8},{5,9},{8,12},{9,13},{12,14},{13,15},{14,10},{15,11},{10,6},{... | collective-permute-start | bytes 835592 | tf_op jit(solution)/shard_map/ppermute | solution.py:271
  41.1 9.6 %collective-permute-start.14 = (bf16[64,2176]{1,0:T(8,128)(2,1)S(1)}, bf16[64,2176]{1,0:T(8,128)(2,1)S(1)}, u32[]{:S(2)}, u32[]{:S(2)}) collective-permute-start(bf16[64,2176]{1,0:T(8,128)(2,1)S(1)} %collective-permute-done.10.refs_3_), channel_id=1, source_target_pairs={{4,0},{5,1},{8,4},{9,5},{12,8},{13,9},{14,12},{15,13},{10,14},{11,... | collective-permute-start | bytes 835592 | tf_op jit(solution)/shard_map/ppermute | solution.py:271
  42.5 9.6 %collective-permute-start.12 = (bf16[64,2176]{1,0:T(8,128)(2,1)S(1)}, bf16[64,2176]{1,0:T(8,128)(2,1)S(1)}, u32[]{:S(2)}, u32[]{:S(2)}) collective-permute-start(bf16[64,2176]{1,0:T(8,128)(2,1)S(1)} %collective-permute-done.11.refs_0_), channel_id=1, source_target_pairs={{4,8},{5,9},{8,12},{9,13},{12,14},{13,15},{14,10},{15,11},{10,6},{... | collective-permute-start | bytes 835592 | tf_op jit(solution)/shard_map/ppermute | solution.py:271
  43.1 14.4 %collective-permute-start.22 = (bf16[64,2176]{1,0:T(8,128)(2,1)S(1)}, bf16[64,2176]{1,0:T(8,128)(2,1)S(1)}, u32[]{:S(2)}, u32[]{:S(2)}) collective-permute-start(bf16[64,2176]{1,0:T(8,128)(2,1)S(1)} %collective-permute-done.9.refs_2_), channel_id=1, source_target_pairs={{4,8},{5,9},{8,12},{9,13},{12,14},{13,15},{14,10},{15,11},{10,6},{... | collective-permute-start | bytes 835592 | tf_op jit(solution)/shard_map/ppermute | solution.py:271
  44.4 13.0 %collective-permute-start.21 = (bf16[64,2176]{1,0:T(8,128)(2,1)S(1)}, bf16[64,2176]{1,0:T(8,128)(2,1)S(1)}, u32[]{:S(2)}, u32[]{:S(2)}) collective-permute-start(bf16[64,2176]{1,0:T(8,128)(2,1)S(1)} %collective-permute-done.15.refs_1_), channel_id=1, source_target_pairs={{4,0},{5,1},{8,4},{9,5},{12,8},{13,9},{14,12},{15,13},{10,14},{11,... | collective-permute-start | bytes 835592 | tf_op jit(solution)/shard_map/ppermute | solution.py:271
  50.6 9.6 %collective-permute-start.16 = (bf16[64,2176]{1,0:T(8,128)(2,1)S(1)}, bf16[64,2176]{1,0:T(8,128)(2,1)S(1)}, u32[]{:S(2)}, u32[]{:S(2)}) collective-permute-start(bf16[64,2176]{1,0:T(8,128)(2,1)S(1)} %collective-permute-done.14.refs_1_), channel_id=1, source_target_pairs={{4,0},{5,1},{8,4},{9,5},{12,8},{13,9},{14,12},{15,13},{10,14},{11,... | collective-permute-start | bytes 835592 | tf_op jit(solution)/shard_map/ppermute | solution.py:271
  52.1 8.3 %collective-permute-start.13 = (bf16[64,2176]{1,0:T(8,128)(2,1)S(1)}, bf16[64,2176]{1,0:T(8,128)(2,1)S(1)}, u32[]{:S(2)}, u32[]{:S(2)}) collective-permute-start(bf16[64,2176]{1,0:T(8,128)(2,1)S(1)} %collective-permute-done.12.refs_0_), channel_id=1, source_target_pairs={{4,8},{5,9},{8,12},{9,13},{12,14},{13,15},{14,10},{15,11},{10,6},{... | collective-permute-start | bytes 835592 | tf_op jit(solution)/shard_map/ppermute | solution.py:271
  65.3 7.1 %collective-permute-start.23 = (bf16[32,2048]{1,0:T(8,128)(2,1)S(1)}, bf16[32,2048]{1,0:T(8,128)(2,1)S(1)}, u32[]{:S(2)}, u32[]{:S(2)}) collective-permute-start(bf16[32,2048]{1,0:T(8,128)(2,1)S(1)} %get-tuple-element.103), channel_id=1, source_target_pairs={{4,8},{5,9},{8,12},{9,13},{12,14},{13,15},{14,10},{15,11},{10,6},{... | collective-permute-start | bytes 393224 | tf_op jit(solution)/shard_map/ppermute | solution.py:271
  66.0 7.1 %collective-permute-start.17 = (bf16[32,2048]{1,0:T(8,128)(2,1)S(1)}, bf16[32,2048]{1,0:T(8,128)(2,1)S(1)}, u32[]{:S(2)}, u32[]{:S(2)}) collective-permute-start(bf16[32,2048]{1,0:T(8,128)(2,1)S(1)} %get-tuple-element.104), channel_id=1, source_target_pairs={{4,0},{5,1},{8,4},{9,5},{12,8},{13,9},{14,12},{15,13},{10,14},{11,... | collective-permute-start | bytes 393224 | tf_op jit(solution)/shard_map/ppermute | solution.py:271
  69.6 9.3 %collective-permute-start.32 = (bf16[64,2048]{1,0:T(8,128)(2,1)S(1)}, bf16[64,2048]{1,0:T(8,128)(2,1)S(1)}, u32[]{:S(2)}, u32[]{:S(2)}) collective-permute-start(bf16[64,2048]{1,0:T(8,128)(2,1)S(1)} %pad_maximum_fusion.5), channel_id=1, source_target_pairs={{4,8},{5,9},{8,12},{9,13},{12,14},{13,15},{14,10},{15,11},{10,6},{... | collective-permute-start | bytes 786440 | tf_op jit(solution)/shard_map/ppermute | solution.py:271
  70.4 9.3 %collective-permute-start.28 = (bf16[64,2048]{1,0:T(8,128)(2,1)S(1)}, bf16[64,2048]{1,0:T(8,128)(2,1)S(1)}, u32[]{:S(2)}, u32[]{:S(2)}) collective-permute-start(bf16[64,2048]{1,0:T(8,128)(2,1)S(1)} %pad_maximum_fusion.4), channel_id=1, source_target_pairs={{4,0},{5,1},{8,4},{9,5},{12,8},{13,9},{14,12},{15,13},{10,14},{11,... | collective-permute-start | bytes 786440 | tf_op jit(solution)/shard_map/ppermute | solution.py:271
  72.4 12.1 %collective-permute-start.24 = (bf16[64,2048]{1,0:T(8,128)(2,1)S(1)}, bf16[64,2048]{1,0:T(8,128)(2,1)S(1)}, u32[]{:S(2)}, u32[]{:S(2)}) collective-permute-start(bf16[64,2048]{1,0:T(8,128)(2,1)S(1)} %pad_maximum_fusion.3), channel_id=1, source_target_pairs={{4,8},{5,9},{8,12},{9,13},{12,14},{13,15},{14,10},{15,11},{10,6},{... | collective-permute-start | bytes 786440 | tf_op jit(solution)/shard_map/ppermute | solution.py:271
  73.2 12.1 %collective-permute-start.18 = (bf16[64,2048]{1,0:T(8,128)(2,1)S(1)}, bf16[64,2048]{1,0:T(8,128)(2,1)S(1)}, u32[]{:S(2)}, u32[]{:S(2)}) collective-permute-start(bf16[64,2048]{1,0:T(8,128)(2,1)S(1)} %pad_maximum_fusion.2), channel_id=1, source_target_pairs={{4,0},{5,1},{8,4},{9,5},{12,8},{13,9},{14,12},{15,13},{10,14},{11,... | collective-permute-start | bytes 786440 | tf_op jit(solution)/shard_map/ppermute | solution.py:271
  79.0 11.2 %collective-permute-start.33 = (bf16[64,2048]{1,0:T(8,128)(2,1)S(1)}, bf16[64,2048]{1,0:T(8,128)(2,1)S(1)}, u32[]{:S(2)}, u32[]{:S(2)}) collective-permute-start(bf16[64,2048]{1,0:T(8,128)(2,1)S(1)} %add_convert_fusion.1), channel_id=1, source_target_pairs={{4,8},{5,9},{8,12},{9,13},{12,14},{13,15},{14,10},{15,11},{10,6},{... | collective-permute-start | bytes 786440 | tf_op jit(solution)/shard_map/ppermute | solution.py:271
  79.7 11.2 %collective-permute-start.29 = (bf16[64,2048]{1,0:T(8,128)(2,1)S(1)}, bf16[64,2048]{1,0:T(8,128)(2,1)S(1)}, u32[]{:S(2)}, u32[]{:S(2)}) collective-permute-start(bf16[64,2048]{1,0:T(8,128)(2,1)S(1)} %add_convert_fusion.3), channel_id=1, source_target_pairs={{4,0},{5,1},{8,4},{9,5},{12,8},{13,9},{14,12},{15,13},{10,14},{11,... | collective-permute-start | bytes 786440 | tf_op jit(solution)/shard_map/ppermute | solution.py:271
  84.6 11.2 %collective-permute-start.25 = (bf16[64,2048]{1,0:T(8,128)(2,1)S(1)}, bf16[64,2048]{1,0:T(8,128)(2,1)S(1)}, u32[]{:S(2)}, u32[]{:S(2)}) collective-permute-start(bf16[64,2048]{1,0:T(8,128)(2,1)S(1)} %add_convert_fusion.5), channel_id=1, source_target_pairs={{4,8},{5,9},{8,12},{9,13},{12,14},{13,15},{14,10},{15,11},{10,6},{... | collective-permute-start | bytes 786440 | tf_op jit(solution)/shard_map/ppermute | solution.py:271
  85.3 11.2 %collective-permute-start.19 = (bf16[64,2048]{1,0:T(8,128)(2,1)S(1)}, bf16[64,2048]{1,0:T(8,128)(2,1)S(1)}, u32[]{:S(2)}, u32[]{:S(2)}) collective-permute-start(bf16[64,2048]{1,0:T(8,128)(2,1)S(1)} %add_convert_fusion.7), channel_id=1, source_target_pairs={{4,0},{5,1},{8,4},{9,5},{12,8},{13,9},{14,12},{15,13},{10,14},{11,... | collective-permute-start | bytes 786440 | tf_op jit(solution)/shard_map/ppermute | solution.py:271
  90.2 9.8 %collective-permute-start.34 = (bf16[64,2048]{1,0:T(8,128)(2,1)S(1)}, bf16[64,2048]{1,0:T(8,128)(2,1)S(1)}, u32[]{:S(2)}, u32[]{:S(2)}) collective-permute-start(bf16[64,2048]{1,0:T(8,128)(2,1)S(1)} %add_convert_fusion), channel_id=1, source_target_pairs={{4,8},{5,9},{8,12},{9,13},{12,14},{13,15},{14,10},{15,11},{10,6},{... | collective-permute-start | bytes 786440 | tf_op jit(solution)/shard_map/ppermute | solution.py:271
  91.0 9.6 %collective-permute-start.30 = (bf16[64,2048]{1,0:T(8,128)(2,1)S(1)}, bf16[64,2048]{1,0:T(8,128)(2,1)S(1)}, u32[]{:S(2)}, u32[]{:S(2)}) collective-permute-start(bf16[64,2048]{1,0:T(8,128)(2,1)S(1)} %add_convert_fusion.2), channel_id=1, source_target_pairs={{4,0},{5,1},{8,4},{9,5},{12,8},{13,9},{14,12},{15,13},{10,14},{11,... | collective-permute-start | bytes 786440 | tf_op jit(solution)/shard_map/ppermute | solution.py:271
  95.8 7.0 %collective-permute-start.26 = (bf16[64,2048]{1,0:T(8,128)(2,1)S(1)}, bf16[64,2048]{1,0:T(8,128)(2,1)S(1)}, u32[]{:S(2)}, u32[]{:S(2)}) collective-permute-start(bf16[64,2048]{1,0:T(8,128)(2,1)S(1)} %add_convert_fusion.4), channel_id=1, source_target_pairs={{4,8},{5,9},{8,12},{9,13},{12,14},{13,15},{14,10},{15,11},{10,6},{... | collective-permute-start | bytes 786440 | tf_op jit(solution)/shard_map/ppermute | solution.py:271
  (4 other events, 27.6 us)
